TPU v7x, 32 devices: a whole 2x2x4 slice. The times are simulated.
32 devices in a mesh: band: 16 (over z, y, core), grid: 2 (over x).
Axes of the slice: x: 2, y: 2, z: 4, core: 2. Of those that a mesh axis runs over, the one named last changes fastest.
Arguments:
- block_coeffs: float32 [128, 32768], P('band', 'grid'), may hold values from -6 to 6
- potential: float32 [96, 9216], P('grid'), may hold values from -4 to 4
- lower_edge: float32 [1], replicated, may hold values from 0.8 to 1.2
- upper_edge: float32 [1], replicated, may hold values from 4.5 to 5.5
- rotation: float32 [8, 3072, 8], P(None, 'band'), may hold values from -0.75 to 0.75
- owners: int32 [8], replicated, may hold values from 0 to 15
Outputs:
- filtered: float32 [128, 32768], P('band', 'grid')
- residents: float32 [3072, 32768], P('band', 'grid')
All inputs are finite; a program needn't handle non-finite values.
Results may differ from a plain program's by a relative error of at most 0.000071.
Values sent between devices are 32-bit elements; how exact they have to be, the bound alone decides.
No kernel may reach another device: no remote copies, remote signals or barrier semaphores. Data moves between devices by JAX's collectives and lax.ppermute only.
A program may use at most 128 MiB of HBM per device.

v0:
```python
import jax
import jax.numpy as jnp
from jax import lax
from jax.sharding import PartitionSpec as P

NG = 96
KEEP = 32


edge_energy = 1.3


def spread(x, axis, root):
    mine = lax.axis_index(axis) == root
    return lax.psum(jnp.where(mine, x, jnp.zeros_like(x)), axis)


def kept_frequency(kept_count, grid_points):
    ordinal = jnp.arange(kept_count, dtype=jnp.int32)
    return jnp.where(ordinal < kept_count // 2, ordinal, ordinal + (grid_points - kept_count))


def hartley_table(kept_count, grid_points):
    points = jnp.arange(grid_points, dtype=jnp.int32)
    phase_turns = points[:, None] * kept_frequency(kept_count, grid_points)[None, :] % grid_points
    angles = phase_turns.astype(jnp.float32) * (2.0 * jnp.pi / grid_points)
    return (jnp.cos(angles) + jnp.sin(angles)) / jnp.sqrt(jnp.float32(grid_points))


def signed_square(kept_count):
    ordinal = jnp.arange(kept_count, dtype=jnp.int32)
    signed = jnp.where(ordinal < kept_count // 2, ordinal, ordinal - kept_count).astype(jnp.float32)
    return signed * signed / jnp.float32((kept_count // 2) ** 2)


def to_real(coeffs, hartley, potential, keep_local):
    bands_now = coeffs.shape[0]
    coef_cube = coeffs.reshape(bands_now, keep_local, KEEP, KEEP)
    along_x = jnp.einsum("bqkz,nk->bqnz", coef_cube, hartley, precision=lax.Precision.HIGHEST)

    def finish(received):
        along_y = jnp.einsum("bqnz,yq->bnyz", received, hartley, precision=lax.Precision.HIGHEST)
        real_field = jnp.einsum("bnyz,wz->bnyw", along_y, hartley, precision=lax.Precision.HIGHEST)
        planes = real_field.reshape(received.shape[0], potential.shape[0], NG * NG)
        return planes * potential[None]

    return finish(lax.all_to_all(along_x, "grid", split_axis=2, concat_axis=1, tiled=True))


def to_plane(product, hartley, planes_local):
    bands_now = product.shape[0]
    real_field = product.reshape(bands_now, planes_local, NG, NG)
    along_z = jnp.einsum("bnyw,wz->bnyz", real_field, hartley, precision=lax.Precision.HIGHEST)
    along_y = jnp.einsum("bnyz,yq->bqnz", along_z, hartley, precision=lax.Precision.HIGHEST)

    def finish(received):
        along_x = jnp.einsum("bqnz,nk->bqkz", received, hartley, precision=lax.Precision.HIGHEST)
        return along_x.reshape(received.shape[0], -1)

    return finish(lax.all_to_all(along_y, "grid", split_axis=1, concat_axis=2, tiled=True))


def body(block_coeffs, potential, lower_edge, upper_edge, rotation, owners):
    slices = lax.axis_size("grid")
    keep_local = KEEP // slices
    planes_local = potential.shape[0]
    hartley = hartley_table(KEEP, NG)
    square = signed_square(KEEP)
    kinetic_full = edge_energy * (
        square[:, None, None] + square[None, :, None] + square[None, None, :]
    )
    kinetic_rows = kinetic_full.reshape(KEEP, KEEP * KEEP)
    kinetic = lax.dynamic_slice_in_dim(
        kinetic_rows, lax.axis_index("grid") * keep_local, keep_local, 0
    ).reshape(1, -1)
    center = (lower_edge[0] + upper_edge[0]) * 0.5
    half_width = (upper_edge[0] - lower_edge[0]) * 0.5

    def hamiltonian(coeffs):
        product = to_real(coeffs, hartley, potential, keep_local)
        return kinetic * coeffs + to_plane(product, hartley, planes_local)

    first_term = (hamiltonian(block_coeffs) - center * block_coeffs) / half_width
    filtered = 2.0 * (hamiltonian(first_term) - center * first_term) / half_width - block_coeffs
    rotated = jnp.zeros((rotation.shape[1], filtered.shape[1]), jnp.float32)
    for step_index in range(rotation.shape[0]):
        arrived = spread(filtered, "band", owners[step_index])
        rotated = rotated + jnp.dot(
            rotation[step_index],
            arrived,
            precision=lax.Precision.HIGHEST,
            preferred_element_type=jnp.float32,
        )
    return (filtered, rotated)


def solution(mesh):
    return jax.shard_map(
        body,
        mesh=mesh,
        in_specs=(P("band", "grid"), P("grid", None), P(), P(), P(None, "band", None), P()),
        out_specs=(P("band", "grid"), P("band", "grid")),
        check_vma=False,
    )
```

profile of v0, /device:TPU:0, one launch (start us, length us, event | category | flops | bytes accessed | tf_op | source)
XLA Modules:
  0.0 708.6 jit_solution(16647388537287186144)
XLA Ops:
  31.8 18.5 %all-to-all-done = f32[2,1,196608]{2,1,0:T(1,128)} async-done(((f32[2,1,196608]{2,1,0:T(1,128)}), f32[2,1,196608]{2,1,0:T(1,128)}, u32[]{:S(2)}, u32[]{:S(2)}) %all-to-all-start) | async-done | bytes 1572896 | tf_op jit(solution)/shard_map/all_to_all | solution.py:47
  65.0 8.7 %copy.53 = f32[8,16,2,48,32]{3,2,4,1,0:T(2,128)} copy(f32[8,16,2,48,32]{4,1,0,3,2:T(8,128)} %bitcast.132) | data formatting | bytes 3145728 | tf_op jit(solution)/shard_map/all_to_all | solution.py:47
  78.3 10.0 %convolution_bitcast_fusion.1 = f32[8,48,96,32]{2,1,3,0:T(8,128)S(1)} fusion(f32[8,32,48,32]{2,1,3,0:T(8,128)S(1)} %bitcast.137, s32[32]{0:T(128)S(1)} %compare_select_fusion), kind=kOutput, calls=%fused_computation.25 | convolution fusion | flops 453018624 | bytes 6291584 | tf_op jit(solution)/shard_map/bqnz,yq->bnyz/dot_general | solution.py:42
  88.4 30.9 %fusion.13 = f32[8,48,96,96]{3,2,1,0:T(8,128)S(1)} fusion(f32[8,48,96,32]{2,1,3,0:T(8,128)S(1)} %convolution_bitcast_fusion.1, s32[32]{0:T(128)S(1)} %compare_select_fusion), kind=kOutput, calls=%fused_computation.20 | convolution fusion | flops 1358988288 | bytes 18874496 | tf_op jit(solution)/shard_map/bnyz,wz->bnyw/dot_general | solution.py:43
  119.2 39.6 %fusion.3 = f32[8,48,96,32]{2,3,1,0:T(8,128)S(1)} fusion(f32[8,48,96,96]{3,2,1,0:T(8,128)S(1)} %fusion.13, f32[48,96,96]{2,1,0:T(8,128)S(1)} %mul.206, s32[32]{0:T(128)S(1)} %compare_select_fusion), kind=kOutput, calls=%fused_computation.10 | convolution fusion | flops 1362527232 | bytes 20643968 | tf_op jit(solution)/shard_map/bnyw,wz->bnyz/dot_general | solution.py:53
  158.9 21.5 %fusion.15 = f32[8,32,48,32]{2,1,3,0:T(8,128)S(1)} fusion(f32[8,48,96,32]{2,3,1,0:T(8,128)S(1)} %fusion.3, s32[32]{0:T(128)S(1)} %compare_select_fusion), kind=kOutput, calls=%fused_computation.26 | convolution fusion | flops 453018624 | bytes 6291584 | tf_op jit(solution)/shard_map/bnyz,yq->bqnz/dot_general | solution.py:54
  197.7 17.1 %all-to-all-done.1 = f32[2,1,196608]{2,1,0:T(1,128)} async-done(((f32[2,1,196608]{2,1,0:T(1,128)}), f32[2,1,196608]{2,1,0:T(1,128)}, u32[]{:S(2)}, u32[]{:S(2)}) %all-to-all-start.1) | async-done | bytes 1572896 | tf_op jit(solution)/shard_map/all_to_all | solution.py:60
  242.3 12.6 %convolution_bitcast_fusion.4 = f32[8,16,32,32]{3,2,1,0:T(8,128)} fusion(f32[8,16,96,32]{2,3,1,0:T(8,128)} %all_to_all.59, s32[32]{0:T(128)S(1)} %compare_select_fusion), kind=kOutput, calls=%fused_computation.30 | convolution fusion | flops 151028736 | bytes 2097280 | tf_op jit(solution)/shard_map/bqnz,nk->bqkz/dot_general | solution.py:57
  278.3 23.3 %all_to_all.72 = f32[2,1,196608]{2,1,0:T(1,128)} all-to-all(f32[2,1,196608]{2,1,0:T(1,128)} %reshape.119), channel_id=1, replica_groups=mesh['band'=16,'grid'=2] {'grid'}, dimensions={0} | all-to-all | bytes 3145728 | tf_op jit(solution)/shard_map/all_to_all | solution.py:47
  328.9 10.0 %convolution_bitcast_fusion = f32[8,48,96,32]{2,1,3,0:T(8,128)S(1)} fusion(f32[8,32,48,32]{2,1,3,0:T(8,128)S(1)} %bitcast.142, s32[32]{0:T(128)S(1)} %compare_select_fusion), kind=kOutput, calls=%fused_computation.24 | convolution fusion | flops 453018624 | bytes 6291584 | tf_op jit(solution)/shard_map/bqnz,yq->bnyz/dot_general | solution.py:42
  338.9 30.9 %fusion.9 = f32[8,48,96,96]{3,2,1,0:T(8,128)S(1)} fusion(f32[8,48,96,32]{2,1,3,0:T(8,128)S(1)} %convolution_bitcast_fusion, s32[32]{0:T(128)S(1)} %compare_select_fusion), kind=kOutput, calls=%fused_computation.16 | convolution fusion | flops 1358988288 | bytes 18874496 | tf_op jit(solution)/shard_map/bnyz,wz->bnyw/dot_general | solution.py:43
  369.8 39.6 %fusion.1 = f32[8,48,96,32]{2,3,1,0:T(8,128)S(1)} fusion(f32[8,48,96,96]{3,2,1,0:T(8,128)S(1)} %fusion.9, f32[48,96,96]{2,1,0:T(8,128)S(1)} %mul.206, s32[32]{0:T(128)S(1)} %compare_select_fusion), kind=kOutput, calls=%fused_computation.8 | convolution fusion | flops 1362527232 | bytes 20643968 | tf_op jit(solution)/shard_map/bnyw,wz->bnyz/dot_general | solution.py:53
  409.4 21.4 %fusion.18 = f32[8,32,48,32]{2,1,3,0:T(8,128)S(1)} fusion(f32[8,48,96,32]{2,3,1,0:T(8,128)S(1)} %fusion.1, s32[32]{0:T(128)S(1)} %compare_select_fusion), kind=kOutput, calls=%fused_computation.27 | convolution fusion | flops 453018624 | bytes 6291584 | tf_op jit(solution)/shard_map/bnyz,yq->bqnz/dot_general | solution.py:54
  451.3 11.2 %all-to-all-done.3 = f32[2,1,196608]{2,1,0:T(1,128)S(1)} async-done(((f32[2,1,196608]{2,1,0:T(1,128)}), f32[2,1,196608]{2,1,0:T(1,128)S(1)}, u32[]{:S(2)}, u32[]{:S(2)}) %all-to-all-start.3) | async-done | bytes 1572896 | tf_op jit(solution)/shard_map/all_to_all | solution.py:60
  485.3 11.0 %convolution_bitcast_fusion.2 = f32[8,16,32,32]{3,2,1,0:T(8,128)} fusion(f32[8,16,96,32]{2,3,1,0:T(8,128)S(1)} %all_to_all.67, s32[32]{0:T(128)S(1)} %compare_select_fusion), kind=kOutput, calls=%fused_computation.28 | convolution fusion | flops 151028736 | bytes 2097280 | tf_op jit(solution)/shard_map/bqnz,nk->bqkz/dot_general | solution.py:57
  501.8 113.3 %all-reduce.3.cloned.1.call-done = (f32[8,16384]{1,0:T(8,128)}, f32[8,16384]{1,0:T(8,128)}, f32[8,16384]{1,0:T(8,128)}, f32[8,16384]{1,0:T(8,128)}, f32[8,16384]...) async-done(((f32[8,16384]{1,0:T(8,128)}, f32[8,16384]{1,0:T(8,128)}, f32[8,16384]{1,0:T(8,128)}, f32[8,16384]{1,0:T(8,128)}, ...) | async-done | bytes 4194320 | tf_op jit(solution)/shard_map/psum | solution.py:15
  615.1 11.3 %fusion.47 = f32[16384,192]{0,1:T(8,128)S(1)} fusion(f32[8,16384]{1,0:T(8,128)} %get-tuple-element.2, f32[8,192,8]{1,2,0:T(8,128)S(1)} %copy-done.12), kind=kOutput, calls=%fused_computation.72 | convolution fusion | flops 301989888 | bytes 13115392 | tf_op jit(solution)/shard_map/dot_general | solution.py:88
  626.5 10.4 %convolution_add_fusion.6 = f32[16384,192]{0,1:T(8,128)S(1)} fusion(f32[16384,192]{0,1:T(8,128)S(1)} %fusion.47, f32[8,16384]{1,0:T(8,128)S(1)} %copy-done.11, f32[8,192,8]{1,2,0:T(8,128)S(1)} %copy-done.12), kind=kOutput, calls=%fused_computation.7 | convolution fusion | flops 305135616 | bytes 25698304 | tf_op jit(solution)/shard_map/dot_general | solution.py:88
  637.0 10.2 %convolution_add_fusion.5 = f32[16384,192]{0,1:T(8,128)S(1)} fusion(f32[16384,192]{0,1:T(8,128)S(1)} %convolution_add_fusion.6, f32[8,16384]{1,0:T(8,128)S(1)} %copy-done.10, f32[8,192,8]{1,2,0:T(8,128)S(1)} %copy-done.12), kind=kOutput, calls=%fused_computation.6 | convolution fusion | flops 305135616 | bytes 25698304 | tf_op jit(solution)/shard_map/dot_general | solution.py:88
  647.2 10.0 %convolution_add_fusion.4 = f32[16384,192]{0,1:T(8,128)S(1)} fusion(f32[16384,192]{0,1:T(8,128)S(1)} %convolution_add_fusion.5, f32[8,16384]{1,0:T(8,128)S(1)} %copy-done.9, f32[8,192,8]{1,2,0:T(8,128)S(1)} %copy-done.12), kind=kOutput, calls=%fused_computation.5 | convolution fusion | flops 305135616 | bytes 25698304 | tf_op jit(solution)/shard_map/dot_general | solution.py:88
  657.3 10.3 %convolution_add_fusion.3 = f32[16384,192]{0,1:T(8,128)S(1)} fusion(f32[16384,192]{0,1:T(8,128)S(1)} %convolution_add_fusion.4, f32[8,16384]{1,0:T(8,128)S(1)} %copy-done.8, f32[8,192,8]{1,2,0:T(8,128)S(1)} %copy-done.12), kind=kOutput, calls=%fused_computation.4 | convolution fusion | flops 305135616 | bytes 25698304 | tf_op jit(solution)/shard_map/dot_general | solution.py:88
  667.5 10.4 %convolution_add_fusion.2 = f32[16384,192]{0,1:T(8,128)S(1)} fusion(f32[16384,192]{0,1:T(8,128)S(1)} %convolution_add_fusion.3, f32[8,16384]{1,0:T(8,128)S(1)} %copy-done.7, f32[8,192,8]{1,2,0:T(8,128)S(1)} %copy-done.12), kind=kOutput, calls=%fused_computation.3 | convolution fusion | flops 305135616 | bytes 25698304 | tf_op jit(solution)/shard_map/dot_general | solution.py:88
  678.0 10.2 %convolution_add_fusion.1 = f32[16384,192]{0,1:T(8,128)S(1)} fusion(f32[16384,192]{0,1:T(8,128)S(1)} %convolution_add_fusion.2, f32[8,16384]{1,0:T(8,128)S(1)} %copy-done.6, f32[8,192,8]{1,2,0:T(8,128)S(1)} %copy-done.12), kind=kOutput, calls=%fused_computation.2 | convolution fusion | flops 305135616 | bytes 25698304 | tf_op jit(solution)/shard_map/dot_general | solution.py:88
  688.2 13.3 %fusion = f32[192,16384]{1,0:T(8,128)} fusion(f32[16384,192]{0,1:T(8,128)S(1)} %convolution_add_fusion.1, f32[8,16384]{1,0:T(8,128)S(1)} %copy-done.5, f32[8,192,8]{1,2,0:T(8,128)S(1)} %copy-done.12), kind=kOutput, calls=%fused_computation.1 | convolution fusion | flops 305135616 | bytes 25698304 | tf_op jit(solution)/shard_map/dot_general | solution.py:88
  (77 shorter events, 181.6 us)
Async XLA Ops:
  24.7 25.7 %all-to-all-start = ((f32[2,1,196608]{2,1,0:T(1,128)}), f32[2,1,196608]{2,1,0:T(1,128)}, u32[]{:S(2)}, u32[]{:S(2)}) async-start(f32[2,1,196608]{2,1,0:T(1,128)} %reshape.115), calls=%async_computation | async-start | bytes 3145728 | tf_op jit(solution)/shard_map/all_to_all | solution.py:47
  191.1 23.7 %all-to-all-start.1 = ((f32[2,1,196608]{2,1,0:T(1,128)}), f32[2,1,196608]{2,1,0:T(1,128)}, u32[]{:S(2)}, u32[]{:S(2)}) async-start(f32[2,1,196608]{2,1,0:T(1,128)} %reshape.117), calls=%async_computation.1 | async-start | bytes 3145728 | tf_op jit(solution)/shard_map/all_to_all | solution.py:60
  236.6 20.7 %copy-start = (f32[8,16384]{1,0:T(8,128)S(1)}, f32[8,16384]{1,0:T(8,128)}, u32[]{:S(2)}) copy-start(f32[8,16384]{1,0:T(8,128)} %param.6) | copy-start | bytes 1572868
  257.4 15.4 %copy-start.2 = (f32[8,16384]{1,0:T(8,128)}, f32[8,16384]{1,0:T(8,128)S(1)}, u32[]{:S(2)}) copy-start(f32[8,16384]{1,0:T(8,128)S(1)} %reshape.111) | copy-start | bytes 1572868
  435.3 10.1 %copy-start.13 = (s32[8]{0:T(128)S(1)}, s32[8]{0:T(128)}, u32[]{:S(2)}) copy-start(s32[8]{0:T(128)} %param.11) | copy-start | bytes 100
  441.7 20.8 %all-to-all-start.3 = ((f32[2,1,196608]{2,1,0:T(1,128)}), f32[2,1,196608]{2,1,0:T(1,128)S(1)}, u32[]{:S(2)}, u32[]{:S(2)}) async-start(f32[2,1,196608]{2,1,0:T(1,128)} %reshape.121), calls=%async_computation.3 | async-start | bytes 3145728 | tf_op jit(solution)/shard_map/all_to_all | solution.py:60
  445.4 169.7 %all-reduce.3.cloned.1.call-start = ((), (), s32[]{:S(2)}) async-start(), calls=%async_computation.4 | async-start | bytes 8388608 | tf_op jit(solution)/shard_map/psum | solution.py:15
  480.7 18.1 %copy-start.1 = (f32[8,16384]{1,0:T(8,128)S(1)}, f32[8,16384]{1,0:T(8,128)}, u32[]{:S(2)}) copy-start(f32[8,16384]{1,0:T(8,128)} %param.6) | copy-start | bytes 1572868
  480.7 18.1 %copy-start.3 = (f32[8,16384]{1,0:T(8,128)S(1)}, f32[8,16384]{1,0:T(8,128)}, u32[]{:S(2)}) copy-start(f32[8,16384]{1,0:T(8,128)} %copy-done.2) | copy-start | bytes 1572868
  496.2 118.9 %copy-start.12 = (f32[8,192,8]{1,2,0:T(8,128)S(1)}, f32[8,192,8]{1,2,0:T(8,128)}, u32[]{:S(2)}) copy-start(f32[8,192,8]{1,2,0:T(8,128)} %param.10) | copy-start | bytes 147460
  499.9 126.6 %copy-start.4 = (f32[8,16384]{1,0:T(8,128)}, f32[8,16384]{1,0:T(8,128)S(1)}, u32[]{:S(2)}) copy-start(f32[8,16384]{1,0:T(8,128)S(1)} %get-tuple-element.11) | copy-start | bytes 1572868
  615.1 11.3 %copy-start.11 = (f32[8,16384]{1,0:T(8,128)S(1)}, f32[8,16384]{1,0:T(8,128)}, u32[]{:S(2)}) copy-start(f32[8,16384]{1,0:T(8,128)} %get-tuple-element.3) | copy-start | bytes 1572868
  626.5 10.5 %copy-start.10 = (f32[8,16384]{1,0:T(8,128)S(1)}, f32[8,16384]{1,0:T(8,128)}, u32[]{:S(2)}) copy-start(f32[8,16384]{1,0:T(8,128)} %get-tuple-element.4) | copy-start | bytes 1572868
  636.9 10.2 %copy-start.9 = (f32[8,16384]{1,0:T(8,128)S(1)}, f32[8,16384]{1,0:T(8,128)}, u32[]{:S(2)}) copy-start(f32[8,16384]{1,0:T(8,128)} %get-tuple-element.5) | copy-start | bytes 1572868
  647.2 10.0 %copy-start.8 = (f32[8,16384]{1,0:T(8,128)S(1)}, f32[8,16384]{1,0:T(8,128)}, u32[]{:S(2)}) copy-start(f32[8,16384]{1,0:T(8,128)} %get-tuple-element.6) | copy-start | bytes 1572868
  657.2 10.3 %copy-start.7 = (f32[8,16384]{1,0:T(8,128)S(1)}, f32[8,16384]{1,0:T(8,128)}, u32[]{:S(2)}) copy-start(f32[8,16384]{1,0:T(8,128)} %get-tuple-element.7) | copy-start | bytes 1572868
  667.5 10.5 %copy-start.6 = (f32[8,16384]{1,0:T(8,128)S(1)}, f32[8,16384]{1,0:T(8,128)}, u32[]{:S(2)}) copy-start(f32[8,16384]{1,0:T(8,128)} %get-tuple-element.8) | copy-start | bytes 1572868
  678.0 10.2 %copy-start.5 = (f32[8,16384]{1,0:T(8,128)S(1)}, f32[8,16384]{1,0:T(8,128)}, u32[]{:S(2)}) copy-start(f32[8,16384]{1,0:T(8,128)} %get-tuple-element.9) | copy-start | bytes 1572868
Sparse Core Ops, SparseCore 0:
  501.9 113.1 all-reduce.2
where the time goes:
time: 715 us; the launch traced here: 709 us
  matrix products  324 us (45%)
  waiting for transfers between devices  160 us (22%)
  local copies, waits for them, and re-layouts  133 us (19%)
  other arithmetic  33.2 us (5%)
  blocking collectives  23.3 us (3%)
  between operations  21.1 us (3%)
  starting transfers between devices  13.2 us (2%)
    psum x1, waiting for transfers between devices, spread(): return lax.psum(jnp.where(mine, x, jnp.zeros_like(x)), axis)  113 us
    dot_general x8, matrix products, body(): jnp.dot(rotation[step_index], arrived, precision=lax.Precision.HIGHEST, p...  86.2 us
    dot_general x2, matrix products, to_plane(): jnp.einsum('bnyw,wz->bnyz', real_field, hartley, precision=lax.Precision....  79.2 us
    dot_general x2, matrix products, finish(): jnp.einsum('bnyz,wz->bnyw', along_y, hartley, precision=lax.Precision.HIG...  61.8 us
    unnamed x37, local copies, waits for them, and re-layouts  46.6 us
    dot_general x2, matrix products, to_plane(): jnp.einsum('bnyz,yq->bqnz', along_z, hartley, precision=lax.Precision.HIG...  42.9 us
    all_to_all x2, waiting for transfers between devices, to_plane(): lax.all_to_all(along_y, 'grid', split_axis=1, concat_axis=2, tiled=True)  28.2 us
    all_to_all x5, local copies, waits for them, and re-layouts, to_real(): lax.all_to_all(along_x, 'grid', split_axis=2, concat_axis=1, tiled=True)  27 us
  transfers between devices with their start and end apart: 4, of which 4 were waited for; matrix products, arithmetic and copies ran while one was open for 1% of the time, Pallas kernels for 0%

commit v1 on v0

v1 whole, which is shorter than its diff:
```python
import functools

import jax
import jax.numpy as jnp
import ml_dtypes
import numpy as np
from jax import lax
from jax.experimental import pallas as pl
from jax.experimental.pallas import tpu as pltpu
from jax.sharding import PartitionSpec as P

NG = 96
KEEP = 32
EDGE_ENERGY = 1.3
NP = 64
LOW = 4
LANES = LOW * KEEP
QUAD = 4
MIB = 1024 * 1024

F32 = jnp.float32
BF16 = jnp.bfloat16


def cas(angle):
    return np.cos(angle) + np.sin(angle)


SIGNED = np.where(np.arange(KEEP) < KEEP // 2, np.arange(KEEP), np.arange(KEEP) - KEEP).astype(np.float64)
POINTS = 2.0 * np.pi * (np.arange(NP) + 0.5) / NP


def product_basis(points):
    return np.concatenate(
        [np.cos(points[:, None] * np.arange(KEEP)), np.sin(points[:, None] * np.arange(1, KEEP + 1))], axis=1
    )


PROJECT = np.linalg.solve(product_basis(POINTS).T, product_basis(2.0 * np.pi * np.arange(NG) / NG).T)
TABLE = cas(POINTS[:, None] * SIGNED[None, :]) / np.sqrt(NG)
KX_ORDER = np.arange(KEEP).reshape(KEEP // LOW, LOW).T.reshape(-1)


ROW_SYN, ROW_PROJECT, ROW_Y_ANA = 0, NP, 2 * NP
ROW_X_ANA = ROW_Y_ANA + KEEP
ROW_Z_SYN = ROW_X_ANA + KEEP
ROW_Z_ANA = ROW_Z_SYN + 3 * LANES
ROW_END = ROW_Z_ANA + 2 * LANES


def halves(table):
    high = table.astype(np.float32).astype(ml_dtypes.bfloat16)
    low = (table - high.astype(np.float64)).astype(np.float32).astype(ml_dtypes.bfloat16)
    return high, low


def left_table(table):
    high, low = halves(table)
    return np.concatenate([high, low, high], axis=1)


def split(x):
    high = x.astype(BF16)
    return high, (x - high.astype(F32)).astype(BF16)


def stack(x):
    high, low = split(x)
    return jnp.concatenate([high, high, low], axis=0)


def mm(a, b):
    return jnp.dot(a, b, preferred_element_type=F32)


def sheet(shape, *parts):
    whole = np.zeros(shape, ml_dtypes.bfloat16)
    for row, lane, part in parts:
        whole[row:row + part.shape[0], lane:lane + part.shape[1]] = part
    return jnp.asarray(whole)


def lane_transpose(parts):
    lane = lax.broadcasted_iota(jnp.int32, (1, LANES), 1)
    second = (lane // 64) == 1
    odd = (lane // 32) % 2 == 1
    a, b, c, d = parts
    p0 = jnp.where(second, pltpu.roll(c, 64, 1), a)
    p2 = jnp.where(second, c, pltpu.roll(a, 64, 1))
    p1 = jnp.where(second, pltpu.roll(d, 64, 1), b)
    p3 = jnp.where(second, d, pltpu.roll(b, 64, 1))
    r0 = jnp.where(odd, pltpu.roll(p1, 32, 1), p0)
    r1 = jnp.where(odd, p1, pltpu.roll(p0, 96, 1))
    r2 = jnp.where(odd, pltpu.roll(p3, 32, 1), p2)
    r3 = jnp.where(odd, p3, pltpu.roll(p2, 96, 1))
    return [r0, r1, r2, r3]


def pack_kernel(slices, c_ref, *rest):
    outs, scratch = rest[:slices], rest[slices]
    rows = scratch.shape[0] // 8
    each = 8 // slices
    g = lax.axis_index("grid")
    for r in range(rows):
        scratch[pl.ds(r, 8, stride=rows), :] = c_ref[:, r * LANES:(r + 1) * LANES]
    for k in range(slices):
        dest = lax.rem(g + k, slices)
        start = pl.multiple_of(dest * (each * rows), each * rows)
        outs[k][...] = scratch[pl.ds(start, each * rows), :].reshape(each, rows, LANES)


def unpack_kernel(slices, *refs):
    ins, out, scratch = refs[:slices], refs[slices], refs[slices + 1]
    rows = scratch.shape[0] // 8
    each = 8 // slices
    g = lax.axis_index("grid")
    for k in range(slices):
        source = lax.rem(g + slices - k, slices)
        start = pl.multiple_of(source * (each * rows), each * rows)
        scratch[pl.ds(start, each * rows), :] = ins[k][...].reshape(each * rows, LANES)
    for r in range(rows):
        out[:, r * LANES:(r + 1) * LANES] = scratch[pl.ds(r, 8, stride=rows), :]


def project_kernel(ways, v_ref, tables, after, out_ref, first, second):
    planes = out_ref.shape[0]
    start = 0
    if ways > 1:
        start = pl.multiple_of(lax.rem(lax.axis_index("band"), ways) * planes, planes)
    z_high, z_low = tables[:NG, :LANES], tables[:NG, LANES:2 * LANES]
    group = 16
    for y0 in range(0, NG, group):
        x = jnp.concatenate(
            [v_ref[pl.ds(start, planes), (y0 + i) * NG:(y0 + i + 1) * NG] for i in range(group)], axis=0
        )
        high, low = split(x)
        first[y0 * planes:(y0 + group) * planes, :] = mm(high, z_high) + mm(high, z_low) + mm(low, z_high)
    y_table = tables[NG:NG + NP, :3 * NG]
    for p in range(0, planes, 2):
        x = jnp.concatenate([first[pl.ds(p + i, NG, stride=planes), :] for i in range(2)], axis=1)
        res = mm(y_table, stack(x))
        for i in range(2):
            second[pl.ds(p + i, NP, stride=planes), :] = res[:, i * LANES:(i + 1) * LANES]
    left = lax.broadcasted_iota(jnp.int32, (1, LANES), 1) < NP
    for j in range(NP // 2):
        even = second[2 * j * planes:(2 * j + 1) * planes, :]
        odd = second[(2 * j + 1) * planes:(2 * j + 2) * planes, :]
        out_ref[:, j * LANES:(j + 1) * LANES] = jnp.where(left, even, odd)


def synthesis_kernel(slices, *refs):
    coeffs, tables = refs[:slices], refs[slices]
    c_all, field, z_first, x1 = refs[slices + 1:]
    g = lax.axis_index("grid")
    each, rows, _ = coeffs[0].shape
    ky_local = KEEP // slices
    kx_high = KEEP // LOW
    for k in range(slices):
        source = lax.rem(g + slices - k, slices)
        parts = [coeffs[k][b] if b < each else jnp.zeros((rows, LANES), F32) for b in range(QUAD)]
        for low, part in enumerate(lane_transpose(parts)):
            c_all[pl.ds(source * ky_local, ky_local), low * kx_high:(low + 1) * kx_high, :] = part.reshape(
                ky_local, kx_high, LANES
            )
    synthesize(c_all, tables, z_first, x1, lambda x, value: put(field, x * NP, value))


def put(ref, row, value):
    ref[row:row + value.shape[0], :] = value


def wide(ref, start, size, stride):
    return jnp.concatenate([ref[h, pl.ds(start, size, stride=stride), :] for h in range(2)], axis=1)


def synthesize(u_all, tables, z_first, x1, give):
    z_syn = tables[ROW_Z_SYN:ROW_Z_SYN + 3 * LANES, :2 * LANES]
    group = 8
    for ky in range(0, KEEP, group):
        high, low = split(u_all[ky:ky + group].reshape(group * KEEP, LANES))
        put(z_first, ky * KEEP, mm(jnp.concatenate([high, high, low], axis=1), z_syn))
    xs = tables[ROW_SYN:ROW_SYN + NP, :3 * KEEP]
    for ky in range(KEEP):
        res = mm(xs, stack(z_first[ky * KEEP:(ky + 1) * KEEP, :]))
        for h in range(2):
            x1[h, ky * NP:(ky + 1) * NP, :] = res[:, h * LANES:(h + 1) * LANES]
    ys = tables[ROW_SYN:ROW_SYN + NP, LANES:LANES + 3 * KEEP]
    for x in range(NP):
        give(x, mm(ys, stack(wide(x1, x, KEEP, NP))))


def filter_kernel(slices, ways, *refs):
    c_all, field = refs[:2]
    pieces = refs[2:2 + slices * ways]
    refs = refs[2 + slices * ways:]
    lower, upper, tables = refs[:3]
    outs, spread = refs[3:3 + slices], refs[3 + slices]
    planes_all, vt, u_all, z_first, x1, y2, packed = refs[4 + slices:]
    g = lax.axis_index("grid")
    core = lax.rem(lax.axis_index("band"), ways)
    each, rows, _ = outs[0].shape
    kx_high = KEEP // LOW
    planes = pieces[0].shape[0]
    slot = planes_all.shape[0] // (slices * ways)
    if slot != planes:
        planes_all[...] = jnp.zeros_like(planes_all)

    for k in range(slices):
        source = lax.rem(g + slices - k, slices)
        for w in range(ways):
            half = lax.rem(core + w, ways)
            start = pl.multiple_of((source * ways + half) * slot, slot)
            planes_all[pl.ds(start, planes), :] = pieces[k * ways + w][...]
    x_table = tables[ROW_PROJECT:ROW_PROJECT + NP, :3 * planes_all.shape[0]]
    left = lax.broadcasted_iota(jnp.int32, (1, LANES), 1) < NP
    width = 512
    for c0 in range(0, NP * NP, width):
        res = mm(x_table, stack(planes_all[:, c0:c0 + width]))
        for j in range(width // LANES):
            v = res[:, j * LANES:(j + 1) * LANES]
            turned = pltpu.roll(v, NP, 1)
            y = 2 * (c0 // LANES + j)
            vt[pl.ds(y, NP, stride=NP), :] = jnp.where(left, v, turned)
            vt[pl.ds(y + 1, NP, stride=NP), :] = jnp.where(left, turned, v)

    low_edge = jnp.full((1, LANES), lower[0], F32)
    high_edge = jnp.full((1, LANES), upper[0], F32)
    center = (low_edge + high_edge) * 0.5
    half_width = (high_edge - low_edge) * 0.5

    row = lax.broadcasted_iota(jnp.int32, (KEEP, LANES), 0)
    lane = lax.broadcasted_iota(jnp.int32, (KEEP, LANES), 1)
    kx = row % kx_high * LOW + row // kx_high
    kz = lane % KEEP
    signed = [jnp.where(k < KEEP // 2, k, k - KEEP).astype(F32) for k in (kx, kz)]
    square = signed[0] * signed[0] + signed[1] * signed[1]

    z_ana = tables[ROW_Z_ANA:ROW_Z_ANA + 2 * LANES, :2 * LANES]
    ya = tables[ROW_Y_ANA:ROW_Y_ANA + KEEP, :3 * NP]
    xa = tables[ROW_X_ANA:ROW_X_ANA + KEEP, :3 * NP]

    def weigh(x, value):
        local = vt[x * NP:(x + 1) * NP, :]
        res = mm(ya, stack(value * jnp.concatenate([local, local], axis=1)))
        for h in range(2):
            y2[h, x * KEEP:(x + 1) * KEEP, :] = res[:, h * LANES:(h + 1) * LANES]

    def finish(u, scale, back):
        for ky in range(KEEP):
            put(z_first, ky * KEEP, mm(xa, stack(wide(y2, ky, NP, KEEP))))
        group = 8
        for ky in range(0, KEEP, group):
            high, low = split(z_first[ky * KEEP:(ky + group) * KEEP, :])
            twice = mm(high, z_ana)
            res = twice[:, :LANES] + twice[:, LANES:] + mm(low, z_ana[:, :LANES])
            for i in range(group):
                kinetic = EDGE_ENERGY * ((square + SIGNED[ky + i] ** 2) * (1.0 / (KEEP // 2) ** 2))
                now = u[ky + i]
                out = scale * (kinetic * now + res[i * KEEP:(i + 1) * KEEP, :] - center * now)
                u_all[ky + i] = out - c_all[ky + i] if back else out

    for x in range(NP):
        weigh(x, field[x * NP:(x + 1) * NP, :])
    finish(c_all, 1.0 / half_width, False)
    synthesize(u_all, tables, z_first, x1, weigh)
    finish(u_all, 2.0 / half_width, True)

    parts = [
        u_all[:, low * kx_high:(low + 1) * kx_high, :].reshape(KEEP * kx_high, LANES) for low in range(LOW)
    ]
    for b, part in enumerate(lane_transpose(parts)[:each]):
        packed[b] = part
    for k in range(slices):
        dest = lax.rem(g + k, slices)
        start = pl.multiple_of(dest * rows, rows)
        for b in range(each):
            outs[k][b] = packed[b, pl.ds(start, rows), :]
    run = spread.shape[1] // each
    groups = rows // run
    for dest in range(groups * slices):
        start = (dest % slices) * rows + (dest // slices) * run
        for b in range(each):
            spread[dest, b * run:(b + 1) * run, :] = packed[b, start:start + run, :]


def select_kernel(owners, came, out):
    steps = owners.shape[0]
    run = out.shape[1] // LANES
    block = out.shape[0] // steps
    for s in range(steps):
        for r in range(run):
            start = owners[s] * (block * run) + r
            out[s * block:(s + 1) * block, r * LANES:(r + 1) * LANES] = came[pl.ds(start, block, stride=run), :]


def rotate_kernel(moves, chips, table, *refs):
    count = sum(parts for _, _, parts in moves)
    blocks = list(refs[:count])
    out, arrived, results, in_sems, out_sems = refs[-5:]
    band = lax.axis_index("band")
    chip, core = band // 2, lax.rem(band, 2)
    position = jnp.where(lax.rem(chip, 2) == 0, chip // 2, chips - 1 - chip // 2)
    slots, _, width = results.shape
    loads = []
    for j, (_, _, parts) in enumerate(moves):
        row, now = 0, []
        for _ in range(parts):
            block = blocks.pop(0)
            size = block.shape[0]
            now.append(
                pltpu.make_async_copy(block, arrived.at[j, pl.ds(row, size)], in_sems.at[len(now) * len(moves) + j])
            )
            row += size
        loads.append(now)
    for now in loads:
        for load in now:
            load.start()
    left = table[...]
    stores = []
    for j, (offset, flip, _) in enumerate(moves):
        for load in loads[j]:
            load.wait()
        res = mm(left, stack(arrived[j]))
        if j >= slots:
            stores[j - slots].wait()
        results[j % slots] = res
        place = lax.rem(position + (chips + offset), chips)
        owner = jnp.where(place < chips // 2, 2 * place, 2 * (chips - 1 - place) + 1)
        start = pl.multiple_of((2 * owner + (core if flip == 0 else 1 - core)) * width, width)
        store = pltpu.make_async_copy(
            results.at[j % slots], out.at[:, pl.ds(start, width)], out_sems.at[j % slots]
        )
        store.start()
        stores.append(store)
    for store in stores[-slots:]:
        store.wait()


def params(mib):
    return pltpu.CompilerParams(vmem_limit_bytes=mib * MIB)


def in_vmem(count):
    return [pl.BlockSpec(memory_space=pltpu.VMEM)] * count


def body(block_coeffs, potential, lower_edge, upper_edge, rotation, owners):
    slices = lax.axis_size("grid")
    groups = lax.axis_size("band")
    block, cols = block_coeffs.shape
    rows = cols // LANES
    each = block // slices
    steps = rotation.shape[0]
    ways = 2 if potential.shape[0] % 16 == 0 else 1
    planes = potential.shape[0] // ways
    slot = -(-planes // 8) * 8

    def shift(x, k):
        return lax.ppermute(x, "grid", [(i, (i + k) % slices) for i in range(slices)])

    def shift_diagonal(x, k):
        pairs = [
            (i * slices + j, (i ^ 1) * slices + (j + k) % slices) for i in range(groups) for j in range(slices)
        ]
        return lax.ppermute(x, ("band", "grid"), pairs)

    def other_core(x):
        return lax.ppermute(x, "band", [(i, i ^ 1) for i in range(groups)])

    piece = jax.ShapeDtypeStruct((each, rows, LANES), F32)
    packed = pl.pallas_call(
        functools.partial(pack_kernel, slices),
        out_shape=[piece] * slices,
        in_specs=in_vmem(1),
        out_specs=in_vmem(slices),
        scratch_shapes=[pltpu.VMEM((block * rows, LANES), F32)],
        compiler_params=params(8),
        name="pack",
    )(block_coeffs)
    coeffs = [packed[0]] + [shift(packed[k], k) for k in range(1, slices)]

    z_high, z_low = halves(np.concatenate([PROJECT.T, PROJECT.T], axis=1))
    project_tables = sheet(
        (NG + NP, 3 * LANES), (0, 0, z_high), (0, LANES, z_low), (NG, 0, left_table(PROJECT))
    )
    projected = pl.pallas_call(
        functools.partial(project_kernel, ways),
        out_shape=jax.ShapeDtypeStruct((planes, NP * NP), F32),
        in_specs=in_vmem(2) + [pl.BlockSpec(memory_space=pl.ANY)],
        out_specs=pl.BlockSpec(memory_space=pltpu.VMEM),
        scratch_shapes=[pltpu.VMEM((NG * planes, LANES), F32), pltpu.VMEM((NP * planes, LANES), F32)],
        compiler_params=params(12),
        name="project",
    )(potential, project_tables, packed[0])
    projected, coeffs = lax.optimization_barrier((projected, coeffs))
    eye = np.eye(QUAD)
    z_high, z_low = halves(np.kron(eye, TABLE.T))
    back_high, back_low = halves(np.kron(eye, TABLE))
    slots = np.zeros((NP, NG // planes, slot))
    slots[:, :, :planes] = PROJECT.reshape(NP, NG // planes, planes)
    tables = sheet(
        (ROW_END, 3 * LANES),
        (ROW_SYN, 0, left_table(TABLE[:, KX_ORDER])),
        (ROW_SYN, LANES, left_table(TABLE)),
        (ROW_PROJECT, 0, left_table(slots.reshape(NP, -1))),
        (ROW_Y_ANA, 0, left_table(TABLE.T)),
        (ROW_X_ANA, 0, left_table(TABLE[:, KX_ORDER].T)),
        (ROW_Z_SYN, 0, np.concatenate([z_high, z_low, z_high], axis=0)),
        (ROW_Z_ANA, 0, np.concatenate([back_high, back_low], axis=1)),
    )
    cube = jax.ShapeDtypeStruct((KEEP, KEEP, LANES), F32)
    c_all, field = pl.pallas_call(
        functools.partial(synthesis_kernel, slices),
        out_shape=[cube, jax.ShapeDtypeStruct((NP * NP, 2 * LANES), F32)],
        in_specs=in_vmem(slices + 1),
        out_specs=in_vmem(2),
        scratch_shapes=[
            pltpu.VMEM((KEEP * KEEP, 2 * LANES), F32),
            pltpu.VMEM((2, KEEP * NP, LANES), F32),
        ],
        compiler_params=params(16),
        cost_estimate=pl.CostEstimate(flops=1, bytes_accessed=1, transcendentals=0),
        name="synthesis",
    )(*coeffs, tables)

    pieces = []
    for k in range(slices):
        if ways == 1:
            pieces.append(projected if k == 0 else shift(projected, k))
        elif k == 0:
            pieces += [projected, other_core(projected)]
        else:
            came, c_all, field = lax.optimization_barrier((shift_diagonal(projected, k), c_all, field))
            pieces += [other_core(came), came]

    *filtered_pieces, spread = pl.pallas_call(
        functools.partial(filter_kernel, slices, ways),
        out_shape=[piece] * slices
        + [jax.ShapeDtypeStruct((groups * slices, each * rows // groups, LANES), F32)],
        in_specs=in_vmem(2 + slices * ways) + [pl.BlockSpec(memory_space=pltpu.SMEM)] * 2 + in_vmem(1),
        out_specs=in_vmem(slices + 1),
        scratch_shapes=[
            pltpu.VMEM((NG // planes * slot, NP * NP), F32),
            pltpu.VMEM((NP * NP, LANES), F32),
            pltpu.VMEM((KEEP, KEEP, LANES), F32),
            pltpu.VMEM((KEEP * KEEP, 2 * LANES), F32),
            pltpu.VMEM((2, KEEP * NP, LANES), F32),
            pltpu.VMEM((2, KEEP * NP, LANES), F32),
            pltpu.VMEM((each, KEEP * KEEP // LOW, LANES), F32),
        ],
        compiler_params=params(28),
        name="chebyshev",
    )(c_all, field, *pieces, lower_edge, upper_edge, tables)
    arrived = [filtered_pieces[0]] + [shift(filtered_pieces[k], k) for k in range(1, slices)]
    filtered = pl.pallas_call(
        functools.partial(unpack_kernel, slices),
        out_shape=jax.ShapeDtypeStruct((block, cols), F32),
        in_specs=in_vmem(slices),
        out_specs=pl.BlockSpec(memory_space=pltpu.VMEM),
        scratch_shapes=[pltpu.VMEM((block * rows, LANES), F32)],
        compiler_params=params(8),
        cost_estimate=pl.CostEstimate(flops=1, bytes_accessed=1, transcendentals=0),
        name="unpack",
    )(*arrived)

    came = lax.all_to_all(spread, ("band", "grid"), split_axis=0, concat_axis=0, tiled=True)
    width = cols // groups
    mine = pl.pallas_call(
        select_kernel,
        out_shape=jax.ShapeDtypeStruct((steps * block, width), F32),
        in_specs=[pl.BlockSpec(memory_space=pltpu.SMEM), pl.BlockSpec(memory_space=pltpu.VMEM)],
        out_specs=pl.BlockSpec(memory_space=pltpu.VMEM),
        compiler_params=params(8),
        name="select",
    )(owners, came.reshape(-1, LANES))

    chips = groups // 2
    ring = list(range(0, chips, 2)) + list(range(1, chips, 2))[::-1]

    def pass_on(x, step):
        pairs = [
            (2 * ring[p] + c, 2 * ring[(p + step) % chips] + c) for p in range(chips) for c in range(2)
        ]
        return lax.ppermute(x, "band", pairs)

    flat = jnp.transpose(rotation, (1, 0, 2)).reshape(rotation.shape[1], steps * block)
    high, low = split(flat)
    table = jnp.concatenate([high, low, high], axis=1)
    rotated_shape = jax.ShapeDtypeStruct((rotation.shape[1], cols), F32)

    def rotate(moves, before):
        arrays = [x for _, _, parts in moves for x in parts]
        plan = tuple((offset, flip, len(parts)) for offset, flip, parts in moves)
        count = len(moves)
        return pl.pallas_call(
            functools.partial(rotate_kernel, plan, chips),
            out_shape=rotated_shape,
            in_specs=[pl.BlockSpec(memory_space=pltpu.VMEM)]
            + [pl.BlockSpec(memory_space=pl.ANY)] * (len(arrays) + len(before)),
            out_specs=pl.BlockSpec(memory_space=pl.ANY),
            scratch_shapes=[
                pltpu.VMEM((count, steps * block, width), F32),
                pltpu.VMEM((min(3, count), rotation.shape[1], width), F32),
                pltpu.SemaphoreType.DMA((2 * count,)),
                pltpu.SemaphoreType.DMA((min(3, count),)),
            ],
            input_output_aliases={len(arrays) + 1: 0} if before else {},
            compiler_params=params(12),
            cost_estimate=pl.CostEstimate(
                flops=200_000_000 * count, bytes_accessed=1_500_000 * count, transcendentals=0
            ),
            name="rotate",
        )(table, *arrays, *before)

    half = chips // 2
    right = left = mine
    ready, later = [(0, 0, [mine]), (0, 1, [other_core(mine)])], []
    rotated = []
    for k in range(1, half):
        right, left = pass_on(right, 1), pass_on(left, -1)
        if k == half - 1:
            filtered, right, left, early = lax.optimization_barrier((filtered, right, left, rotate(ready, rotated)))
            ready, rotated = [], [early]
        ready += [(-k, 0, [right]), (k, 0, [left])] + later
        later = [(-k, 1, [other_core(right)]), (k, 1, [other_core(left)])]
    last = [
        pass_on(lax.slice_in_dim(right, 0, steps * block // 2, axis=0), 1),
        pass_on(lax.slice_in_dim(left, steps * block // 2, steps * block, axis=0), -1),
    ]
    last, early = lax.optimization_barrier((last, rotate(ready, rotated)))
    rotated = rotate([(half, 0, last)] + later, [early])
    rotated = rotate([(half, 1, [other_core(x) for x in last])], [rotated])
    return (filtered, rotated)


def solution(mesh):
    return jax.shard_map(
        body,
        mesh=mesh,
        in_specs=(P("band", "grid"), P("grid", None), P(), P(), P(None, "band", None), P()),
        out_specs=(P("band", "grid"), P("band", "grid")),
        check_vma=False,
    )
```

time: 715 us -> 97.7 us (0.14)
  matrix products: 324 us -> 0 us
  waiting for transfers between devices: 160 us -> 23.1 us
  local copies, waits for them, and re-layouts: 133 us -> 6.46 us
  other arithmetic: 33.2 us -> 0.12 us
  Pallas kernels: 0 us -> 28.7 us
  between operations: 21.1 us -> 2.25 us
    dot_general x20 -> x0, matrix products: 324 us -> none  [the longest x8 86.2 us: body(): jnp.dot(rotation[step_index], arrived, precision=lax.Precision.HIGHEST, p...]
    psum x1 -> x0, waiting for transfers between devices: 113 us -> none  [spread(): return lax.psum(jnp.where(mine, x, jnp.zeros_like(x)), axis)]
    all_to_all x9 -> x0, local copies, waits for them, and re-layouts: 53.6 us -> none  [the longest x5 27 us: to_real(): lax.all_to_all(along_x, 'grid', split_axis=2, concat_axis=1, tiled=True)]
    all_to_all x3 -> x0, waiting for transfers between devices: 46.8 us -> none  [the longest x2 28.2 us: to_plane(): lax.all_to_all(along_y, 'grid', split_axis=1, concat_axis=2, tiled=True)]
    unnamed x37 -> x14, local copies, waits for them, and re-layouts: 46.6 us -> 6.23 us
    all_to_all x4 -> x0, other arithmetic: 29.2 us -> none  [the longest x2 15.2 us: to_real(): lax.all_to_all(along_x, 'grid', split_axis=2, concat_axis=1, tiled=True)]
    pallas_call x0 -> x10, Pallas kernels: none -> 28.7 us  [the longest x1 13.1 us: body(): pl.pallas_call(functools.partial(filter_kernel, slices, ways), out_shape=...]
    ppermute x0 -> x22, waiting for transfers between devices: none -> 23.1 us  [the longest x8 14.7 us: pass_on(): return lax.ppermute(x, 'band', pairs)]
  transfers between devices with their start and end apart: 4 -> 22, of which waited for: 4 -> 10; matrix products, arithmetic and copies ran while one was open for 1% -> 0% of each run, Pallas kernels for 0% -> 13%
where the time goes in v1:
time: 97.7 us; the launch traced here: 97.3 us
  Pallas kernels  28.7 us (29%)
  waiting for transfers between devices  23.1 us (24%)
  blocking collectives  20.4 us (21%)
  starting transfers between devices  16.4 us (17%)
  local copies, waits for them, and re-layouts  6.46 us (7%)
  between operations  2.25 us (2%)
    all_to_all x1, blocking collectives, body(): lax.all_to_all(spread, ('band', 'grid'), split_axis=0, concat_axis=0, til...  20.4 us
    ppermute x8, waiting for transfers between devices, pass_on(): return lax.ppermute(x, 'band', pairs)  14.7 us
    pallas_call x1, Pallas kernels, body(): pl.pallas_call(functools.partial(filter_kernel, slices, ways), out_shape=...  13.1 us
    pallas_call x4, Pallas kernels, rotate(): pl.pallas_call(functools.partial(rotate_kernel, plan, chips), out_shape=r...  9.51 us
    ppermute x8, starting transfers between devices, pass_on(): return lax.ppermute(x, 'band', pairs)  7.84 us
    unnamed x14, local copies, waits for them, and re-layouts  6.23 us
    ppermute x1, waiting for transfers between devices, shift_diagonal(): return lax.ppermute(x, ('band', 'grid'), pairs)  5.52 us
    ppermute x2, starting transfers between devices, shift(): lax.ppermute(x, 'grid', [(i, (i + k) % slices) for i in range(slices)])  4.8 us
  transfers between devices with their start and end apart: 22, of which 10 were waited for; matrix products, arithmetic and copies ran while one was open for 0% of the time, Pallas kernels for 13%

profile of v1, /device:TPU:0, one launch (start us, length us, event | category | flops | bytes accessed | tf_op | source)
XLA Modules:
  0.0 97.3 jit_solution(14134756315484003235)
XLA Ops:
  2.0 3.0 %collective-permute-start = (f32[4,128,128]{2,1,0:T(8,128)S(1)}, f32[4,128,128]{2,1,0:T(8,128)S(1)}, u32[]{:S(2)}, u32[]{:S(2)}) collective-permute-start(f32[4,128,128]{2,1,0:T(8,128)S(1)} %get-tuple-element.23), channel_id=1, source_target_pairs={{0,1},{1,0},{2,3},{3,2},{4,5},{5,4},{6,7},{7,6},{8,9},{9,8},{10,11... | collective-permute-start | bytes 786440 | tf_op jit(solution)/shard_map/ppermute | solution.py:359
  5.0 1.5 %copy-done.2 = f32[48,9216]{1,0:T(8,128)S(1)} copy-done((f32[48,9216]{1,0:T(8,128)S(1)}, f32[48,9216]{1,0:T(8,128)}, u32[]{:S(2)}) %copy-start.2) | copy-done | bytes 1769496
  7.4 1.3 %project.1.refs_2_ = f32[24,4096]{1,0:T(8,128)S(1)} custom-call(f32[48,9216]{1,0:T(8,128)S(1)} %copy-done.2, bf16[160,384]{1,0:T(8,128)(2,1)S(1)} %copy-done.4, f32[4,128,128]{2,1,0:T(8,128)S(1)} %get-tuple-element.25.after.refs_0_), custom_call_target="tpu_custom_call" | custom-call | tf_op jit(solution)/shard_map/project/pallas_call | solution.py:386
  8.7 2.6 %collective-permute-done.refs_1_ = f32[4,128,128]{2,1,0:T(8,128)S(1)} collective-permute-done((f32[4,128,128]{2,1,0:T(8,128)S(1)}, f32[4,128,128]{2,1,0:T(8,128)S(1)}, u32[]{:S(2)}, u32[]{:S(2)}) %collective-permute-start) | collective-permute-done | bytes 262176 | tf_op jit(solution)/shard_map/ppermute | solution.py:359
  11.6 1.5 %collective-permute-start.2 = (f32[24,4096]{1,0:T(8,128)S(1)}, f32[24,4096]{1,0:T(8,128)S(1)}, u32[]{:S(2)}, u32[]{:S(2)}) collective-permute-start(f32[24,4096]{1,0:T(8,128)S(1)} %project.1.refs_2_), channel_id=1, source_target_pairs={{0,2},{2,0},{4,6},{6,4},{8,10},{10,8},{12,14},{14,12},{16,18},{18,... | collective-permute-start | bytes 1179656 | tf_op jit(solution)/shard_map/ppermute | solution.py:368
  14.3 2.6 %synthesis.1 = (f32[32,32,128]{2,1,0:T(8,128)S(1)}, f32[4096,256]{1,0:T(8,128)S(1)}) custom-call(f32[4,128,128]{2,1,0:T(8,128)S(1)} %get-tuple-element.25.after.refs_0_, f32[4,128,128]{2,1,0:T(8,128)S(1)} %collective-permute-done.refs_1_, bf16[832,384]{1,0:T(8,128)(2,1)S(1)} %copy-done), custom_call_target="tpu_custom_call" | custom-call | flops 1 | bytes 1 | tf_op jit(solution)/shard_map/synthesis/pallas_call | solution.py:412
  16.9 5.5 %collective-permute-done.1.refs_5_ = f32[24,4096]{1,0:T(8,128)S(1)} collective-permute-done((f32[24,4096]{1,0:T(8,128)S(1)}, f32[24,4096]{1,0:T(8,128)S(1)}, u32[]{:S(2)}, u32[]{:S(2)}) %collective-permute-start.1) | collective-permute-done | bytes 393248 | tf_op jit(solution)/shard_map/ppermute | solution.py:365
  24.2 1.1 %copy-done.1 = bf16[832,384]{1,0:T(8,128)(2,1)S(1)} copy-done((bf16[832,384]{1,0:T(8,128)(2,1)S(1)}, bf16[832,384]{1,0:T(8,128)(2,1)}, u32[]{:S(2)}) %copy-start.1) | copy-done | bytes 639000
  25.2 13.1 %chebyshev.1 = (f32[4,128,128]{2,1,0:T(8,128)S(1)}, f32[4,128,128]{2,1,0:T(8,128)S(1)}, f32[32,32,128]{2,1,0:T(8,128)S(1)}) custom-call(f32[32,32,128]{2,1,0:T(8,128)S(1)} %get-tuple-element.29.refs_0_, f32[4096,256]{1,0:T(8,128)S(1)} %get-tuple-element.30.refs_1_, f32[24,4096]{1,0:T(8,128)S(1)} %project.1.refs_2_, ...), custom_call_target="tpu_custom_call" | custom-call | tf_op jit(solution)/shard_map/chebyshev/pallas_call | solution.py:436
  38.4 20.4 %all_to_all.5 = f32[32,32,128]{2,1,0:T(8,128)S(1)} all-to-all(f32[32,32,128]{2,1,0:T(8,128)S(1)} %get-tuple-element.34), channel_id=1, replica_groups=mesh['band'=16,'grid'=2] {'band','grid'}, dimensions={0} | all-to-all | bytes 1048576 | tf_op jit(solution)/shard_map/all_to_all | solution.py:466
  60.7 1.4 %collective-permute-start.8 = (f32[64,1024]{1,0:T(8,128)S(1)}, f32[64,1024]{1,0:T(8,128)S(1)}, u32[]{:S(2)}, u32[]{:S(2)}) collective-permute-start(f32[64,1024]{1,0:T(8,128)S(1)} %select.1.refs_0_), channel_id=1, source_target_pairs={{0,4},{2,6},{8,0},{10,2},{16,8},{18,10},{24,16},{26,18},{28,24},{3... | collective-permute-start | bytes 786440 | tf_op jit(solution)/shard_map/ppermute | solution.py:484
  62.1 1.8 %collective-permute-start.4 = (f32[4,128,128]{2,1,0:T(8,128)S(1)}, f32[4,128,128]{2,1,0:T(8,128)S(1)}, u32[]{:S(2)}, u32[]{:S(2)}) collective-permute-start(f32[4,128,128]{2,1,0:T(8,128)S(1)} %get-tuple-element.33), channel_id=1, source_target_pairs={{0,1},{1,0},{2,3},{3,2},{4,5},{5,4},{6,7},{7,6},{8,9},{9,8},{10,11... | collective-permute-start | bytes 786440 | tf_op jit(solution)/shard_map/ppermute | solution.py:359
  63.9 5.3 %collective-permute-done.5.refs_2_ = f32[64,1024]{1,0:T(8,128)S(1)} collective-permute-done((f32[64,1024]{1,0:T(8,128)S(1)}, f32[64,1024]{1,0:T(8,128)S(1)}, u32[]{:S(2)}, u32[]{:S(2)}) %collective-permute-start.5) | collective-permute-done | bytes 262176 | tf_op jit(solution)/shard_map/ppermute | solution.py:484
  69.9 1.3 %collective-permute-start.9 = (f32[64,1024]{1,0:T(8,128)S(1)}, f32[64,1024]{1,0:T(8,128)S(1)}, u32[]{:S(2)}, u32[]{:S(2)}) collective-permute-start(f32[64,1024]{1,0:T(8,128)S(1)} %collective-permute-done.8.refs_3_), channel_id=1, source_target_pairs={{0,4},{2,6},{8,0},{10,2},{16,8},{18,10},{24,16},{26,18},{28,24},{3... | collective-permute-start | bytes 786440 | tf_op jit(solution)/shard_map/ppermute | solution.py:484
  72.0 5.6 %collective-permute-done.6.refs_4_ = f32[64,1024]{1,0:T(8,128)S(1)} collective-permute-done((f32[64,1024]{1,0:T(8,128)S(1)}, f32[64,1024]{1,0:T(8,128)S(1)}, u32[]{:S(2)}, u32[]{:S(2)}) %collective-permute-start.6) | collective-permute-done | bytes 262176 | tf_op jit(solution)/shard_map/ppermute | solution.py:484
  78.3 1.4 %collective-permute-start.10 = (f32[64,1024]{1,0:T(8,128)S(1)}, f32[64,1024]{1,0:T(8,128)S(1)}, u32[]{:S(2)}, u32[]{:S(2)}) collective-permute-start(f32[64,1024]{1,0:T(8,128)S(1)} %collective-permute-done.9.refs_5_), channel_id=1, source_target_pairs={{0,4},{2,6},{8,0},{10,2},{16,8},{18,10},{24,16},{26,18},{28,24},{3... | collective-permute-start | bytes 786440 | tf_op jit(solution)/shard_map/ppermute | solution.py:484
  79.7 1.1 %unpack.1 = f32[8,16384]{1,0:T(8,128)} custom-call(f32[4,128,128]{2,1,0:T(8,128)S(1)} %get-tuple-element.32.refs_0_, f32[4,128,128]{2,1,0:T(8,128)S(1)} %collective-permute-done.4.refs_1_), custom_call_target="tpu_custom_call" | custom-call | flops 1 | bytes 1 | tf_op jit(solution)/shard_map/unpack/pallas_call | solution.py:455
  81.1 3.6 %rotate.4.refs_4_ = f32[192,16384]{1,0:T(8,128)} custom-call(bf16[192,192]{1,0:T(8,128)(2,1)S(1)} %pad_maximum_fusion.table, f32[64,1024]{1,0:T(8,128)S(1)} %select.1.refs_0_, f32[64,1024]{1,0:T(8,128)S(1)} %collective-permute-done.11.refs_1_, f32[64,1024]{1,0:T(8,128)S(1)} %collective-permute-done.5.refs_2_, f32[64,1024]{1,0:T(8,128)S(1)} %collective-permute-done.8.refs_3_, ...), custom_call_target="tpu_custom_call" | custom-call | flops 1600000000 | bytes 12000000 | tf_op jit(solution)/shard_map/rotate/pallas_call | solution.py:495
  84.7 2.2 %collective-permute-done.10.refs_1_ = f32[64,1024]{1,0:T(8,128)S(1)} collective-permute-done((f32[64,1024]{1,0:T(8,128)S(1)}, f32[64,1024]{1,0:T(8,128)S(1)}, u32[]{:S(2)}, u32[]{:S(2)}) %collective-permute-start.10) | collective-permute-done | bytes 262176 | tf_op jit(solution)/shard_map/ppermute | solution.py:484
  87.8 1.7 %collective-permute-start.15 = (f32[32,1024]{1,0:T(8,128)S(1)}, f32[32,1024]{1,0:T(8,128)S(1)}, u32[]{:S(2)}, u32[]{:S(2)}) collective-permute-start(f32[32,1024]{1,0:T(8,128)S(1)} %slice.7), channel_id=1, source_target_pairs={{0,4},{2,6},{8,0},{10,2},{16,8},{18,10},{24,16},{26,18},{28,24},{3... | collective-permute-start | bytes 393224 | tf_op jit(solution)/shard_map/ppermute | solution.py:484
  89.5 2.2 %rotate.5.refs_4_ = f32[192,16384]{1,0:T(8,128)} custom-call(bf16[192,192]{1,0:T(8,128)(2,1)S(1)} %pad_maximum_fusion.table, f32[64,1024]{1,0:T(8,128)S(1)} %collective-permute-done.7.refs_0_, f32[64,1024]{1,0:T(8,128)S(1)} %collective-permute-done.10.refs_1_, f32[64,1024]{1,0:T(8,128)S(1)} %collective-permute-done.16.refs_2_, ...), custom_call_target="tpu_custom_call", output_to_operand_aliasing={{}: (5, {})} | custom-call | flops 800000000 | bytes 6000000 | tf_op jit(solution)/shard_map/rotate/pallas_call | solution.py:495
  91.8 1.1 %collective-permute-done.14.refs_0_ = f32[32,1024]{1,0:T(8,128)S(1)} collective-permute-done((f32[32,1024]{1,0:T(8,128)S(1)}, f32[32,1024]{1,0:T(8,128)S(1)}, u32[]{:S(2)}, u32[]{:S(2)}) %collective-permute-start.14) | collective-permute-done | bytes 131104 | tf_op jit(solution)/shard_map/ppermute | solution.py:484
  93.5 2.1 %rotate.6.refs_2_ = f32[192,16384]{1,0:T(8,128)} custom-call(bf16[192,192]{1,0:T(8,128)(2,1)S(1)} %pad_maximum_fusion.table, f32[32,1024]{1,0:T(8,128)S(1)} %collective-permute-done.14.refs_0_, f32[32,1024]{1,0:T(8,128)S(1)} %collective-permute-done.15.refs_1_, f32[64,1024]{1,0:T(8,128)S(1)} %collective-permute-done.20.refs_2_, ...), custom_call_target="tpu_custom_call", output_to_operand_aliasing={{}: (5, {})} | custom-call | flops 600000000 | bytes 4500000 | tf_op jit(solution)/shard_map/rotate/pallas_call | solution.py:495
  95.6 1.5 %rotate.7 = f32[192,16384]{1,0:T(8,128)} custom-call(bf16[192,192]{1,0:T(8,128)(2,1)S(1)} %pad_maximum_fusion.table, f32[32,1024]{1,0:T(8,128)S(1)} %collective-permute-done.18.refs_0_, f32[32,1024]{1,0:T(8,128)S(1)} %collective-permute-done.19.refs_1_, f32[192,16384]{1,0:T(8,128)} %rotate.6.refs_2_), custom_call_target="tpu_custom_call", output_to_operand_aliasing={{}: (3, {})} | custom-call | flops 200000000 | bytes 1500000 | tf_op jit(solution)/shard_map/rotate/pallas_call | solution.py:495
  (52 shorter events, 10.0 us)
Async XLA Ops:
  1.7 69.5 %copy-start.6 = (f32[8,192,8]{1,2,0:T(8,128)S(1)}, f32[8,192,8]{1,2,0:T(8,128)}, u32[]{:S(2)}) copy-start(f32[8,192,8]{1,2,0:T(8,128)} %param.12) | copy-start | bytes 147460
  2.0 9.3 %collective-permute-start = (f32[4,128,128]{2,1,0:T(8,128)S(1)}, f32[4,128,128]{2,1,0:T(8,128)S(1)}, u32[]{:S(2)}, u32[]{:S(2)}) collective-permute-start(f32[4,128,128]{2,1,0:T(8,128)S(1)} %get-tuple-element.23), channel_id=1, source_target_pairs={{0,1},{1,0},{2,3},{3,2},{4,5},{5,4},{6,7},{7,6},{8,9},{9,8},{10,11... | collective-permute-start | bytes 786440 | tf_op jit(solution)/shard_map/ppermute | solution.py:359
  5.0 1.5 %copy-start.2 = (f32[48,9216]{1,0:T(8,128)S(1)}, f32[48,9216]{1,0:T(8,128)}, u32[]{:S(2)}) copy-start(f32[48,9216]{1,0:T(8,128)} %v_ref.1) | copy-start | bytes 5308420
  11.3 11.1 %collective-permute-start.1 = (f32[24,4096]{1,0:T(8,128)S(1)}, f32[24,4096]{1,0:T(8,128)S(1)}, u32[]{:S(2)}, u32[]{:S(2)}) collective-permute-start(f32[24,4096]{1,0:T(8,128)S(1)} %project.1.refs_2_), channel_id=1, source_target_pairs={{0,3},{1,2},{2,1},{3,0},{4,7},{5,6},{6,5},{7,4},{8,11},{9,10},{10,... | collective-permute-start | bytes 1179656 | tf_op jit(solution)/shard_map/ppermute | solution.py:365
  11.6 12.2 %collective-permute-start.2 = (f32[24,4096]{1,0:T(8,128)S(1)}, f32[24,4096]{1,0:T(8,128)S(1)}, u32[]{:S(2)}, u32[]{:S(2)}) collective-permute-start(f32[24,4096]{1,0:T(8,128)S(1)} %project.1.refs_2_), channel_id=1, source_target_pairs={{0,2},{2,0},{4,6},{6,4},{8,10},{10,8},{12,14},{14,12},{16,18},{18,... | collective-permute-start | bytes 1179656 | tf_op jit(solution)/shard_map/ppermute | solution.py:368
  22.4 1.7 %collective-permute-start.3 = (f32[24,4096]{1,0:T(8,128)S(1)}, f32[24,4096]{1,0:T(8,128)S(1)}, u32[]{:S(2)}, u32[]{:S(2)}) collective-permute-start(f32[24,4096]{1,0:T(8,128)S(1)} %collective-permute-done.1.refs_5_), channel_id=1, source_target_pairs={{0,2},{2,0},{4,6},{6,4},{8,10},{10,8},{12,14},{14,12},{16,18},{18,... | collective-permute-start | bytes 1179656 | tf_op jit(solution)/shard_map/ppermute | solution.py:368
  60.0 9.1 %collective-permute-start.5 = (f32[64,1024]{1,0:T(8,128)S(1)}, f32[64,1024]{1,0:T(8,128)S(1)}, u32[]{:S(2)}, u32[]{:S(2)}) collective-permute-start(f32[64,1024]{1,0:T(8,128)S(1)} %select.1.refs_0_), channel_id=1, source_target_pairs={{0,8},{2,10},{8,16},{10,18},{16,24},{18,26},{24,28},{26,30},{28,20... | collective-permute-start | bytes 786440 | tf_op jit(solution)/shard_map/ppermute | solution.py:484
  60.7 9.2 %collective-permute-start.8 = (f32[64,1024]{1,0:T(8,128)S(1)}, f32[64,1024]{1,0:T(8,128)S(1)}, u32[]{:S(2)}, u32[]{:S(2)}) collective-permute-start(f32[64,1024]{1,0:T(8,128)S(1)} %select.1.refs_0_), channel_id=1, source_target_pairs={{0,4},{2,6},{8,0},{10,2},{16,8},{18,10},{24,16},{26,18},{28,24},{3... | collective-permute-start | bytes 786440 | tf_op jit(solution)/shard_map/ppermute | solution.py:484
  62.1 9.4 %collective-permute-start.4 = (f32[4,128,128]{2,1,0:T(8,128)S(1)}, f32[4,128,128]{2,1,0:T(8,128)S(1)}, u32[]{:S(2)}, u32[]{:S(2)}) collective-permute-start(f32[4,128,128]{2,1,0:T(8,128)S(1)} %get-tuple-element.33), channel_id=1, source_target_pairs={{0,1},{1,0},{2,3},{3,2},{4,5},{5,4},{6,7},{7,6},{8,9},{9,8},{10,11... | collective-permute-start | bytes 786440 | tf_op jit(solution)/shard_map/ppermute | solution.py:359
  63.8 14.3 %collective-permute-start.11 = (f32[64,1024]{1,0:T(8,128)S(1)}, f32[64,1024]{1,0:T(8,128)S(1)}, u32[]{:S(2)}, u32[]{:S(2)}) collective-permute-start(f32[64,1024]{1,0:T(8,128)S(1)} %select.1.refs_0_), channel_id=1, source_target_pairs={{0,2},{2,0},{4,6},{6,4},{8,10},{10,8},{12,14},{14,12},{16,18},{18,... | collective-permute-start | bytes 786440 | tf_op jit(solution)/shard_map/ppermute | solution.py:368
  69.1 8.4 %collective-permute-start.6 = (f32[64,1024]{1,0:T(8,128)S(1)}, f32[64,1024]{1,0:T(8,128)S(1)}, u32[]{:S(2)}, u32[]{:S(2)}) collective-permute-start(f32[64,1024]{1,0:T(8,128)S(1)} %collective-permute-done.5.refs_2_), channel_id=1, source_target_pairs={{0,8},{2,10},{8,16},{10,18},{16,24},{18,26},{24,28},{26,30},{28,20... | collective-permute-start | bytes 786440 | tf_op jit(solution)/shard_map/ppermute | solution.py:484
  69.9 8.4 %collective-permute-start.9 = (f32[64,1024]{1,0:T(8,128)S(1)}, f32[64,1024]{1,0:T(8,128)S(1)}, u32[]{:S(2)}, u32[]{:S(2)}) collective-permute-start(f32[64,1024]{1,0:T(8,128)S(1)} %collective-permute-done.8.refs_3_), channel_id=1, source_target_pairs={{0,4},{2,6},{8,0},{10,2},{16,8},{18,10},{24,16},{26,18},{28,24},{3... | collective-permute-start | bytes 786440 | tf_op jit(solution)/shard_map/ppermute | solution.py:484
  71.4 9.5 %collective-permute-start.12 = (f32[64,1024]{1,0:T(8,128)S(1)}, f32[64,1024]{1,0:T(8,128)S(1)}, u32[]{:S(2)}, u32[]{:S(2)}) collective-permute-start(f32[64,1024]{1,0:T(8,128)S(1)} %collective-permute-done.5.refs_2_), channel_id=1, source_target_pairs={{0,2},{2,0},{4,6},{6,4},{8,10},{10,8},{12,14},{14,12},{16,18},{18,... | collective-permute-start | bytes 786440 | tf_op jit(solution)/shard_map/ppermute | solution.py:368
  71.5 9.6 %collective-permute-start.13 = (f32[64,1024]{1,0:T(8,128)S(1)}, f32[64,1024]{1,0:T(8,128)S(1)}, u32[]{:S(2)}, u32[]{:S(2)}) collective-permute-start(f32[64,1024]{1,0:T(8,128)S(1)} %collective-permute-done.8.refs_3_), channel_id=1, source_target_pairs={{0,2},{2,0},{4,6},{6,4},{8,10},{10,8},{12,14},{14,12},{16,18},{18,... | collective-permute-start | bytes 786440 | tf_op jit(solution)/shard_map/ppermute | solution.py:368
  77.5 9.4 %collective-permute-start.7 = (f32[64,1024]{1,0:T(8,128)S(1)}, f32[64,1024]{1,0:T(8,128)S(1)}, u32[]{:S(2)}, u32[]{:S(2)}) collective-permute-start(f32[64,1024]{1,0:T(8,128)S(1)} %collective-permute-done.6.refs_4_), channel_id=1, source_target_pairs={{0,8},{2,10},{8,16},{10,18},{16,24},{18,26},{24,28},{26,30},{28,20... | collective-permute-start | bytes 786440 | tf_op jit(solution)/shard_map/ppermute | solution.py:484
  78.2 9.6 %collective-permute-start.16 = (f32[64,1024]{1,0:T(8,128)S(1)}, f32[64,1024]{1,0:T(8,128)S(1)}, u32[]{:S(2)}, u32[]{:S(2)}) collective-permute-start(f32[64,1024]{1,0:T(8,128)S(1)} %collective-permute-done.6.refs_4_), channel_id=1, source_target_pairs={{0,2},{2,0},{4,6},{6,4},{8,10},{10,8},{12,14},{14,12},{16,18},{18,... | collective-permute-start | bytes 786440 | tf_op jit(solution)/shard_map/ppermute | solution.py:368
  78.3 8.6 %collective-permute-start.10 = (f32[64,1024]{1,0:T(8,128)S(1)}, f32[64,1024]{1,0:T(8,128)S(1)}, u32[]{:S(2)}, u32[]{:S(2)}) collective-permute-start(f32[64,1024]{1,0:T(8,128)S(1)} %collective-permute-done.9.refs_5_), channel_id=1, source_target_pairs={{0,4},{2,6},{8,0},{10,2},{16,8},{18,10},{24,16},{26,18},{28,24},{3... | collective-permute-start | bytes 786440 | tf_op jit(solution)/shard_map/ppermute | solution.py:484
  80.9 8.7 %collective-permute-start.17 = (f32[64,1024]{1,0:T(8,128)S(1)}, f32[64,1024]{1,0:T(8,128)S(1)}, u32[]{:S(2)}, u32[]{:S(2)}) collective-permute-start(f32[64,1024]{1,0:T(8,128)S(1)} %collective-permute-done.9.refs_5_), channel_id=1, source_target_pairs={{0,2},{2,0},{4,6},{6,4},{8,10},{10,8},{12,14},{14,12},{16,18},{18,... | collective-permute-start | bytes 786440 | tf_op jit(solution)/shard_map/ppermute | solution.py:368
  86.9 6.6 %collective-permute-start.20 = (f32[64,1024]{1,0:T(8,128)S(1)}, f32[64,1024]{1,0:T(8,128)S(1)}, u32[]{:S(2)}, u32[]{:S(2)}) collective-permute-start(f32[64,1024]{1,0:T(8,128)S(1)} %collective-permute-done.7.refs_0_), channel_id=1, source_target_pairs={{0,2},{2,0},{4,6},{6,4},{8,10},{10,8},{12,14},{14,12},{16,18},{18,... | collective-permute-start | bytes 786440 | tf_op jit(solution)/shard_map/ppermute | solution.py:368
  86.9 6.6 %collective-permute-start.21 = (f32[64,1024]{1,0:T(8,128)S(1)}, f32[64,1024]{1,0:T(8,128)S(1)}, u32[]{:S(2)}, u32[]{:S(2)}) collective-permute-start(f32[64,1024]{1,0:T(8,128)S(1)} %collective-permute-done.10.refs_1_), channel_id=1, source_target_pairs={{0,2},{2,0},{4,6},{6,4},{8,10},{10,8},{12,14},{14,12},{16,18},{18,... | collective-permute-start | bytes 786440 | tf_op jit(solution)/shard_map/ppermute | solution.py:368
  87.4 5.5 %collective-permute-start.14 = (f32[32,1024]{1,0:T(8,128)S(1)}, f32[32,1024]{1,0:T(8,128)S(1)}, u32[]{:S(2)}, u32[]{:S(2)}) collective-permute-start(f32[32,1024]{1,0:T(8,128)S(1)} %slice.6), channel_id=1, source_target_pairs={{0,8},{2,10},{8,16},{10,18},{16,24},{18,26},{24,28},{26,30},{28,20... | collective-permute-start | bytes 393224 | tf_op jit(solution)/shard_map/ppermute | solution.py:484
  87.8 5.2 %collective-permute-start.15 = (f32[32,1024]{1,0:T(8,128)S(1)}, f32[32,1024]{1,0:T(8,128)S(1)}, u32[]{:S(2)}, u32[]{:S(2)}) collective-permute-start(f32[32,1024]{1,0:T(8,128)S(1)} %slice.7), channel_id=1, source_target_pairs={{0,4},{2,6},{8,0},{10,2},{16,8},{18,10},{24,16},{26,18},{28,24},{3... | collective-permute-start | bytes 393224 | tf_op jit(solution)/shard_map/ppermute | solution.py:484
  93.0 2.6 %collective-permute-start.18 = (f32[32,1024]{1,0:T(8,128)S(1)}, f32[32,1024]{1,0:T(8,128)S(1)}, u32[]{:S(2)}, u32[]{:S(2)}) collective-permute-start(f32[32,1024]{1,0:T(8,128)S(1)} %collective-permute-done.14.refs_0_), channel_id=1, source_target_pairs={{0,2},{2,0},{4,6},{6,4},{8,10},{10,8},{12,14},{14,12},{16,18},{18,... | collective-permute-start | bytes 393224 | tf_op jit(solution)/shard_map/ppermute | solution.py:368
  93.0 2.6 %collective-permute-start.19 = (f32[32,1024]{1,0:T(8,128)S(1)}, f32[32,1024]{1,0:T(8,128)S(1)}, u32[]{:S(2)}, u32[]{:S(2)}) collective-permute-start(f32[32,1024]{1,0:T(8,128)S(1)} %collective-permute-done.15.refs_1_), channel_id=1, source_target_pairs={{0,2},{2,0},{4,6},{6,4},{8,10},{10,8},{12,14},{14,12},{16,18},{18,... | collective-permute-start | bytes 393224 | tf_op jit(solution)/shard_map/ppermute | solution.py:368
  (5 other events, 4.8 us)

commit v2 on v1

--- a/solution.py
+++ b/solution.py
@@ -16,6 +16,7 @@
 LOW = 4
 LANES = LOW * KEEP
 QUAD = 4
+GROUP = 4
 MIB = 1024 * 1024
 
 F32 = jnp.float32
@@ -38,14 +39,14 @@
 
 PROJECT = np.linalg.solve(product_basis(POINTS).T, product_basis(2.0 * np.pi * np.arange(NG) / NG).T)
 TABLE = cas(POINTS[:, None] * SIGNED[None, :]) / np.sqrt(NG)
+Y_ORDER = np.arange(NP).reshape(NP // 2, 2).T.reshape(-1)
 KX_ORDER = np.arange(KEEP).reshape(KEEP // LOW, LOW).T.reshape(-1)
 
 
-ROW_SYN, ROW_PROJECT, ROW_Y_ANA = 0, NP, 2 * NP
-ROW_X_ANA = ROW_Y_ANA + KEEP
-ROW_Z_SYN = ROW_X_ANA + KEEP
+ROW_SYN, ROW_ANA = 0, NP
+ROW_Z_SYN = ROW_ANA + 2 * KEEP
 ROW_Z_ANA = ROW_Z_SYN + 3 * LANES
-ROW_END = ROW_Z_ANA + 2 * LANES
+ROW_PROJECT = ROW_Z_ANA + 2 * LANES
 
 
 def halves(table):
@@ -59,6 +60,13 @@
     return np.concatenate([high, low, high], axis=1)
 
 
+def summed_table(table):
+    high, low = halves(table)
+    return np.concatenate(
+        [np.concatenate([high, high], axis=1), np.concatenate([low, np.zeros_like(low)], axis=1)], axis=0
+    )
+
+
 def split(x):
     high = x.astype(BF16)
     return high, (x - high.astype(F32)).astype(BF16)
@@ -67,6 +75,19 @@
 def stack(x):
     high, low = split(x)
     return jnp.concatenate([high, high, low], axis=0)
+
+
+def times(table, parts):
+    res = mm(table, stack(jnp.concatenate(parts, axis=1)))
+    width = parts[0].shape[1]
+    return [res[:, i * width:(i + 1) * width] for i in range(len(parts))]
+
+
+def times_summed(table, parts):
+    res = mm(table, jnp.concatenate(split(jnp.concatenate(parts, axis=1)), axis=0))
+    half, width = res.shape[0] // 2, parts[0].shape[1]
+    res = res[:half] + res[half:]
+    return [res[:, i * width:(i + 1) * width] for i in range(len(parts))]
 
 
 def mm(a, b):
@@ -110,7 +131,7 @@
 
 
 def unpack_kernel(slices, *refs):
-    ins, out, scratch = refs[:slices], refs[slices], refs[slices + 1]
+    ins, (out, scratch) = refs[:slices], refs[slices:]
     rows = scratch.shape[0] // 8
     each = 8 // slices
     g = lax.axis_index("grid")
@@ -138,7 +159,7 @@
     y_table = tables[NG:NG + NP, :3 * NG]
     for p in range(0, planes, 2):
         x = jnp.concatenate([first[pl.ds(p + i, NG, stride=planes), :] for i in range(2)], axis=1)
-        res = mm(y_table, stack(x))
+        res, = times(y_table, [x])
         for i in range(2):
             second[pl.ds(p + i, NP, stride=planes), :] = res[:, i * LANES:(i + 1) * LANES]
     left = lax.broadcasted_iota(jnp.int32, (1, LANES), 1) < NP
@@ -148,9 +169,11 @@
         out_ref[:, j * LANES:(j + 1) * LANES] = jnp.where(left, even, odd)
 
 
-def synthesis_kernel(slices, *refs):
-    coeffs, tables = refs[:slices], refs[slices]
-    c_all, field, z_first, x1 = refs[slices + 1:]
+def synthesis_kernel(slices, ways, *refs):
+    coeffs, pieces, (tables, who) = refs[:slices], refs[slices:slices + ways], refs[slices + ways:slices + ways + 2]
+    c_all, field, tables_out, projection, who_out, z_first, x1, planes_now = refs[slices + ways + 2:]
+    tables_out[...] = tables[...]
+    who_out[...] = who[...]
     g = lax.axis_index("grid")
     each, rows, _ = coeffs[0].shape
     ky_local = KEEP // slices
@@ -162,11 +185,38 @@
             c_all[pl.ds(source * ky_local, ky_local), low * kx_high:(low + 1) * kx_high, :] = part.reshape(
                 ky_local, kx_high, LANES
             )
-    synthesize(c_all, tables, z_first, x1, lambda x, value: put(field, x * NP, value))
+    project_x(pieces, g, tables, planes_now, lambda lanes, value: put_lanes(projection, lanes, value))
+    synthesize(c_all, tables, z_first, x1, lambda x, values: put(field, x * NP, jnp.concatenate(values, axis=0)))
+
+
+def put_lanes(ref, lanes, value):
+    ref[:, lanes] = value
+
+
+def project_x(pieces, source, tables, planes_now, give):
+    ways = len(pieces)
+    planes = pieces[0].shape[0]
+    slot = planes_now.shape[0] // ways
+    core = lax.rem(lax.axis_index("band"), ways)
+    if slot != planes:
+        planes_now[...] = jnp.zeros_like(planes_now)
+    for w in range(ways):
+        start = pl.multiple_of(lax.rem(core + w, ways) * slot, slot)
+        planes_now[pl.ds(start, planes), :] = pieces[w][...]
+    row = pl.multiple_of(ROW_PROJECT + source * NP, NP)
+    table = tables[pl.ds(row, NP), :][:, :3 * ways * slot]
+    width = 512
+    for lane in range(0, NP * NP, width):
+        give(slice(lane, lane + width), mm(table, stack(planes_now[:, lane:lane + width])))
 
 
 def put(ref, row, value):
     ref[row:row + value.shape[0], :] = value
+
+
+def put_wide(ref, row, value):
+    for h in range(2):
+        ref[h, row:row + value.shape[0], :] = value[:, h * LANES:(h + 1) * LANES]
 
 
 def wide(ref, start, size, stride):
@@ -180,48 +230,45 @@
         high, low = split(u_all[ky:ky + group].reshape(group * KEEP, LANES))
         put(z_first, ky * KEEP, mm(jnp.concatenate([high, high, low], axis=1), z_syn))
     xs = tables[ROW_SYN:ROW_SYN + NP, :3 * KEEP]
-    for ky in range(KEEP):
-        res = mm(xs, stack(z_first[ky * KEEP:(ky + 1) * KEEP, :]))
-        for h in range(2):
-            x1[h, ky * NP:(ky + 1) * NP, :] = res[:, h * LANES:(h + 1) * LANES]
+    for ky in range(0, KEEP, GROUP):
+        parts = [z_first[(ky + i) * KEEP:(ky + i + 1) * KEEP, :] for i in range(GROUP)]
+        for i, res in enumerate(times(xs, parts)):
+            put_wide(x1, (ky + i) * NP, res)
     ys = tables[ROW_SYN:ROW_SYN + NP, LANES:LANES + 3 * KEEP]
-    for x in range(NP):
-        give(x, mm(ys, stack(wide(x1, x, KEEP, NP))))
+    for x in range(0, NP, GROUP):
+        give(x, times(ys, [wide(x1, x + i, KEEP, NP) for i in range(GROUP)]))
 
 
 def filter_kernel(slices, ways, *refs):
-    c_all, field = refs[:2]
-    pieces = refs[2:2 + slices * ways]
-    refs = refs[2 + slices * ways:]
+    c_all, field, projection = refs[:3]
+    pieces = refs[3:3 + (slices - 1) * ways]
+    refs = refs[3 + (slices - 1) * ways:]
     lower, upper, tables = refs[:3]
     outs, spread = refs[3:3 + slices], refs[3 + slices]
-    planes_all, vt, u_all, z_first, x1, y2, packed = refs[4 + slices:]
+    planes_now, total, vx, u_all, z_first, x1, y2, packed = refs[4 + slices:]
     g = lax.axis_index("grid")
-    core = lax.rem(lax.axis_index("band"), ways)
     each, rows, _ = outs[0].shape
     kx_high = KEEP // LOW
-    planes = pieces[0].shape[0]
-    slot = planes_all.shape[0] // (slices * ways)
-    if slot != planes:
-        planes_all[...] = jnp.zeros_like(planes_all)
-
-    for k in range(slices):
-        source = lax.rem(g + slices - k, slices)
-        for w in range(ways):
-            half = lax.rem(core + w, ways)
-            start = pl.multiple_of((source * ways + half) * slot, slot)
-            planes_all[pl.ds(start, planes), :] = pieces[k * ways + w][...]
-    x_table = tables[ROW_PROJECT:ROW_PROJECT + NP, :3 * planes_all.shape[0]]
+
+    def add(lanes, value):
+        total[:, lanes] += value
+
+    def finish_projection(lanes, value):
+        value = value + (projection if slices == 2 else total)[:, lanes]
+        for j in range(value.shape[1] // LANES):
+            put(vx, (lanes.start // LANES + j) * NP, value[:, j * LANES:(j + 1) * LANES])
+
+    if slices > 2:
+        total[...] = projection[...]
+    for k in range(1, slices):
+        project_x(
+            pieces[(k - 1) * ways:k * ways],
+            lax.rem(g + slices - k, slices),
+            tables,
+            planes_now,
+            finish_projection if k == slices - 1 else add,
+        )
     left = lax.broadcasted_iota(jnp.int32, (1, LANES), 1) < NP
-    width = 512
-    for c0 in range(0, NP * NP, width):
-        res = mm(x_table, stack(planes_all[:, c0:c0 + width]))
-        for j in range(width // LANES):
-            v = res[:, j * LANES:(j + 1) * LANES]
-            turned = pltpu.roll(v, NP, 1)
-            y = 2 * (c0 // LANES + j)
-            vt[pl.ds(y, NP, stride=NP), :] = jnp.where(left, v, turned)
-            vt[pl.ds(y + 1, NP, stride=NP), :] = jnp.where(left, turned, v)
 
     low_edge = jnp.full((1, LANES), lower[0], F32)
     high_edge = jnp.full((1, LANES), upper[0], F32)
@@ -236,18 +283,23 @@
     square = signed[0] * signed[0] + signed[1] * signed[1]
 
     z_ana = tables[ROW_Z_ANA:ROW_Z_ANA + 2 * LANES, :2 * LANES]
-    ya = tables[ROW_Y_ANA:ROW_Y_ANA + KEEP, :3 * NP]
-    xa = tables[ROW_X_ANA:ROW_X_ANA + KEEP, :3 * NP]
-
-    def weigh(x, value):
-        local = vt[x * NP:(x + 1) * NP, :]
-        res = mm(ya, stack(value * jnp.concatenate([local, local], axis=1)))
-        for h in range(2):
-            y2[h, x * KEEP:(x + 1) * KEEP, :] = res[:, h * LANES:(h + 1) * LANES]
+    ya = tables[ROW_ANA:ROW_ANA + 2 * KEEP, :2 * NP]
+    xa = tables[ROW_ANA:ROW_ANA + 2 * KEEP, 2 * NP:4 * NP]
+
+    def weigh(x, values):
+        parts = []
+        for i, value in enumerate(values):
+            local = vx[pl.ds(x + i, NP // 2, stride=NP), :]
+            turned = pltpu.roll(local, NP, 1)
+            local = jnp.concatenate([jnp.where(left, local, turned), jnp.where(left, turned, local)], axis=0)
+            parts.append(value * jnp.concatenate([local, local], axis=1))
+        for i, res in enumerate(times_summed(ya, parts)):
+            put_wide(y2, (x + i) * KEEP, res)
 
     def finish(u, scale, back):
-        for ky in range(KEEP):
-            put(z_first, ky * KEEP, mm(xa, stack(wide(y2, ky, NP, KEEP))))
+        for ky in range(0, KEEP, GROUP):
+            res = times_summed(xa, [wide(y2, ky + i, NP, KEEP) for i in range(GROUP)])
+            put(z_first, ky * KEEP, jnp.concatenate(res, axis=0))
         group = 8
         for ky in range(0, KEEP, group):
             high, low = split(z_first[ky * KEEP:(ky + group) * KEEP, :])
@@ -259,8 +311,8 @@
                 out = scale * (kinetic * now + res[i * KEEP:(i + 1) * KEEP, :] - center * now)
                 u_all[ky + i] = out - c_all[ky + i] if back else out
 
-    for x in range(NP):
-        weigh(x, field[x * NP:(x + 1) * NP, :])
+    for x in range(0, NP, GROUP):
+        weigh(x, [field[(x + i) * NP:(x + i + 1) * NP, :] for i in range(GROUP)])
     finish(c_all, 1.0 / half_width, False)
     synthesize(u_all, tables, z_first, x1, weigh)
     finish(u_all, 2.0 / half_width, True)
@@ -283,53 +335,50 @@
             spread[dest, b * run:(b + 1) * run, :] = packed[b, start:start + run, :]
 
 
-def select_kernel(owners, came, out):
-    steps = owners.shape[0]
-    run = out.shape[1] // LANES
-    block = out.shape[0] // steps
+def select_kernel(owners, came, *outs):
+    steps = owners.shape[1]
+    run = outs[0].shape[1] // LANES
+    each = steps // len(outs)
+    block = outs[0].shape[0] // each
     for s in range(steps):
+        out, row = outs[s // each], s % each * block
         for r in range(run):
-            start = owners[s] * (block * run) + r
-            out[s * block:(s + 1) * block, r * LANES:(r + 1) * LANES] = came[pl.ds(start, block, stride=run), :]
-
-
-def rotate_kernel(moves, chips, table, *refs):
-    count = sum(parts for _, _, parts in moves)
-    blocks = list(refs[:count])
-    out, arrived, results, in_sems, out_sems = refs[-5:]
+            start = owners[0, s] * (block * run) + r
+            out[row:row + block, r * LANES:(r + 1) * LANES] = came[pl.ds(start, block, stride=run), :]
+
+
+def rotate_kernel(moves, chips, continued, keep, table, *refs):
+    refs = list(refs)
+    results, sems = refs[-2:]
+    together = None
+    pieces = []
+    for _, _, parts in moves:
+        if parts < 0:
+            together = refs.pop(0) if together is None else together
+            pieces.append([together.at[-1 - parts]])
+        else:
+            pieces.append([refs.pop(0) for _ in range(parts)])
+    if continued:
+        refs.pop(0)
+    out, kept = refs[0], refs[1] if keep else None
     band = lax.axis_index("band")
     chip, core = band // 2, lax.rem(band, 2)
     position = jnp.where(lax.rem(chip, 2) == 0, chip // 2, chips - 1 - chip // 2)
     slots, _, width = results.shape
-    loads = []
-    for j, (_, _, parts) in enumerate(moves):
-        row, now = 0, []
-        for _ in range(parts):
-            block = blocks.pop(0)
-            size = block.shape[0]
-            now.append(
-                pltpu.make_async_copy(block, arrived.at[j, pl.ds(row, size)], in_sems.at[len(now) * len(moves) + j])
-            )
-            row += size
-        loads.append(now)
-    for now in loads:
-        for load in now:
-            load.start()
     left = table[...]
     stores = []
-    for j, (offset, flip, _) in enumerate(moves):
-        for load in loads[j]:
-            load.wait()
-        res = mm(left, stack(arrived[j]))
+    for j, ((offset, flip, _), parts) in enumerate(zip(moves, pieces)):
+        block = jnp.concatenate([part[...] for part in parts], axis=0)
+        if j < keep:
+            kept[j] = block
+        res = mm(left, stack(block))
         if j >= slots:
             stores[j - slots].wait()
         results[j % slots] = res
         place = lax.rem(position + (chips + offset), chips)
         owner = jnp.where(place < chips // 2, 2 * place, 2 * (chips - 1 - place) + 1)
         start = pl.multiple_of((2 * owner + (core if flip == 0 else 1 - core)) * width, width)
-        store = pltpu.make_async_copy(
-            results.at[j % slots], out.at[:, pl.ds(start, width)], out_sems.at[j % slots]
-        )
+        store = pltpu.make_async_copy(results.at[j % slots], out.at[:, pl.ds(start, width)], sems.at[j % slots])
         store.start()
         stores.append(store)
     for store in stores[-slots:]:
@@ -393,42 +442,49 @@
         name="project",
     )(potential, project_tables, packed[0])
     projected, coeffs = lax.optimization_barrier((projected, coeffs))
+    own_pieces = [projected, other_core(projected)] if ways > 1 else [projected]
+
     eye = np.eye(QUAD)
     z_high, z_low = halves(np.kron(eye, TABLE.T))
     back_high, back_low = halves(np.kron(eye, TABLE))
-    slots = np.zeros((NP, NG // planes, slot))
-    slots[:, :, :planes] = PROJECT.reshape(NP, NG // planes, planes)
+    slots = np.zeros((NP, slices, ways, slot))
+    slots[..., :planes] = PROJECT.reshape(NP, slices, ways, planes)
     tables = sheet(
-        (ROW_END, 3 * LANES),
+        (ROW_PROJECT + slices * NP, 2 * LANES),
         (ROW_SYN, 0, left_table(TABLE[:, KX_ORDER])),
-        (ROW_SYN, LANES, left_table(TABLE)),
-        (ROW_PROJECT, 0, left_table(slots.reshape(NP, -1))),
-        (ROW_Y_ANA, 0, left_table(TABLE.T)),
-        (ROW_X_ANA, 0, left_table(TABLE[:, KX_ORDER].T)),
+        (ROW_SYN, LANES, left_table(TABLE[Y_ORDER])),
+        (ROW_ANA, 0, summed_table(TABLE[Y_ORDER].T)),
+        (ROW_ANA, 2 * NP, summed_table(TABLE[:, KX_ORDER].T)),
         (ROW_Z_SYN, 0, np.concatenate([z_high, z_low, z_high], axis=0)),
         (ROW_Z_ANA, 0, np.concatenate([back_high, back_low], axis=1)),
+        *[(ROW_PROJECT + k * NP, 0, left_table(slots[:, k].reshape(NP, -1))) for k in range(slices)],
     )
     cube = jax.ShapeDtypeStruct((KEEP, KEEP, LANES), F32)
-    c_all, field = pl.pallas_call(
-        functools.partial(synthesis_kernel, slices),
-        out_shape=[cube, jax.ShapeDtypeStruct((NP * NP, 2 * LANES), F32)],
-        in_specs=in_vmem(slices + 1),
-        out_specs=in_vmem(2),
+    c_all, field, tables, projection, owners = pl.pallas_call(
+        functools.partial(synthesis_kernel, slices, ways),
+        out_shape=[
+            cube,
+            jax.ShapeDtypeStruct((NP * NP, 2 * LANES), F32),
+            jax.ShapeDtypeStruct(tables.shape, tables.dtype),
+            jax.ShapeDtypeStruct((NP, NP * NP), F32),
+            jax.ShapeDtypeStruct((1, steps), jnp.int32),
+        ],
+        in_specs=in_vmem(slices + ways + 2),
+        out_specs=in_vmem(5),
         scratch_shapes=[
             pltpu.VMEM((KEEP * KEEP, 2 * LANES), F32),
             pltpu.VMEM((2, KEEP * NP, LANES), F32),
+            pltpu.VMEM((ways * slot, NP * NP), F32),
         ],
-        compiler_params=params(16),
+        compiler_params=params(20),
         cost_estimate=pl.CostEstimate(flops=1, bytes_accessed=1, transcendentals=0),
         name="synthesis",
-    )(*coeffs, tables)
+    )(*coeffs, *own_pieces, tables, owners.reshape(1, steps))
 
     pieces = []
-    for k in range(slices):
+    for k in range(1, slices):
         if ways == 1:
-            pieces.append(projected if k == 0 else shift(projected, k))
-        elif k == 0:
-            pieces += [projected, other_core(projected)]
+            pieces.append(shift(projected, k))
         else:
             came, c_all, field = lax.optimization_barrier((shift_diagonal(projected, k), c_all, field))
             pieces += [other_core(came), came]
@@ -437,11 +493,12 @@
         functools.partial(filter_kernel, slices, ways),
         out_shape=[piece] * slices
         + [jax.ShapeDtypeStruct((groups * slices, each * rows // groups, LANES), F32)],
-        in_specs=in_vmem(2 + slices * ways) + [pl.BlockSpec(memory_space=pltpu.SMEM)] * 2 + in_vmem(1),
+        in_specs=in_vmem(3 + (slices - 1) * ways) + [pl.BlockSpec(memory_space=pltpu.SMEM)] * 2 + in_vmem(1),
         out_specs=in_vmem(slices + 1),
         scratch_shapes=[
-            pltpu.VMEM((NG // planes * slot, NP * NP), F32),
-            pltpu.VMEM((NP * NP, LANES), F32),
+            pltpu.VMEM((ways * slot, NP * NP), F32),
+            pltpu.VMEM((NP if slices > 2 else 8, NP * NP), F32),
+            pltpu.VMEM((NP * NP // 2, LANES), F32),
             pltpu.VMEM((KEEP, KEEP, LANES), F32),
             pltpu.VMEM((KEEP * KEEP, 2 * LANES), F32),
             pltpu.VMEM((2, KEEP * NP, LANES), F32),
@@ -450,7 +507,7 @@
         ],
         compiler_params=params(28),
         name="chebyshev",
-    )(c_all, field, *pieces, lower_edge, upper_edge, tables)
+    )(c_all, field, projection, *pieces, lower_edge, upper_edge, tables)
     arrived = [filtered_pieces[0]] + [shift(filtered_pieces[k], k) for k in range(1, slices)]
     filtered = pl.pallas_call(
         functools.partial(unpack_kernel, slices),
@@ -463,13 +520,18 @@
         name="unpack",
     )(*arrived)
 
+    flat = jnp.transpose(rotation, (1, 0, 2)).reshape(rotation.shape[1], steps * block)
+    high, low = split(flat)
+    table = jnp.concatenate([high, low, high], axis=1)
+
     came = lax.all_to_all(spread, ("band", "grid"), split_axis=0, concat_axis=0, tiled=True)
+    came, table = lax.optimization_barrier((came, table))
     width = cols // groups
     mine = pl.pallas_call(
         select_kernel,
-        out_shape=jax.ShapeDtypeStruct((steps * block, width), F32),
+        out_shape=[jax.ShapeDtypeStruct((steps * block // 2, width), F32)] * 2,
         in_specs=[pl.BlockSpec(memory_space=pltpu.SMEM), pl.BlockSpec(memory_space=pltpu.VMEM)],
-        out_specs=pl.BlockSpec(memory_space=pltpu.VMEM),
+        out_specs=in_vmem(2),
         compiler_params=params(8),
         name="select",
     )(owners, came.reshape(-1, LANES))
@@ -477,59 +539,62 @@
     chips = groups // 2
     ring = list(range(0, chips, 2)) + list(range(1, chips, 2))[::-1]
 
-    def pass_on(x, step):
+    def pass_on(x, step, cross=0):
         pairs = [
-            (2 * ring[p] + c, 2 * ring[(p + step) % chips] + c) for p in range(chips) for c in range(2)
+            (2 * ring[p] + c, 2 * ring[(p + step) % chips] + (c ^ cross)) for p in range(chips) for c in range(2)
         ]
         return lax.ppermute(x, "band", pairs)
 
-    flat = jnp.transpose(rotation, (1, 0, 2)).reshape(rotation.shape[1], steps * block)
-    high, low = split(flat)
-    table = jnp.concatenate([high, low, high], axis=1)
     rotated_shape = jax.ShapeDtypeStruct((rotation.shape[1], cols), F32)
 
-    def rotate(moves, before):
-        arrays = [x for _, _, parts in moves for x in parts]
-        plan = tuple((offset, flip, len(parts)) for offset, flip, parts in moves)
-        count = len(moves)
+    def rotate(moves, before, keep=0):
+        arrays, plan = [], []
+        for offset, flip, parts in moves:
+            if isinstance(parts, tuple):
+                arrays += parts[:1] if parts[1] == 0 else []
+                plan.append((offset, flip, -1 - parts[1]))
+            else:
+                arrays += parts
+                plan.append((offset, flip, len(parts)))
+        depth = min(3, len(moves))
+        kept = [jax.ShapeDtypeStruct((keep, steps * block, width), F32)] if keep else []
         return pl.pallas_call(
-            functools.partial(rotate_kernel, plan, chips),
-            out_shape=rotated_shape,
-            in_specs=[pl.BlockSpec(memory_space=pltpu.VMEM)]
-            + [pl.BlockSpec(memory_space=pl.ANY)] * (len(arrays) + len(before)),
-            out_specs=pl.BlockSpec(memory_space=pl.ANY),
+            functools.partial(rotate_kernel, tuple(plan), chips, bool(before), keep),
+            out_shape=[jax.ShapeDtypeStruct((rotation.shape[1], cols), F32)] + kept,
+            in_specs=in_vmem(1 + len(arrays)) + [pl.BlockSpec(memory_space=pl.ANY)] * len(before),
+            out_specs=[pl.BlockSpec(memory_space=pl.ANY)] + in_vmem(len(kept)),
             scratch_shapes=[
-                pltpu.VMEM((count, steps * block, width), F32),
-                pltpu.VMEM((min(3, count), rotation.shape[1], width), F32),
-                pltpu.SemaphoreType.DMA((2 * count,)),
-                pltpu.SemaphoreType.DMA((min(3, count),)),
+                pltpu.VMEM((depth, rotation.shape[1], width), F32),
+                pltpu.SemaphoreType.DMA((depth,)),
             ],
             input_output_aliases={len(arrays) + 1: 0} if before else {},
-            compiler_params=params(12),
-            cost_estimate=pl.CostEstimate(
-                flops=200_000_000 * count, bytes_accessed=1_500_000 * count, transcendentals=0
-            ),
+            compiler_params=params(16),
+            cost_estimate=pl.CostEstimate(flops=1_000_000_000, bytes_accessed=4_000_000, transcendentals=0),
             name="rotate",
         )(table, *arrays, *before)
 
     half = chips // 2
-    right = left = mine
-    ready, later = [(0, 0, [mine]), (0, 1, [other_core(mine)])], []
-    rotated = []
+    right, left = list(mine), list(mine)
+    own = [(0, 0, list(mine))]
     for k in range(1, half):
-        right, left = pass_on(right, 1), pass_on(left, -1)
+        right, left = [pass_on(x, 1) for x in right], [pass_on(x, -1) for x in left]
+        if k == half - 2:
+            filtered, left[1] = lax.optimization_barrier((filtered, left[1]))
         if k == half - 1:
-            filtered, right, left, early = lax.optimization_barrier((filtered, right, left, rotate(ready, rotated)))
-            ready, rotated = [], [early]
-        ready += [(-k, 0, [right]), (k, 0, [left])] + later
-        later = [(-k, 1, [other_core(right)]), (k, 1, [other_core(left)])]
-    last = [
-        pass_on(lax.slice_in_dim(right, 0, steps * block // 2, axis=0), 1),
-        pass_on(lax.slice_in_dim(left, steps * block // 2, steps * block, axis=0), -1),
-    ]
-    last, early = lax.optimization_barrier((last, rotate(ready, rotated)))
-    rotated = rotate([(half, 0, last)] + later, [early])
-    rotated = rotate([(half, 1, [other_core(x) for x in last])], [rotated])
+            early, kept = rotate(own, [], len(own))
+            right, left, early, kept = lax.optimization_barrier((right, left, early, kept))
+            together = other_core(kept)
+            ready = [(offset, 1, (together, i)) for i, (offset, _, _) in enumerate(own)]
+            own = []
+        own += [(-k, 0, right), (k, 0, left)]
+    last = [pass_on(right[0], 1), pass_on(left[1], -1)]
+    crossed = [pass_on(right[0], 1, 1), pass_on(left[1], -1, 1)]
+    early, kept = rotate(own + ready, [early], len(own))
+    last, crossed, early, kept = lax.optimization_barrier((last, crossed, early, kept))
+    together = other_core(kept)
+    later = [(offset, 1, (together, i)) for i, (offset, _, _) in enumerate(own)]
+    rotated, = rotate([(half, 0, last), (half, 1, crossed)], [early])
+    rotated, = rotate(later, [rotated])
     return (filtered, rotated)
 
 

time: 97.7 us -> 90.6 us (0.927)
  blocking collectives: 20.4 us -> 0 us
  starting transfers between devices: 16.4 us -> 29.6 us
  waiting for transfers between devices: 23.1 us -> 27.6 us
  Pallas kernels: 28.7 us -> 25.5 us
  local copies, waits for them, and re-layouts: 6.46 us -> 5.29 us
    all_to_all x1 -> x0, blocking collectives: 20.4 us -> none  [body(): lax.all_to_all(spread, ('band', 'grid'), split_axis=0, concat_axis=0, til...]
    all_to_all x0 -> x1, waiting for transfers between devices: none -> 12.8 us  [body(): lax.all_to_all(spread, ('band', 'grid'), split_axis=0, concat_axis=0, til...]
    ppermute x8 -> x16, starting transfers between devices: 7.84 us -> 16 us  [pass_on(): return lax.ppermute(x, 'band', pairs)]
    ppermute x8 -> x16, waiting for transfers between devices: 14.7 us -> 7.32 us  [pass_on(): return lax.ppermute(x, 'band', pairs)]
    all_to_all x0 -> x1, starting transfers between devices: none -> 5.97 us  [body(): lax.all_to_all(spread, ('band', 'grid'), split_axis=0, concat_axis=0, til...]
    ppermute x11 -> x4, starting transfers between devices: 3.43 us -> 0.88 us  [other_core(): return lax.ppermute(x, 'band', [(i, i ^ 1) for i in range(groups)])]
    pallas_call x1, Pallas kernels: 13.1 us -> 11 us  [body(): pl.pallas_call(functools.partial(filter_kernel, slices, ways), out_shape=...]
    ppermute x1, starting transfers between devices: 0.31 us -> 1.85 us  [shift_diagonal(): return lax.ppermute(x, ('band', 'grid'), pairs)]
  transfers between devices with their start and end apart: 22 -> 24, of which waited for: 10 -> 14; matrix products, arithmetic and copies ran while one was open for 0% -> 0% of each run, Pallas kernels for 13% -> 14%
where the time goes in v2:
time: 90.6 us; the launch traced here: 90.3 us
  starting transfers between devices  29.6 us (33%)
  waiting for transfers between devices  27.6 us (30%)
  Pallas kernels  25.5 us (28%)
  local copies, waits for them, and re-layouts  5.29 us (6%)
  between operations  2.24 us (2%)
    ppermute x16, starting transfers between devices, pass_on(): return lax.ppermute(x, 'band', pairs)  16 us
    all_to_all x1, waiting for transfers between devices, body(): lax.all_to_all(spread, ('band', 'grid'), split_axis=0, concat_axis=0, til...  12.8 us
    pallas_call x1, Pallas kernels, body(): pl.pallas_call(functools.partial(filter_kernel, slices, ways), out_shape=...  11 us
    pallas_call x4, Pallas kernels, rotate(): pl.pallas_call(functools.partial(rotate_kernel, tuple(plan), chips, bool(...  8.31 us
    ppermute x16, waiting for transfers between devices, pass_on(): return lax.ppermute(x, 'band', pairs)  7.32 us
    all_to_all x1, starting transfers between devices, body(): lax.all_to_all(spread, ('band', 'grid'), split_axis=0, concat_axis=0, til...  5.97 us
    unnamed x12, local copies, waits for them, and re-layouts  5.09 us
    ppermute x2, starting transfers between devices, shift(): lax.ppermute(x, 'grid', [(i, (i + k) % slices) for i in range(slices)])  4.84 us
  transfers between devices with their start and end apart: 24, of which 14 were waited for; matrix products, arithmetic and copies ran while one was open for 0% of the time, Pallas kernels for 14%

profile of v2, /device:TPU:0, one launch (start us, length us, event | category | flops | bytes accessed | tf_op | source)
XLA Modules:
  0.0 90.3 jit_solution(12022243959600796252)
XLA Ops:
  2.0 3.0 %collective-permute-start = (f32[4,128,128]{2,1,0:T(8,128)S(1)}, f32[4,128,128]{2,1,0:T(8,128)S(1)}, u32[]{:S(2)}, u32[]{:S(2)}) collective-permute-start(f32[4,128,128]{2,1,0:T(8,128)S(1)} %get-tuple-element.41), channel_id=1, source_target_pairs={{0,1},{1,0},{2,3},{3,2},{4,5},{5,4},{6,7},{7,6},{8,9},{9,8},{10,11... | collective-permute-start | bytes 786440 | tf_op jit(solution)/shard_map/ppermute | solution.py:408
  5.0 1.5 %copy-done = f32[48,9216]{1,0:T(8,128)S(1)} copy-done((f32[48,9216]{1,0:T(8,128)S(1)}, f32[48,9216]{1,0:T(8,128)}, u32[]{:S(2)}) %copy-start) | copy-done | bytes 1769496
  7.4 1.3 %project.1.refs_2_ = f32[24,4096]{1,0:T(8,128)S(1)} custom-call(f32[48,9216]{1,0:T(8,128)S(1)} %copy-done, bf16[160,384]{1,0:T(8,128)(2,1)S(1)} %copy-done.3, f32[4,128,128]{2,1,0:T(8,128)S(1)} %get-tuple-element.43.after.refs_0_), custom_call_target="tpu_custom_call" | custom-call | tf_op jit(solution)/shard_map/project/pallas_call | solution.py:435
  8.7 2.6 %collective-permute-done.refs_1_ = f32[4,128,128]{2,1,0:T(8,128)S(1)} collective-permute-done((f32[4,128,128]{2,1,0:T(8,128)S(1)}, f32[4,128,128]{2,1,0:T(8,128)S(1)}, u32[]{:S(2)}, u32[]{:S(2)}) %collective-permute-start) | collective-permute-done | bytes 262176 | tf_op jit(solution)/shard_map/ppermute | solution.py:408
  11.3 1.9 %collective-permute-start.1 = (f32[24,4096]{1,0:T(8,128)S(1)}, f32[24,4096]{1,0:T(8,128)S(1)}, u32[]{:S(2)}, u32[]{:S(2)}) collective-permute-start(f32[24,4096]{1,0:T(8,128)S(1)} %project.1.refs_2_), channel_id=1, source_target_pairs={{0,3},{1,2},{2,1},{3,0},{4,7},{5,6},{6,5},{7,4},{8,11},{9,10},{10,... | collective-permute-start | bytes 1179656 | tf_op jit(solution)/shard_map/ppermute | solution.py:414
  14.9 2.8 %synthesis.1 = (f32[32,32,128]{2,1,0:T(8,128)S(1)}, f32[4096,256]{1,0:T(8,128)S(1)}, bf16[896,256]{1,0:T(8,128)(2,1)S(1)}, f32[64,4096]{1,0:T(8,128)S(1)}, s32[1,8]{1,0:T(1,128)S(1)}) custom-call(f32[4,128,128]{2,1,0:T(8,128)S(1)} %get-tuple-element.43.after.refs_0_, f32[4,128,128]{2,1,0:T(8,128)S(1)} %collective-permute-done.refs_1_, ...), custom_call_target="tpu_custom_call" | custom-call | flops 1 | bytes 1 | tf_op jit(solution)/shard_map/synthesis/pallas_call | solution.py:463
  17.6 4.7 %collective-permute-done.1.refs_4_ = f32[24,4096]{1,0:T(8,128)S(1)} collective-permute-done((f32[24,4096]{1,0:T(8,128)S(1)}, f32[24,4096]{1,0:T(8,128)S(1)}, u32[]{:S(2)}, u32[]{:S(2)}) %collective-permute-start.1) | collective-permute-done | bytes 393248 | tf_op jit(solution)/shard_map/ppermute | solution.py:414
  24.0 11.0 %chebyshev.1 = (f32[4,128,128]{2,1,0:T(8,128)S(1)}, f32[4,128,128]{2,1,0:T(8,128)S(1)}, f32[32,32,128]{2,1,0:T(8,128)}) custom-call(f32[32,32,128]{2,1,0:T(8,128)S(1)} %get-tuple-element.47.refs_0_, f32[4096,256]{1,0:T(8,128)S(1)} %get-tuple-element.48.refs_1_, f32[64,4096]{1,0:T(8,128)S(1)} %get-tuple-element.49.refs_2_, ...), custom_call_target="tpu_custom_call" | custom-call | tf_op jit(solution)/shard_map/chebyshev/pallas_call | solution.py:492
  35.0 6.0 %all-to-all-start = ((f32[32,32,128]{2,1,0:T(8,128)}), f32[32,32,128]{2,1,0:T(8,128)S(1)}, u32[]{:S(2)}, u32[]{:S(2)}) async-start(f32[32,32,128]{2,1,0:T(8,128)} %get-tuple-element.55), calls=%async_computation | async-start | bytes 1048576 | tf_op jit(solution)/shard_map/all_to_all | solution.py:527
  41.4 1.8 %collective-permute-start.4 = (f32[4,128,128]{2,1,0:T(8,128)S(1)}, f32[4,128,128]{2,1,0:T(8,128)S(1)}, u32[]{:S(2)}, u32[]{:S(2)}) collective-permute-start(f32[4,128,128]{2,1,0:T(8,128)S(1)} %get-tuple-element.53), channel_id=1, source_target_pairs={{0,1},{1,0},{2,3},{3,2},{4,5},{5,4},{6,7},{7,6},{8,9},{9,8},{10,11... | collective-permute-start | bytes 786440 | tf_op jit(solution)/shard_map/ppermute | solution.py:408
  43.2 12.8 %all-to-all-done = f32[32,32,128]{2,1,0:T(8,128)S(1)} async-done(((f32[32,32,128]{2,1,0:T(8,128)}), f32[32,32,128]{2,1,0:T(8,128)S(1)}, u32[]{:S(2)}, u32[]{:S(2)}) %all-to-all-start) | async-done | bytes 524320 | tf_op jit(solution)/shard_map/all_to_all | solution.py:527
  56.6 1.5 %collective-permute-start.5 = (f32[32,1024]{1,0:T(8,128)S(1)}, f32[32,1024]{1,0:T(8,128)S(1)}, u32[]{:S(2)}, u32[]{:S(2)}) collective-permute-start(f32[32,1024]{1,0:T(8,128)S(1)} %get-tuple-element.57.refs_1_), channel_id=1, source_target_pairs={{0,4},{2,6},{8,0},{10,2},{16,8},{18,10},{24,16},{26,18},{28,24},{3... | collective-permute-start | bytes 393224 | tf_op jit(solution)/shard_map/ppermute | solution.py:546
  58.7 1.5 %collective-permute-start.13 = (f32[32,1024]{1,0:T(8,128)S(1)}, f32[32,1024]{1,0:T(8,128)S(1)}, u32[]{:S(2)}, u32[]{:S(2)}) collective-permute-start(f32[32,1024]{1,0:T(8,128)S(1)} %get-tuple-element.60.refs_0_), channel_id=1, source_target_pairs={{0,4},{2,6},{8,0},{10,2},{16,8},{18,10},{24,16},{26,18},{28,24},{3... | collective-permute-start | bytes 393224 | tf_op jit(solution)/shard_map/ppermute | solution.py:546
  60.7 2.2 %collective-permute-done.5.refs_5_ = f32[32,1024]{1,0:T(8,128)S(1)} collective-permute-done((f32[32,1024]{1,0:T(8,128)S(1)}, f32[32,1024]{1,0:T(8,128)S(1)}, u32[]{:S(2)}, u32[]{:S(2)}) %collective-permute-start.5) | collective-permute-done | bytes 131104 | tf_op jit(solution)/shard_map/ppermute | solution.py:546
  62.9 1.5 %collective-permute-start.6 = (f32[32,1024]{1,0:T(8,128)S(1)}, f32[32,1024]{1,0:T(8,128)S(1)}, u32[]{:S(2)}, u32[]{:S(2)}) collective-permute-start(f32[32,1024]{1,0:T(8,128)S(1)} %collective-permute-done.5.refs_5_), channel_id=1, source_target_pairs={{0,4},{2,6},{8,0},{10,2},{16,8},{18,10},{24,16},{26,18},{28,24},{3... | collective-permute-start | bytes 393224 | tf_op jit(solution)/shard_map/ppermute | solution.py:546
  65.7 1.5 %collective-permute-start.14 = (f32[32,1024]{1,0:T(8,128)S(1)}, f32[32,1024]{1,0:T(8,128)S(1)}, u32[]{:S(2)}, u32[]{:S(2)}) collective-permute-start(f32[32,1024]{1,0:T(8,128)S(1)} %collective-permute-done.13.refs_4_), channel_id=1, source_target_pairs={{0,4},{2,6},{8,0},{10,2},{16,8},{18,10},{24,16},{26,18},{28,24},{3... | collective-permute-start | bytes 393224 | tf_op jit(solution)/shard_map/ppermute | solution.py:546
  68.9 1.5 %collective-permute-start.16 = (f32[32,1024]{1,0:T(8,128)S(1)}, f32[32,1024]{1,0:T(8,128)S(1)}, u32[]{:S(2)}, u32[]{:S(2)}) collective-permute-start(f32[32,1024]{1,0:T(8,128)S(1)} %collective-permute-done.6.refs_9_), channel_id=1, source_target_pairs={{0,4},{2,6},{8,0},{10,2},{16,8},{18,10},{24,16},{26,18},{28,24},{3... | collective-permute-start | bytes 393224 | tf_op jit(solution)/shard_map/ppermute | solution.py:546
  71.7 1.5 %collective-permute-start.15 = (f32[32,1024]{1,0:T(8,128)S(1)}, f32[32,1024]{1,0:T(8,128)S(1)}, u32[]{:S(2)}, u32[]{:S(2)}) collective-permute-start(f32[32,1024]{1,0:T(8,128)S(1)} %collective-permute-done.14.refs_8_), channel_id=1, source_target_pairs={{0,4},{2,6},{8,0},{10,2},{16,8},{18,10},{24,16},{26,18},{28,24},{3... | collective-permute-start | bytes 393224 | tf_op jit(solution)/shard_map/ppermute | solution.py:546
  73.7 2.4 %rotate.4 = (f32[192,16384]{1,0:T(8,128)}, f32[5,64,1024]{2,1,0:T(8,128)S(1)}) custom-call(bf16[192,192]{1,0:T(8,128)(2,1)S(1)} %pad_maximum_fusion.table, f32[32,1024]{1,0:T(8,128)S(1)} %get-tuple-element.60.refs_0_, f32[32,1024]{1,0:T(8,128)S(1)} %get-tuple-element.57.refs_1_, f32[32,1024]{1,0:T(8,128)S(1)} %collective-permute-done.7.refs_2_, ...), custom_call_target="tpu_custom_call" | custom-call | flops 1000000000 | bytes 4000000 | tf_op jit(solution)/shard_map/rotate/pallas_call | solution.py:561
  78.9 1.2 %collective-permute-start.18 = (f32[32,1024]{1,0:T(8,128)S(1)}, f32[32,1024]{1,0:T(8,128)S(1)}, u32[]{:S(2)}, u32[]{:S(2)}) collective-permute-start(f32[32,1024]{1,0:T(8,128)S(1)} %collective-permute-done.16.refs_3_), channel_id=1, source_target_pairs={{0,4},{2,6},{8,0},{10,2},{16,8},{18,10},{24,16},{26,18},{28,24},{3... | collective-permute-start | bytes 393224 | tf_op jit(solution)/shard_map/ppermute | solution.py:546
  80.5 1.4 %collective-permute-start.20 = (f32[32,1024]{1,0:T(8,128)S(1)}, f32[32,1024]{1,0:T(8,128)S(1)}, u32[]{:S(2)}, u32[]{:S(2)}) collective-permute-start(f32[32,1024]{1,0:T(8,128)S(1)} %collective-permute-done.16.refs_3_), channel_id=1, source_target_pairs={{0,6},{2,4},{8,2},{10,0},{16,10},{18,8},{24,18},{26,16},{28,26},{3... | collective-permute-start | bytes 393224 | tf_op jit(solution)/shard_map/ppermute | solution.py:546
  81.9 3.0 %rotate.5 = (f32[192,16384]{1,0:T(8,128)}, f32[2,64,1024]{2,1,0:T(8,128)S(1)}) custom-call(bf16[192,192]{1,0:T(8,128)(2,1)S(1)} %pad_maximum_fusion.table, f32[32,1024]{1,0:T(8,128)S(1)} %collective-permute-done.9.refs_0_, f32[32,1024]{1,0:T(8,128)S(1)} %collective-permute-done.12.refs_1_, ...), custom_call_target="tpu_custom_call", output_to_operand_aliasing={{0}: (6, {})} | custom-call | flops 1000000000 | bytes 4000000 | tf_op jit(solution)/shard_map/rotate/pallas_call | solution.py:561
  87.2 1.4 %rotate.6.refs_1_ = f32[192,16384]{1,0:T(8,128)} custom-call(bf16[192,192]{1,0:T(8,128)(2,1)S(1)} %pad_maximum_fusion.table, f32[32,1024]{1,0:T(8,128)S(1)} %collective-permute-done.17.refs_0_, f32[32,1024]{1,0:T(8,128)S(1)} %collective-permute-done.18.refs_1_, f32[32,1024]{1,0:T(8,128)S(1)} %collective-permute-done.19.refs_2_, ...), custom_call_target="tpu_custom_call", output_to_operand_aliasing={{}: (5, {})} | custom-call | flops 1000000000 | bytes 4000000 | tf_op jit(solution)/shard_map/rotate/pallas_call | solution.py:561
  88.7 1.4 %rotate.7 = f32[192,16384]{1,0:T(8,128)} custom-call(bf16[192,192]{1,0:T(8,128)(2,1)S(1)} %pad_maximum_fusion.table, f32[2,64,1024]{2,1,0:T(8,128)S(1)} %collective-permute-done.22.refs_0_, f32[192,16384]{1,0:T(8,128)} %rotate.6.refs_1_), custom_call_target="tpu_custom_call", output_to_operand_aliasing={{}: (2, {})} | custom-call | flops 1000000000 | bytes 4000000 | tf_op jit(solution)/shard_map/rotate/pallas_call | solution.py:561
  (51 shorter events, 16.7 us)
Async XLA Ops:
  2.0 9.3 %collective-permute-start = (f32[4,128,128]{2,1,0:T(8,128)S(1)}, f32[4,128,128]{2,1,0:T(8,128)S(1)}, u32[]{:S(2)}, u32[]{:S(2)}) collective-permute-start(f32[4,128,128]{2,1,0:T(8,128)S(1)} %get-tuple-element.41), channel_id=1, source_target_pairs={{0,1},{1,0},{2,3},{3,2},{4,5},{5,4},{6,7},{7,6},{8,9},{9,8},{10,11... | collective-permute-start | bytes 786440 | tf_op jit(solution)/shard_map/ppermute | solution.py:408
  11.3 1.9 %collective-permute-start.2 = (f32[24,4096]{1,0:T(8,128)S(1)}, f32[24,4096]{1,0:T(8,128)S(1)}, u32[]{:S(2)}, u32[]{:S(2)}) collective-permute-start(f32[24,4096]{1,0:T(8,128)S(1)} %project.1.refs_2_), channel_id=1, source_target_pairs={{0,2},{2,0},{4,6},{6,4},{8,10},{10,8},{12,14},{14,12},{16,18},{18,... | collective-permute-start | bytes 1179656 | tf_op jit(solution)/shard_map/ppermute | solution.py:417
  11.3 11.0 %collective-permute-start.1 = (f32[24,4096]{1,0:T(8,128)S(1)}, f32[24,4096]{1,0:T(8,128)S(1)}, u32[]{:S(2)}, u32[]{:S(2)}) collective-permute-start(f32[24,4096]{1,0:T(8,128)S(1)} %project.1.refs_2_), channel_id=1, source_target_pairs={{0,3},{1,2},{2,1},{3,0},{4,7},{5,6},{6,5},{7,4},{8,11},{9,10},{10,... | collective-permute-start | bytes 1179656 | tf_op jit(solution)/shard_map/ppermute | solution.py:414
  22.3 1.7 %collective-permute-start.3 = (f32[24,4096]{1,0:T(8,128)S(1)}, f32[24,4096]{1,0:T(8,128)S(1)}, u32[]{:S(2)}, u32[]{:S(2)}) collective-permute-start(f32[24,4096]{1,0:T(8,128)S(1)} %collective-permute-done.1.refs_4_), channel_id=1, source_target_pairs={{0,2},{2,0},{4,6},{6,4},{8,10},{10,8},{12,14},{14,12},{16,18},{18,... | collective-permute-start | bytes 1179656 | tf_op jit(solution)/shard_map/ppermute | solution.py:417
  35.0 21.0 %all-to-all-start = ((f32[32,32,128]{2,1,0:T(8,128)}), f32[32,32,128]{2,1,0:T(8,128)S(1)}, u32[]{:S(2)}, u32[]{:S(2)}) async-start(f32[32,32,128]{2,1,0:T(8,128)} %get-tuple-element.55), calls=%async_computation | async-start | bytes 1048576 | tf_op jit(solution)/shard_map/all_to_all | solution.py:527
  41.4 26.4 %collective-permute-start.4 = (f32[4,128,128]{2,1,0:T(8,128)S(1)}, f32[4,128,128]{2,1,0:T(8,128)S(1)}, u32[]{:S(2)}, u32[]{:S(2)}) collective-permute-start(f32[4,128,128]{2,1,0:T(8,128)S(1)} %get-tuple-element.53), channel_id=1, source_target_pairs={{0,1},{1,0},{2,3},{3,2},{4,5},{5,4},{6,7},{7,6},{8,9},{9,8},{10,11... | collective-permute-start | bytes 786440 | tf_op jit(solution)/shard_map/ppermute | solution.py:408
  56.6 6.3 %collective-permute-start.5 = (f32[32,1024]{1,0:T(8,128)S(1)}, f32[32,1024]{1,0:T(8,128)S(1)}, u32[]{:S(2)}, u32[]{:S(2)}) collective-permute-start(f32[32,1024]{1,0:T(8,128)S(1)} %get-tuple-element.57.refs_1_), channel_id=1, source_target_pairs={{0,4},{2,6},{8,0},{10,2},{16,8},{18,10},{24,16},{26,18},{28,24},{3... | collective-permute-start | bytes 393224 | tf_op jit(solution)/shard_map/ppermute | solution.py:546
  58.1 6.3 %collective-permute-start.10 = (f32[32,1024]{1,0:T(8,128)S(1)}, f32[32,1024]{1,0:T(8,128)S(1)}, u32[]{:S(2)}, u32[]{:S(2)}) collective-permute-start(f32[32,1024]{1,0:T(8,128)S(1)} %get-tuple-element.57.refs_1_), channel_id=1, source_target_pairs={{0,8},{2,10},{8,16},{10,18},{16,24},{18,26},{24,28},{26,30},{28,20... | collective-permute-start | bytes 393224 | tf_op jit(solution)/shard_map/ppermute | solution.py:546
  58.7 7.1 %collective-permute-start.13 = (f32[32,1024]{1,0:T(8,128)S(1)}, f32[32,1024]{1,0:T(8,128)S(1)}, u32[]{:S(2)}, u32[]{:S(2)}) collective-permute-start(f32[32,1024]{1,0:T(8,128)S(1)} %get-tuple-element.60.refs_0_), channel_id=1, source_target_pairs={{0,4},{2,6},{8,0},{10,2},{16,8},{18,10},{24,16},{26,18},{28,24},{3... | collective-permute-start | bytes 393224 | tf_op jit(solution)/shard_map/ppermute | solution.py:546
  60.2 7.1 %collective-permute-start.7 = (f32[32,1024]{1,0:T(8,128)S(1)}, f32[32,1024]{1,0:T(8,128)S(1)}, u32[]{:S(2)}, u32[]{:S(2)}) collective-permute-start(f32[32,1024]{1,0:T(8,128)S(1)} %get-tuple-element.60.refs_0_), channel_id=1, source_target_pairs={{0,8},{2,10},{8,16},{10,18},{16,24},{18,26},{24,28},{26,30},{28,20... | collective-permute-start | bytes 393224 | tf_op jit(solution)/shard_map/ppermute | solution.py:546
  62.9 6.0 %collective-permute-start.6 = (f32[32,1024]{1,0:T(8,128)S(1)}, f32[32,1024]{1,0:T(8,128)S(1)}, u32[]{:S(2)}, u32[]{:S(2)}) collective-permute-start(f32[32,1024]{1,0:T(8,128)S(1)} %collective-permute-done.5.refs_5_), channel_id=1, source_target_pairs={{0,4},{2,6},{8,0},{10,2},{16,8},{18,10},{24,16},{26,18},{28,24},{3... | collective-permute-start | bytes 393224 | tf_op jit(solution)/shard_map/ppermute | solution.py:546
  64.5 6.0 %collective-permute-start.11 = (f32[32,1024]{1,0:T(8,128)S(1)}, f32[32,1024]{1,0:T(8,128)S(1)}, u32[]{:S(2)}, u32[]{:S(2)}) collective-permute-start(f32[32,1024]{1,0:T(8,128)S(1)} %collective-permute-done.10.refs_3_), channel_id=1, source_target_pairs={{0,8},{2,10},{8,16},{10,18},{16,24},{18,26},{24,28},{26,30},{28,20... | collective-permute-start | bytes 393224 | tf_op jit(solution)/shard_map/ppermute | solution.py:546
  65.7 5.9 %collective-permute-start.14 = (f32[32,1024]{1,0:T(8,128)S(1)}, f32[32,1024]{1,0:T(8,128)S(1)}, u32[]{:S(2)}, u32[]{:S(2)}) collective-permute-start(f32[32,1024]{1,0:T(8,128)S(1)} %collective-permute-done.13.refs_4_), channel_id=1, source_target_pairs={{0,4},{2,6},{8,0},{10,2},{16,8},{18,10},{24,16},{26,18},{28,24},{3... | collective-permute-start | bytes 393224 | tf_op jit(solution)/shard_map/ppermute | solution.py:546
  67.2 5.9 %collective-permute-start.8 = (f32[32,1024]{1,0:T(8,128)S(1)}, f32[32,1024]{1,0:T(8,128)S(1)}, u32[]{:S(2)}, u32[]{:S(2)}) collective-permute-start(f32[32,1024]{1,0:T(8,128)S(1)} %collective-permute-done.7.refs_2_), channel_id=1, source_target_pairs={{0,8},{2,10},{8,16},{10,18},{16,24},{18,26},{24,28},{26,30},{28,20... | collective-permute-start | bytes 393224 | tf_op jit(solution)/shard_map/ppermute | solution.py:546
  68.9 7.2 %collective-permute-start.16 = (f32[32,1024]{1,0:T(8,128)S(1)}, f32[32,1024]{1,0:T(8,128)S(1)}, u32[]{:S(2)}, u32[]{:S(2)}) collective-permute-start(f32[32,1024]{1,0:T(8,128)S(1)} %collective-permute-done.6.refs_9_), channel_id=1, source_target_pairs={{0,4},{2,6},{8,0},{10,2},{16,8},{18,10},{24,16},{26,18},{28,24},{3... | collective-permute-start | bytes 393224 | tf_op jit(solution)/shard_map/ppermute | solution.py:546
  70.4 6.1 %collective-permute-start.12 = (f32[32,1024]{1,0:T(8,128)S(1)}, f32[32,1024]{1,0:T(8,128)S(1)}, u32[]{:S(2)}, u32[]{:S(2)}) collective-permute-start(f32[32,1024]{1,0:T(8,128)S(1)} %collective-permute-done.11.refs_7_), channel_id=1, source_target_pairs={{0,8},{2,10},{8,16},{10,18},{16,24},{18,26},{24,28},{26,30},{28,20... | collective-permute-start | bytes 393224 | tf_op jit(solution)/shard_map/ppermute | solution.py:546
  71.7 5.4 %collective-permute-start.15 = (f32[32,1024]{1,0:T(8,128)S(1)}, f32[32,1024]{1,0:T(8,128)S(1)}, u32[]{:S(2)}, u32[]{:S(2)}) collective-permute-start(f32[32,1024]{1,0:T(8,128)S(1)} %collective-permute-done.14.refs_8_), channel_id=1, source_target_pairs={{0,4},{2,6},{8,0},{10,2},{16,8},{18,10},{24,16},{26,18},{28,24},{3... | collective-permute-start | bytes 393224 | tf_op jit(solution)/shard_map/ppermute | solution.py:546
  73.1 5.0 %collective-permute-start.9 = (f32[32,1024]{1,0:T(8,128)S(1)}, f32[32,1024]{1,0:T(8,128)S(1)}, u32[]{:S(2)}, u32[]{:S(2)}) collective-permute-start(f32[32,1024]{1,0:T(8,128)S(1)} %collective-permute-done.8.refs_6_), channel_id=1, source_target_pairs={{0,8},{2,10},{8,16},{10,18},{16,24},{18,26},{24,28},{26,30},{28,20... | collective-permute-start | bytes 393224 | tf_op jit(solution)/shard_map/ppermute | solution.py:546
  78.1 3.8 %collective-permute-start.21 = (f32[5,64,1024]{2,1,0:T(8,128)S(1)}, f32[5,64,1024]{2,1,0:T(8,128)S(1)}, u32[]{:S(2)}, u32[]{:S(2)}) collective-permute-start(f32[5,64,1024]{2,1,0:T(8,128)S(1)} %get-tuple-element.68), channel_id=1, source_target_pairs={{0,2},{2,0},{4,6},{6,4},{8,10},{10,8},{12,14},{14,12},{16,18},{18,... | collective-permute-start | bytes 3932168 | tf_op jit(solution)/shard_map/ppermute | solution.py:417
  78.1 6.8 %collective-permute-start.17 = (f32[32,1024]{1,0:T(8,128)S(1)}, f32[32,1024]{1,0:T(8,128)S(1)}, u32[]{:S(2)}, u32[]{:S(2)}) collective-permute-start(f32[32,1024]{1,0:T(8,128)S(1)} %collective-permute-done.9.refs_0_), channel_id=1, source_target_pairs={{0,8},{2,10},{8,16},{10,18},{16,24},{18,26},{24,28},{26,30},{28,20... | collective-permute-start | bytes 393224 | tf_op jit(solution)/shard_map/ppermute | solution.py:546
  78.9 6.3 %collective-permute-start.18 = (f32[32,1024]{1,0:T(8,128)S(1)}, f32[32,1024]{1,0:T(8,128)S(1)}, u32[]{:S(2)}, u32[]{:S(2)}) collective-permute-start(f32[32,1024]{1,0:T(8,128)S(1)} %collective-permute-done.16.refs_3_), channel_id=1, source_target_pairs={{0,4},{2,6},{8,0},{10,2},{16,8},{18,10},{24,16},{26,18},{28,24},{3... | collective-permute-start | bytes 393224 | tf_op jit(solution)/shard_map/ppermute | solution.py:546
  80.1 6.3 %collective-permute-start.19 = (f32[32,1024]{1,0:T(8,128)S(1)}, f32[32,1024]{1,0:T(8,128)S(1)}, u32[]{:S(2)}, u32[]{:S(2)}) collective-permute-start(f32[32,1024]{1,0:T(8,128)S(1)} %collective-permute-done.9.refs_0_), channel_id=1, source_target_pairs={{0,10},{2,8},{8,18},{10,16},{16,26},{18,24},{24,30},{26,28},{28,22... | collective-permute-start | bytes 393224 | tf_op jit(solution)/shard_map/ppermute | solution.py:546
  80.5 6.2 %collective-permute-start.20 = (f32[32,1024]{1,0:T(8,128)S(1)}, f32[32,1024]{1,0:T(8,128)S(1)}, u32[]{:S(2)}, u32[]{:S(2)}) collective-permute-start(f32[32,1024]{1,0:T(8,128)S(1)} %collective-permute-done.16.refs_3_), channel_id=1, source_target_pairs={{0,6},{2,4},{8,2},{10,0},{16,10},{18,8},{24,18},{26,16},{28,26},{3... | collective-permute-start | bytes 393224 | tf_op jit(solution)/shard_map/ppermute | solution.py:546
  86.7 2.1 %collective-permute-start.22 = (f32[2,64,1024]{2,1,0:T(8,128)S(1)}, f32[2,64,1024]{2,1,0:T(8,128)S(1)}, u32[]{:S(2)}, u32[]{:S(2)}) collective-permute-start(f32[2,64,1024]{2,1,0:T(8,128)S(1)} %get-tuple-element.72), channel_id=1, source_target_pairs={{0,2},{2,0},{4,6},{6,4},{8,10},{10,8},{12,14},{14,12},{16,18},{18,... | collective-permute-start | bytes 1572872 | tf_op jit(solution)/shard_map/ppermute | solution.py:417
  (6 other events, 44.4 us)

commit v3 on v2

--- a/solution.py
+++ b/solution.py
@@ -16,7 +16,7 @@
 LOW = 4
 LANES = LOW * KEEP
 QUAD = 4
-GROUP = 4
+GROUP = 16
 MIB = 1024 * 1024
 
 F32 = jnp.float32
@@ -521,8 +521,8 @@
     )(*arrived)
 
     flat = jnp.transpose(rotation, (1, 0, 2)).reshape(rotation.shape[1], steps * block)
-    high, low = split(flat)
-    table = jnp.concatenate([high, low, high], axis=1)
+    high = lax.reduce_precision(flat, exponent_bits=8, mantissa_bits=7)
+    table = jnp.concatenate([high, flat - high, high], axis=1).astype(BF16)
 
     came = lax.all_to_all(spread, ("band", "grid"), split_axis=0, concat_axis=0, tiled=True)
     came, table = lax.optimization_barrier((came, table))
@@ -539,9 +539,9 @@
     chips = groups // 2
     ring = list(range(0, chips, 2)) + list(range(1, chips, 2))[::-1]
 
-    def pass_on(x, step, cross=0):
+    def pass_on(x, step):
         pairs = [
-            (2 * ring[p] + c, 2 * ring[(p + step) % chips] + (c ^ cross)) for p in range(chips) for c in range(2)
+            (2 * ring[p] + c, 2 * ring[(p + step) % chips] + c) for p in range(chips) for c in range(2)
         ]
         return lax.ppermute(x, "band", pairs)
 
@@ -588,13 +588,12 @@
             own = []
         own += [(-k, 0, right), (k, 0, left)]
     last = [pass_on(right[0], 1), pass_on(left[1], -1)]
-    crossed = [pass_on(right[0], 1, 1), pass_on(left[1], -1, 1)]
     early, kept = rotate(own + ready, [early], len(own))
-    last, crossed, early, kept = lax.optimization_barrier((last, crossed, early, kept))
+    last, early, kept = lax.optimization_barrier((last, early, kept))
     together = other_core(kept)
     later = [(offset, 1, (together, i)) for i, (offset, _, _) in enumerate(own)]
-    rotated, = rotate([(half, 0, last), (half, 1, crossed)], [early])
-    rotated, = rotate(later, [rotated])
+    rotated, = rotate([(half, 0, last)], [early])
+    rotated, = rotate(later + [(half, 1, [other_core(x) for x in last])], [rotated])
     return (filtered, rotated)
 
 

time: 90.6 us -> 87.9 us (0.970)
  starting transfers between devices: 29.6 us -> 27.8 us
  Pallas kernels: 25.5 us -> 24.3 us
    ppermute x16 -> x14, starting transfers between devices: 16 us -> 14.3 us  [pass_on(): return lax.ppermute(x, 'band', pairs)]
    ppermute x4 -> x6, waiting for transfers between devices: 0.2 us -> 1.71 us  [other_core(): return lax.ppermute(x, 'band', [(i, i ^ 1) for i in range(groups)])]
    ppermute x16 -> x14, waiting for transfers between devices: 7.32 us -> 5.96 us  [pass_on(): return lax.ppermute(x, 'band', pairs)]
    pallas_call x1, Pallas kernels: 11 us -> 9.83 us  [body(): pl.pallas_call(functools.partial(filter_kernel, slices, ways), out_shape=...]
where the time goes in v3:
time: 87.9 us; the launch traced here: 87.5 us
  starting transfers between devices  27.8 us (32%)
  waiting for transfers between devices  27.7 us (32%)
  Pallas kernels  24.3 us (28%)
  local copies, waits for them, and re-layouts  5.27 us (6%)
  between operations  2.24 us (3%)
    ppermute x14, starting transfers between devices, pass_on(): return lax.ppermute(x, 'band', pairs)  14.3 us
    all_to_all x1, waiting for transfers between devices, body(): lax.all_to_all(spread, ('band', 'grid'), split_axis=0, concat_axis=0, til...  12.8 us
    pallas_call x1, Pallas kernels, body(): pl.pallas_call(functools.partial(filter_kernel, slices, ways), out_shape=...  9.83 us
    pallas_call x4, Pallas kernels, rotate(): pl.pallas_call(functools.partial(rotate_kernel, tuple(plan), chips, bool(...  8.31 us
    all_to_all x1, starting transfers between devices, body(): lax.all_to_all(spread, ('band', 'grid'), split_axis=0, concat_axis=0, til...  5.97 us
    ppermute x14, waiting for transfers between devices, pass_on(): return lax.ppermute(x, 'band', pairs)  5.96 us
    unnamed x12, local copies, waits for them, and re-layouts  5.09 us
    ppermute x2, starting transfers between devices, shift(): lax.ppermute(x, 'grid', [(i, (i + k) % slices) for i in range(slices)])  4.84 us
  transfers between devices with their start and end apart: 24, of which 14 were waited for; matrix products, arithmetic and copies ran while one was open for 0% of the time, Pallas kernels for 14%

profile of v3, /device:TPU:0, one launch (start us, length us, event | category | flops | bytes accessed | tf_op | source)
XLA Modules:
  0.0 87.5 jit_solution(14922357743586069803)
XLA Ops:
  2.0 3.0 %collective-permute-start = (f32[4,128,128]{2,1,0:T(8,128)S(1)}, f32[4,128,128]{2,1,0:T(8,128)S(1)}, u32[]{:S(2)}, u32[]{:S(2)}) collective-permute-start(f32[4,128,128]{2,1,0:T(8,128)S(1)} %get-tuple-element.39), channel_id=1, source_target_pairs={{0,1},{1,0},{2,3},{3,2},{4,5},{5,4},{6,7},{7,6},{8,9},{9,8},{10,11... | collective-permute-start | bytes 786440 | tf_op jit(solution)/shard_map/ppermute | solution.py:408
  5.0 1.5 %copy-done = f32[48,9216]{1,0:T(8,128)S(1)} copy-done((f32[48,9216]{1,0:T(8,128)S(1)}, f32[48,9216]{1,0:T(8,128)}, u32[]{:S(2)}) %copy-start) | copy-done | bytes 1769496
  7.4 1.3 %project.1.refs_2_ = f32[24,4096]{1,0:T(8,128)S(1)} custom-call(f32[48,9216]{1,0:T(8,128)S(1)} %copy-done, bf16[160,384]{1,0:T(8,128)(2,1)S(1)} %copy-done.3, f32[4,128,128]{2,1,0:T(8,128)S(1)} %get-tuple-element.41.after.refs_0_), custom_call_target="tpu_custom_call" | custom-call | tf_op jit(solution)/shard_map/project/pallas_call | solution.py:435
  8.7 2.6 %collective-permute-done.refs_1_ = f32[4,128,128]{2,1,0:T(8,128)S(1)} collective-permute-done((f32[4,128,128]{2,1,0:T(8,128)S(1)}, f32[4,128,128]{2,1,0:T(8,128)S(1)}, u32[]{:S(2)}, u32[]{:S(2)}) %collective-permute-start) | collective-permute-done | bytes 262176 | tf_op jit(solution)/shard_map/ppermute | solution.py:408
  11.3 1.9 %collective-permute-start.1 = (f32[24,4096]{1,0:T(8,128)S(1)}, f32[24,4096]{1,0:T(8,128)S(1)}, u32[]{:S(2)}, u32[]{:S(2)}) collective-permute-start(f32[24,4096]{1,0:T(8,128)S(1)} %project.1.refs_2_), channel_id=1, source_target_pairs={{0,3},{1,2},{2,1},{3,0},{4,7},{5,6},{6,5},{7,4},{8,11},{9,10},{10,... | collective-permute-start | bytes 1179656 | tf_op jit(solution)/shard_map/ppermute | solution.py:414
  14.9 2.8 %synthesis.1 = (f32[32,32,128]{2,1,0:T(8,128)S(1)}, f32[4096,256]{1,0:T(8,128)S(1)}, bf16[896,256]{1,0:T(8,128)(2,1)S(1)}, f32[64,4096]{1,0:T(8,128)S(1)}, s32[1,8]{1,0:T(1,128)S(1)}) custom-call(f32[4,128,128]{2,1,0:T(8,128)S(1)} %get-tuple-element.41.after.refs_0_, f32[4,128,128]{2,1,0:T(8,128)S(1)} %collective-permute-done.refs_1_, ...), custom_call_target="tpu_custom_call" | custom-call | flops 1 | bytes 1 | tf_op jit(solution)/shard_map/synthesis/pallas_call | solution.py:463
  17.6 4.7 %collective-permute-done.1.refs_4_ = f32[24,4096]{1,0:T(8,128)S(1)} collective-permute-done((f32[24,4096]{1,0:T(8,128)S(1)}, f32[24,4096]{1,0:T(8,128)S(1)}, u32[]{:S(2)}, u32[]{:S(2)}) %collective-permute-start.1) | collective-permute-done | bytes 393248 | tf_op jit(solution)/shard_map/ppermute | solution.py:414
  24.0 9.8 %chebyshev.1 = (f32[4,128,128]{2,1,0:T(8,128)S(1)}, f32[4,128,128]{2,1,0:T(8,128)S(1)}, f32[32,32,128]{2,1,0:T(8,128)}) custom-call(f32[32,32,128]{2,1,0:T(8,128)S(1)} %get-tuple-element.45.refs_0_, f32[4096,256]{1,0:T(8,128)S(1)} %get-tuple-element.46.refs_1_, f32[64,4096]{1,0:T(8,128)S(1)} %get-tuple-element.47.refs_2_, ...), custom_call_target="tpu_custom_call" | custom-call | tf_op jit(solution)/shard_map/chebyshev/pallas_call | solution.py:492
  33.9 6.0 %all-to-all-start = ((f32[32,32,128]{2,1,0:T(8,128)}), f32[32,32,128]{2,1,0:T(8,128)S(1)}, u32[]{:S(2)}, u32[]{:S(2)}) async-start(f32[32,32,128]{2,1,0:T(8,128)} %get-tuple-element.53), calls=%async_computation | async-start | bytes 1048576 | tf_op jit(solution)/shard_map/all_to_all | solution.py:527
  40.2 1.8 %collective-permute-start.4 = (f32[4,128,128]{2,1,0:T(8,128)S(1)}, f32[4,128,128]{2,1,0:T(8,128)S(1)}, u32[]{:S(2)}, u32[]{:S(2)}) collective-permute-start(f32[4,128,128]{2,1,0:T(8,128)S(1)} %get-tuple-element.51), channel_id=1, source_target_pairs={{0,1},{1,0},{2,3},{3,2},{4,5},{5,4},{6,7},{7,6},{8,9},{9,8},{10,11... | collective-permute-start | bytes 786440 | tf_op jit(solution)/shard_map/ppermute | solution.py:408
  42.0 12.8 %all-to-all-done = f32[32,32,128]{2,1,0:T(8,128)S(1)} async-done(((f32[32,32,128]{2,1,0:T(8,128)}), f32[32,32,128]{2,1,0:T(8,128)S(1)}, u32[]{:S(2)}, u32[]{:S(2)}) %all-to-all-start) | async-done | bytes 524320 | tf_op jit(solution)/shard_map/all_to_all | solution.py:527
  55.5 1.5 %collective-permute-start.5 = (f32[32,1024]{1,0:T(8,128)S(1)}, f32[32,1024]{1,0:T(8,128)S(1)}, u32[]{:S(2)}, u32[]{:S(2)}) collective-permute-start(f32[32,1024]{1,0:T(8,128)S(1)} %get-tuple-element.55.refs_1_), channel_id=1, source_target_pairs={{0,4},{2,6},{8,0},{10,2},{16,8},{18,10},{24,16},{26,18},{28,24},{3... | collective-permute-start | bytes 393224 | tf_op jit(solution)/shard_map/ppermute | solution.py:546
  57.5 1.5 %collective-permute-start.13 = (f32[32,1024]{1,0:T(8,128)S(1)}, f32[32,1024]{1,0:T(8,128)S(1)}, u32[]{:S(2)}, u32[]{:S(2)}) collective-permute-start(f32[32,1024]{1,0:T(8,128)S(1)} %get-tuple-element.58.refs_0_), channel_id=1, source_target_pairs={{0,4},{2,6},{8,0},{10,2},{16,8},{18,10},{24,16},{26,18},{28,24},{3... | collective-permute-start | bytes 393224 | tf_op jit(solution)/shard_map/ppermute | solution.py:546
  59.6 2.2 %collective-permute-done.5.refs_5_ = f32[32,1024]{1,0:T(8,128)S(1)} collective-permute-done((f32[32,1024]{1,0:T(8,128)S(1)}, f32[32,1024]{1,0:T(8,128)S(1)}, u32[]{:S(2)}, u32[]{:S(2)}) %collective-permute-start.5) | collective-permute-done | bytes 131104 | tf_op jit(solution)/shard_map/ppermute | solution.py:546
  61.8 1.5 %collective-permute-start.6 = (f32[32,1024]{1,0:T(8,128)S(1)}, f32[32,1024]{1,0:T(8,128)S(1)}, u32[]{:S(2)}, u32[]{:S(2)}) collective-permute-start(f32[32,1024]{1,0:T(8,128)S(1)} %collective-permute-done.5.refs_5_), channel_id=1, source_target_pairs={{0,4},{2,6},{8,0},{10,2},{16,8},{18,10},{24,16},{26,18},{28,24},{3... | collective-permute-start | bytes 393224 | tf_op jit(solution)/shard_map/ppermute | solution.py:546
  64.6 1.5 %collective-permute-start.14 = (f32[32,1024]{1,0:T(8,128)S(1)}, f32[32,1024]{1,0:T(8,128)S(1)}, u32[]{:S(2)}, u32[]{:S(2)}) collective-permute-start(f32[32,1024]{1,0:T(8,128)S(1)} %collective-permute-done.13.refs_4_), channel_id=1, source_target_pairs={{0,4},{2,6},{8,0},{10,2},{16,8},{18,10},{24,16},{26,18},{28,24},{3... | collective-permute-start | bytes 393224 | tf_op jit(solution)/shard_map/ppermute | solution.py:546
  66.6 1.1 %unpack.1 = f32[8,16384]{1,0:T(8,128)} custom-call(f32[4,128,128]{2,1,0:T(8,128)S(1)} %get-tuple-element.50.refs_0_, f32[4,128,128]{2,1,0:T(8,128)S(1)} %collective-permute-done.4.refs_1_), custom_call_target="tpu_custom_call" | custom-call | flops 1 | bytes 1 | tf_op jit(solution)/shard_map/unpack/pallas_call | solution.py:512
  67.8 1.5 %collective-permute-start.16 = (f32[32,1024]{1,0:T(8,128)S(1)}, f32[32,1024]{1,0:T(8,128)S(1)}, u32[]{:S(2)}, u32[]{:S(2)}) collective-permute-start(f32[32,1024]{1,0:T(8,128)S(1)} %collective-permute-done.6.refs_9_), channel_id=1, source_target_pairs={{0,4},{2,6},{8,0},{10,2},{16,8},{18,10},{24,16},{26,18},{28,24},{3... | collective-permute-start | bytes 393224 | tf_op jit(solution)/shard_map/ppermute | solution.py:546
  70.5 1.5 %collective-permute-start.15 = (f32[32,1024]{1,0:T(8,128)S(1)}, f32[32,1024]{1,0:T(8,128)S(1)}, u32[]{:S(2)}, u32[]{:S(2)}) collective-permute-start(f32[32,1024]{1,0:T(8,128)S(1)} %collective-permute-done.14.refs_8_), channel_id=1, source_target_pairs={{0,4},{2,6},{8,0},{10,2},{16,8},{18,10},{24,16},{26,18},{28,24},{3... | collective-permute-start | bytes 393224 | tf_op jit(solution)/shard_map/ppermute | solution.py:546
  72.6 2.4 %rotate.4 = (f32[192,16384]{1,0:T(8,128)}, f32[5,64,1024]{2,1,0:T(8,128)S(1)}) custom-call(bf16[192,192]{1,0:T(8,128)(2,1)S(1)} %pad_maximum_fusion.table, f32[32,1024]{1,0:T(8,128)S(1)} %get-tuple-element.58.refs_0_, f32[32,1024]{1,0:T(8,128)S(1)} %get-tuple-element.55.refs_1_, f32[32,1024]{1,0:T(8,128)S(1)} %collective-permute-done.7.refs_2_, ...), custom_call_target="tpu_custom_call" | custom-call | flops 1000000000 | bytes 4000000 | tf_op jit(solution)/shard_map/rotate/pallas_call | solution.py:561
  77.8 1.2 %collective-permute-start.18 = (f32[32,1024]{1,0:T(8,128)S(1)}, f32[32,1024]{1,0:T(8,128)S(1)}, u32[]{:S(2)}, u32[]{:S(2)}) collective-permute-start(f32[32,1024]{1,0:T(8,128)S(1)} %collective-permute-done.16.refs_3_), channel_id=1, source_target_pairs={{0,4},{2,6},{8,0},{10,2},{16,8},{18,10},{24,16},{26,18},{28,24},{3... | collective-permute-start | bytes 393224 | tf_op jit(solution)/shard_map/ppermute | solution.py:546
  80.0 3.0 %rotate.5 = (f32[192,16384]{1,0:T(8,128)}, f32[2,64,1024]{2,1,0:T(8,128)S(1)}) custom-call(bf16[192,192]{1,0:T(8,128)(2,1)S(1)} %pad_maximum_fusion.table, f32[32,1024]{1,0:T(8,128)S(1)} %collective-permute-done.9.refs_0_, f32[32,1024]{1,0:T(8,128)S(1)} %collective-permute-done.12.refs_1_, ...), custom_call_target="tpu_custom_call", output_to_operand_aliasing={{0}: (6, {})} | custom-call | flops 1000000000 | bytes 4000000 | tf_op jit(solution)/shard_map/rotate/pallas_call | solution.py:561
  83.9 1.1 %rotate.6.refs_3_ = f32[192,16384]{1,0:T(8,128)} custom-call(bf16[192,192]{1,0:T(8,128)(2,1)S(1)} %pad_maximum_fusion.table, f32[32,1024]{1,0:T(8,128)S(1)} %collective-permute-done.17.refs_0_, f32[32,1024]{1,0:T(8,128)S(1)} %collective-permute-done.18.refs_1_, f32[192,16384]{1,0:T(8,128)} %get-tuple-element.73.refs_2_), custom_call_target="tpu_custom_call", output_to_operand_aliasing={{}: (3, {})} | custom-call | flops 1000000000 | bytes 4000000 | tf_op jit(solution)/shard_map/rotate/pallas_call | solution.py:561
  85.7 1.7 %rotate.7 = f32[192,16384]{1,0:T(8,128)} custom-call(bf16[192,192]{1,0:T(8,128)(2,1)S(1)} %pad_maximum_fusion.table, f32[2,64,1024]{2,1,0:T(8,128)S(1)} %collective-permute-done.20.refs_0_, f32[32,1024]{1,0:T(8,128)S(1)} %collective-permute-done.21.refs_1_, f32[32,1024]{1,0:T(8,128)S(1)} %collective-permute-done.22.refs_2_, ...), custom_call_target="tpu_custom_call", output_to_operand_aliasing={{}: (4, {})} | custom-call | flops 1000000000 | bytes 4000000 | tf_op jit(solution)/shard_map/rotate/pallas_call | solution.py:561
  (51 shorter events, 15.3 us)
Async XLA Ops:
  2.0 9.3 %collective-permute-start = (f32[4,128,128]{2,1,0:T(8,128)S(1)}, f32[4,128,128]{2,1,0:T(8,128)S(1)}, u32[]{:S(2)}, u32[]{:S(2)}) collective-permute-start(f32[4,128,128]{2,1,0:T(8,128)S(1)} %get-tuple-element.39), channel_id=1, source_target_pairs={{0,1},{1,0},{2,3},{3,2},{4,5},{5,4},{6,7},{7,6},{8,9},{9,8},{10,11... | collective-permute-start | bytes 786440 | tf_op jit(solution)/shard_map/ppermute | solution.py:408
  11.3 1.9 %collective-permute-start.2 = (f32[24,4096]{1,0:T(8,128)S(1)}, f32[24,4096]{1,0:T(8,128)S(1)}, u32[]{:S(2)}, u32[]{:S(2)}) collective-permute-start(f32[24,4096]{1,0:T(8,128)S(1)} %project.1.refs_2_), channel_id=1, source_target_pairs={{0,2},{2,0},{4,6},{6,4},{8,10},{10,8},{12,14},{14,12},{16,18},{18,... | collective-permute-start | bytes 1179656 | tf_op jit(solution)/shard_map/ppermute | solution.py:417
  11.3 11.0 %collective-permute-start.1 = (f32[24,4096]{1,0:T(8,128)S(1)}, f32[24,4096]{1,0:T(8,128)S(1)}, u32[]{:S(2)}, u32[]{:S(2)}) collective-permute-start(f32[24,4096]{1,0:T(8,128)S(1)} %project.1.refs_2_), channel_id=1, source_target_pairs={{0,3},{1,2},{2,1},{3,0},{4,7},{5,6},{6,5},{7,4},{8,11},{9,10},{10,... | collective-permute-start | bytes 1179656 | tf_op jit(solution)/shard_map/ppermute | solution.py:414
  22.3 1.7 %collective-permute-start.3 = (f32[24,4096]{1,0:T(8,128)S(1)}, f32[24,4096]{1,0:T(8,128)S(1)}, u32[]{:S(2)}, u32[]{:S(2)}) collective-permute-start(f32[24,4096]{1,0:T(8,128)S(1)} %collective-permute-done.1.refs_4_), channel_id=1, source_target_pairs={{0,2},{2,0},{4,6},{6,4},{8,10},{10,8},{12,14},{14,12},{16,18},{18,... | collective-permute-start | bytes 1179656 | tf_op jit(solution)/shard_map/ppermute | solution.py:417
  33.9 21.0 %all-to-all-start = ((f32[32,32,128]{2,1,0:T(8,128)}), f32[32,32,128]{2,1,0:T(8,128)S(1)}, u32[]{:S(2)}, u32[]{:S(2)}) async-start(f32[32,32,128]{2,1,0:T(8,128)} %get-tuple-element.53), calls=%async_computation | async-start | bytes 1048576 | tf_op jit(solution)/shard_map/all_to_all | solution.py:527
  40.2 26.4 %collective-permute-start.4 = (f32[4,128,128]{2,1,0:T(8,128)S(1)}, f32[4,128,128]{2,1,0:T(8,128)S(1)}, u32[]{:S(2)}, u32[]{:S(2)}) collective-permute-start(f32[4,128,128]{2,1,0:T(8,128)S(1)} %get-tuple-element.51), channel_id=1, source_target_pairs={{0,1},{1,0},{2,3},{3,2},{4,5},{5,4},{6,7},{7,6},{8,9},{9,8},{10,11... | collective-permute-start | bytes 786440 | tf_op jit(solution)/shard_map/ppermute | solution.py:408
  55.5 6.3 %collective-permute-start.5 = (f32[32,1024]{1,0:T(8,128)S(1)}, f32[32,1024]{1,0:T(8,128)S(1)}, u32[]{:S(2)}, u32[]{:S(2)}) collective-permute-start(f32[32,1024]{1,0:T(8,128)S(1)} %get-tuple-element.55.refs_1_), channel_id=1, source_target_pairs={{0,4},{2,6},{8,0},{10,2},{16,8},{18,10},{24,16},{26,18},{28,24},{3... | collective-permute-start | bytes 393224 | tf_op jit(solution)/shard_map/ppermute | solution.py:546
  57.0 6.3 %collective-permute-start.10 = (f32[32,1024]{1,0:T(8,128)S(1)}, f32[32,1024]{1,0:T(8,128)S(1)}, u32[]{:S(2)}, u32[]{:S(2)}) collective-permute-start(f32[32,1024]{1,0:T(8,128)S(1)} %get-tuple-element.55.refs_1_), channel_id=1, source_target_pairs={{0,8},{2,10},{8,16},{10,18},{16,24},{18,26},{24,28},{26,30},{28,20... | collective-permute-start | bytes 393224 | tf_op jit(solution)/shard_map/ppermute | solution.py:546
  57.5 7.1 %collective-permute-start.13 = (f32[32,1024]{1,0:T(8,128)S(1)}, f32[32,1024]{1,0:T(8,128)S(1)}, u32[]{:S(2)}, u32[]{:S(2)}) collective-permute-start(f32[32,1024]{1,0:T(8,128)S(1)} %get-tuple-element.58.refs_0_), channel_id=1, source_target_pairs={{0,4},{2,6},{8,0},{10,2},{16,8},{18,10},{24,16},{26,18},{28,24},{3... | collective-permute-start | bytes 393224 | tf_op jit(solution)/shard_map/ppermute | solution.py:546
  59.0 7.1 %collective-permute-start.7 = (f32[32,1024]{1,0:T(8,128)S(1)}, f32[32,1024]{1,0:T(8,128)S(1)}, u32[]{:S(2)}, u32[]{:S(2)}) collective-permute-start(f32[32,1024]{1,0:T(8,128)S(1)} %get-tuple-element.58.refs_0_), channel_id=1, source_target_pairs={{0,8},{2,10},{8,16},{10,18},{16,24},{18,26},{24,28},{26,30},{28,20... | collective-permute-start | bytes 393224 | tf_op jit(solution)/shard_map/ppermute | solution.py:546
  61.8 6.0 %collective-permute-start.6 = (f32[32,1024]{1,0:T(8,128)S(1)}, f32[32,1024]{1,0:T(8,128)S(1)}, u32[]{:S(2)}, u32[]{:S(2)}) collective-permute-start(f32[32,1024]{1,0:T(8,128)S(1)} %collective-permute-done.5.refs_5_), channel_id=1, source_target_pairs={{0,4},{2,6},{8,0},{10,2},{16,8},{18,10},{24,16},{26,18},{28,24},{3... | collective-permute-start | bytes 393224 | tf_op jit(solution)/shard_map/ppermute | solution.py:546
  63.3 6.0 %collective-permute-start.11 = (f32[32,1024]{1,0:T(8,128)S(1)}, f32[32,1024]{1,0:T(8,128)S(1)}, u32[]{:S(2)}, u32[]{:S(2)}) collective-permute-start(f32[32,1024]{1,0:T(8,128)S(1)} %collective-permute-done.10.refs_3_), channel_id=1, source_target_pairs={{0,8},{2,10},{8,16},{10,18},{16,24},{18,26},{24,28},{26,30},{28,20... | collective-permute-start | bytes 393224 | tf_op jit(solution)/shard_map/ppermute | solution.py:546
  64.6 5.9 %collective-permute-start.14 = (f32[32,1024]{1,0:T(8,128)S(1)}, f32[32,1024]{1,0:T(8,128)S(1)}, u32[]{:S(2)}, u32[]{:S(2)}) collective-permute-start(f32[32,1024]{1,0:T(8,128)S(1)} %collective-permute-done.13.refs_4_), channel_id=1, source_target_pairs={{0,4},{2,6},{8,0},{10,2},{16,8},{18,10},{24,16},{26,18},{28,24},{3... | collective-permute-start | bytes 393224 | tf_op jit(solution)/shard_map/ppermute | solution.py:546
  66.1 5.9 %collective-permute-start.8 = (f32[32,1024]{1,0:T(8,128)S(1)}, f32[32,1024]{1,0:T(8,128)S(1)}, u32[]{:S(2)}, u32[]{:S(2)}) collective-permute-start(f32[32,1024]{1,0:T(8,128)S(1)} %collective-permute-done.7.refs_2_), channel_id=1, source_target_pairs={{0,8},{2,10},{8,16},{10,18},{16,24},{18,26},{24,28},{26,30},{28,20... | collective-permute-start | bytes 393224 | tf_op jit(solution)/shard_map/ppermute | solution.py:546
  67.8 7.2 %collective-permute-start.16 = (f32[32,1024]{1,0:T(8,128)S(1)}, f32[32,1024]{1,0:T(8,128)S(1)}, u32[]{:S(2)}, u32[]{:S(2)}) collective-permute-start(f32[32,1024]{1,0:T(8,128)S(1)} %collective-permute-done.6.refs_9_), channel_id=1, source_target_pairs={{0,4},{2,6},{8,0},{10,2},{16,8},{18,10},{24,16},{26,18},{28,24},{3... | collective-permute-start | bytes 393224 | tf_op jit(solution)/shard_map/ppermute | solution.py:546
  69.3 6.1 %collective-permute-start.12 = (f32[32,1024]{1,0:T(8,128)S(1)}, f32[32,1024]{1,0:T(8,128)S(1)}, u32[]{:S(2)}, u32[]{:S(2)}) collective-permute-start(f32[32,1024]{1,0:T(8,128)S(1)} %collective-permute-done.11.refs_7_), channel_id=1, source_target_pairs={{0,8},{2,10},{8,16},{10,18},{16,24},{18,26},{24,28},{26,30},{28,20... | collective-permute-start | bytes 393224 | tf_op jit(solution)/shard_map/ppermute | solution.py:546
  70.5 5.4 %collective-permute-start.15 = (f32[32,1024]{1,0:T(8,128)S(1)}, f32[32,1024]{1,0:T(8,128)S(1)}, u32[]{:S(2)}, u32[]{:S(2)}) collective-permute-start(f32[32,1024]{1,0:T(8,128)S(1)} %collective-permute-done.14.refs_8_), channel_id=1, source_target_pairs={{0,4},{2,6},{8,0},{10,2},{16,8},{18,10},{24,16},{26,18},{28,24},{3... | collective-permute-start | bytes 393224 | tf_op jit(solution)/shard_map/ppermute | solution.py:546
  72.0 5.0 %collective-permute-start.9 = (f32[32,1024]{1,0:T(8,128)S(1)}, f32[32,1024]{1,0:T(8,128)S(1)}, u32[]{:S(2)}, u32[]{:S(2)}) collective-permute-start(f32[32,1024]{1,0:T(8,128)S(1)} %collective-permute-done.8.refs_6_), channel_id=1, source_target_pairs={{0,8},{2,10},{8,16},{10,18},{16,24},{18,26},{24,28},{26,30},{28,20... | collective-permute-start | bytes 393224 | tf_op jit(solution)/shard_map/ppermute | solution.py:546
  76.9 3.0 %collective-permute-start.19 = (f32[5,64,1024]{2,1,0:T(8,128)S(1)}, f32[5,64,1024]{2,1,0:T(8,128)S(1)}, u32[]{:S(2)}, u32[]{:S(2)}) collective-permute-start(f32[5,64,1024]{2,1,0:T(8,128)S(1)} %get-tuple-element.66), channel_id=1, source_target_pairs={{0,2},{2,0},{4,6},{6,4},{8,10},{10,8},{12,14},{14,12},{16,18},{18,... | collective-permute-start | bytes 3932168 | tf_op jit(solution)/shard_map/ppermute | solution.py:417
  77.0 6.1 %collective-permute-start.17 = (f32[32,1024]{1,0:T(8,128)S(1)}, f32[32,1024]{1,0:T(8,128)S(1)}, u32[]{:S(2)}, u32[]{:S(2)}) collective-permute-start(f32[32,1024]{1,0:T(8,128)S(1)} %collective-permute-done.9.refs_0_), channel_id=1, source_target_pairs={{0,8},{2,10},{8,16},{10,18},{16,24},{18,26},{24,28},{26,30},{28,20... | collective-permute-start | bytes 393224 | tf_op jit(solution)/shard_map/ppermute | solution.py:546
  77.8 5.6 %collective-permute-start.18 = (f32[32,1024]{1,0:T(8,128)S(1)}, f32[32,1024]{1,0:T(8,128)S(1)}, u32[]{:S(2)}, u32[]{:S(2)}) collective-permute-start(f32[32,1024]{1,0:T(8,128)S(1)} %collective-permute-done.16.refs_3_), channel_id=1, source_target_pairs={{0,4},{2,6},{8,0},{10,2},{16,8},{18,10},{24,16},{26,18},{28,24},{3... | collective-permute-start | bytes 393224 | tf_op jit(solution)/shard_map/ppermute | solution.py:546
  83.4 2.3 %collective-permute-start.20 = (f32[2,64,1024]{2,1,0:T(8,128)S(1)}, f32[2,64,1024]{2,1,0:T(8,128)S(1)}, u32[]{:S(2)}, u32[]{:S(2)}) collective-permute-start(f32[2,64,1024]{2,1,0:T(8,128)S(1)} %get-tuple-element.70), channel_id=1, source_target_pairs={{0,2},{2,0},{4,6},{6,4},{8,10},{10,8},{12,14},{14,12},{16,18},{18,... | collective-permute-start | bytes 1572872 | tf_op jit(solution)/shard_map/ppermute | solution.py:417
  83.4 2.1 %collective-permute-start.21 = (f32[32,1024]{1,0:T(8,128)S(1)}, f32[32,1024]{1,0:T(8,128)S(1)}, u32[]{:S(2)}, u32[]{:S(2)}) collective-permute-start(f32[32,1024]{1,0:T(8,128)S(1)} %collective-permute-done.17.refs_0_), channel_id=1, source_target_pairs={{0,2},{2,0},{4,6},{6,4},{8,10},{10,8},{12,14},{14,12},{16,18},{18,... | collective-permute-start | bytes 393224 | tf_op jit(solution)/shard_map/ppermute | solution.py:417
  83.9 1.8 %collective-permute-start.22 = (f32[32,1024]{1,0:T(8,128)S(1)}, f32[32,1024]{1,0:T(8,128)S(1)}, u32[]{:S(2)}, u32[]{:S(2)}) collective-permute-start(f32[32,1024]{1,0:T(8,128)S(1)} %collective-permute-done.18.refs_1_), channel_id=1, source_target_pairs={{0,2},{2,0},{4,6},{6,4},{8,10},{10,8},{12,14},{14,12},{16,18},{18,... | collective-permute-start | bytes 393224 | tf_op jit(solution)/shard_map/ppermute | solution.py:417
  (6 other events, 43.3 us)

commit v4 on v3

--- a/solution.py
+++ b/solution.py
@@ -225,7 +225,7 @@
 
 def synthesize(u_all, tables, z_first, x1, give):
     z_syn = tables[ROW_Z_SYN:ROW_Z_SYN + 3 * LANES, :2 * LANES]
-    group = 8
+    group = 16
     for ky in range(0, KEEP, group):
         high, low = split(u_all[ky:ky + group].reshape(group * KEEP, LANES))
         put(z_first, ky * KEEP, mm(jnp.concatenate([high, high, low], axis=1), z_syn))
@@ -551,7 +551,7 @@
         arrays, plan = [], []
         for offset, flip, parts in moves:
             if isinstance(parts, tuple):
-                arrays += parts[:1] if parts[1] == 0 else []
+                arrays += [] if any(x is parts[0] for x in arrays) else parts[:1]
                 plan.append((offset, flip, -1 - parts[1]))
             else:
                 arrays += parts
@@ -588,11 +588,11 @@
             own = []
         own += [(-k, 0, right), (k, 0, left)]
     last = [pass_on(right[0], 1), pass_on(left[1], -1)]
-    early, kept = rotate(own + ready, [early], len(own))
+    early, kept = rotate(own + ready[:-2], [early], len(own))
     last, early, kept = lax.optimization_barrier((last, early, kept))
     together = other_core(kept)
     later = [(offset, 1, (together, i)) for i, (offset, _, _) in enumerate(own)]
-    rotated, = rotate([(half, 0, last)], [early])
+    rotated, = rotate([(half, 0, last)] + ready[-2:], [early])
     rotated, = rotate(later + [(half, 1, [other_core(x) for x in last])], [rotated])
     return (filtered, rotated)
 

time: 87.9 us -> 87.9 us (level)
  no operation moved by 1% of the time
where the time goes in v4:
time: 87.9 us; the launch traced here: 87.5 us
  waiting for transfers between devices  27.9 us (32%)
  starting transfers between devices  27.8 us (32%)
  Pallas kernels  24.1 us (27%)
  local copies, waits for them, and re-layouts  5.27 us (6%)
  between operations  2.24 us (3%)
    ppermute x14, starting transfers between devices, pass_on(): return lax.ppermute(x, 'band', pairs)  14.3 us
    all_to_all x1, waiting for transfers between devices, body(): lax.all_to_all(spread, ('band', 'grid'), split_axis=0, concat_axis=0, til...  12.8 us
    pallas_call x1, Pallas kernels, body(): pl.pallas_call(functools.partial(filter_kernel, slices, ways), out_shape=...  9.78 us
    pallas_call x4, Pallas kernels, rotate(): pl.pallas_call(functools.partial(rotate_kernel, tuple(plan), chips, bool(...  8.23 us
    ppermute x14, waiting for transfers between devices, pass_on(): return lax.ppermute(x, 'band', pairs)  6.59 us
    all_to_all x1, starting transfers between devices, body(): lax.all_to_all(spread, ('band', 'grid'), split_axis=0, concat_axis=0, til...  5.98 us
    unnamed x12, local copies, waits for them, and re-layouts  5.09 us
    ppermute x2, starting transfers between devices, shift(): lax.ppermute(x, 'grid', [(i, (i + k) % slices) for i in range(slices)])  4.84 us
  transfers between devices with their start and end apart: 24, of which 14 were waited for; matrix products, arithmetic and copies ran while one was open for 0% of the time, Pallas kernels for 14%

profile of v4, /device:TPU:0, one launch (start us, length us, event | category | flops | bytes accessed | tf_op | source)
XLA Modules:
  0.0 87.5 jit_solution(3630686619609639094)
XLA Ops:
  2.0 3.0 %collective-permute-start = (f32[4,128,128]{2,1,0:T(8,128)S(1)}, f32[4,128,128]{2,1,0:T(8,128)S(1)}, u32[]{:S(2)}, u32[]{:S(2)}) collective-permute-start(f32[4,128,128]{2,1,0:T(8,128)S(1)} %get-tuple-element.39), channel_id=1, source_target_pairs={{0,1},{1,0},{2,3},{3,2},{4,5},{5,4},{6,7},{7,6},{8,9},{9,8},{10,11... | collective-permute-start | bytes 786440 | tf_op jit(solution)/shard_map/ppermute | solution.py:408
  5.0 1.5 %copy-done = f32[48,9216]{1,0:T(8,128)S(1)} copy-done((f32[48,9216]{1,0:T(8,128)S(1)}, f32[48,9216]{1,0:T(8,128)}, u32[]{:S(2)}) %copy-start) | copy-done | bytes 1769496
  7.4 1.3 %project.1.refs_2_ = f32[24,4096]{1,0:T(8,128)S(1)} custom-call(f32[48,9216]{1,0:T(8,128)S(1)} %copy-done, bf16[160,384]{1,0:T(8,128)(2,1)S(1)} %copy-done.3, f32[4,128,128]{2,1,0:T(8,128)S(1)} %get-tuple-element.41.after.refs_0_), custom_call_target="tpu_custom_call" | custom-call | tf_op jit(solution)/shard_map/project/pallas_call | solution.py:435
  8.7 2.6 %collective-permute-done.refs_1_ = f32[4,128,128]{2,1,0:T(8,128)S(1)} collective-permute-done((f32[4,128,128]{2,1,0:T(8,128)S(1)}, f32[4,128,128]{2,1,0:T(8,128)S(1)}, u32[]{:S(2)}, u32[]{:S(2)}) %collective-permute-start) | collective-permute-done | bytes 262176 | tf_op jit(solution)/shard_map/ppermute | solution.py:408
  11.3 1.9 %collective-permute-start.1 = (f32[24,4096]{1,0:T(8,128)S(1)}, f32[24,4096]{1,0:T(8,128)S(1)}, u32[]{:S(2)}, u32[]{:S(2)}) collective-permute-start(f32[24,4096]{1,0:T(8,128)S(1)} %project.1.refs_2_), channel_id=1, source_target_pairs={{0,3},{1,2},{2,1},{3,0},{4,7},{5,6},{6,5},{7,4},{8,11},{9,10},{10,... | collective-permute-start | bytes 1179656 | tf_op jit(solution)/shard_map/ppermute | solution.py:414
  14.9 2.7 %synthesis.1 = (f32[32,32,128]{2,1,0:T(8,128)S(1)}, f32[4096,256]{1,0:T(8,128)S(1)}, bf16[896,256]{1,0:T(8,128)(2,1)S(1)}, f32[64,4096]{1,0:T(8,128)S(1)}, s32[1,8]{1,0:T(1,128)S(1)}) custom-call(f32[4,128,128]{2,1,0:T(8,128)S(1)} %get-tuple-element.41.after.refs_0_, f32[4,128,128]{2,1,0:T(8,128)S(1)} %collective-permute-done.refs_1_, ...), custom_call_target="tpu_custom_call" | custom-call | flops 1 | bytes 1 | tf_op jit(solution)/shard_map/synthesis/pallas_call | solution.py:463
  17.6 4.8 %collective-permute-done.1.refs_4_ = f32[24,4096]{1,0:T(8,128)S(1)} collective-permute-done((f32[24,4096]{1,0:T(8,128)S(1)}, f32[24,4096]{1,0:T(8,128)S(1)}, u32[]{:S(2)}, u32[]{:S(2)}) %collective-permute-start.1) | collective-permute-done | bytes 393248 | tf_op jit(solution)/shard_map/ppermute | solution.py:414
  24.0 9.8 %chebyshev.1 = (f32[4,128,128]{2,1,0:T(8,128)S(1)}, f32[4,128,128]{2,1,0:T(8,128)S(1)}, f32[32,32,128]{2,1,0:T(8,128)}) custom-call(f32[32,32,128]{2,1,0:T(8,128)S(1)} %get-tuple-element.45.refs_0_, f32[4096,256]{1,0:T(8,128)S(1)} %get-tuple-element.46.refs_1_, f32[64,4096]{1,0:T(8,128)S(1)} %get-tuple-element.47.refs_2_, ...), custom_call_target="tpu_custom_call" | custom-call | tf_op jit(solution)/shard_map/chebyshev/pallas_call | solution.py:492
  33.8 6.0 %all-to-all-start = ((f32[32,32,128]{2,1,0:T(8,128)}), f32[32,32,128]{2,1,0:T(8,128)S(1)}, u32[]{:S(2)}, u32[]{:S(2)}) async-start(f32[32,32,128]{2,1,0:T(8,128)} %get-tuple-element.53), calls=%async_computation | async-start | bytes 1048576 | tf_op jit(solution)/shard_map/all_to_all | solution.py:527
  40.2 1.8 %collective-permute-start.4 = (f32[4,128,128]{2,1,0:T(8,128)S(1)}, f32[4,128,128]{2,1,0:T(8,128)S(1)}, u32[]{:S(2)}, u32[]{:S(2)}) collective-permute-start(f32[4,128,128]{2,1,0:T(8,128)S(1)} %get-tuple-element.51), channel_id=1, source_target_pairs={{0,1},{1,0},{2,3},{3,2},{4,5},{5,4},{6,7},{7,6},{8,9},{9,8},{10,11... | collective-permute-start | bytes 786440 | tf_op jit(solution)/shard_map/ppermute | solution.py:408
  42.0 12.8 %all-to-all-done = f32[32,32,128]{2,1,0:T(8,128)S(1)} async-done(((f32[32,32,128]{2,1,0:T(8,128)}), f32[32,32,128]{2,1,0:T(8,128)S(1)}, u32[]{:S(2)}, u32[]{:S(2)}) %all-to-all-start) | async-done | bytes 524320 | tf_op jit(solution)/shard_map/all_to_all | solution.py:527
  55.4 1.5 %collective-permute-start.5 = (f32[32,1024]{1,0:T(8,128)S(1)}, f32[32,1024]{1,0:T(8,128)S(1)}, u32[]{:S(2)}, u32[]{:S(2)}) collective-permute-start(f32[32,1024]{1,0:T(8,128)S(1)} %get-tuple-element.55.refs_1_), channel_id=1, source_target_pairs={{0,4},{2,6},{8,0},{10,2},{16,8},{18,10},{24,16},{26,18},{28,24},{3... | collective-permute-start | bytes 393224 | tf_op jit(solution)/shard_map/ppermute | solution.py:546
  57.5 1.5 %collective-permute-start.13 = (f32[32,1024]{1,0:T(8,128)S(1)}, f32[32,1024]{1,0:T(8,128)S(1)}, u32[]{:S(2)}, u32[]{:S(2)}) collective-permute-start(f32[32,1024]{1,0:T(8,128)S(1)} %get-tuple-element.58.refs_0_), channel_id=1, source_target_pairs={{0,4},{2,6},{8,0},{10,2},{16,8},{18,10},{24,16},{26,18},{28,24},{3... | collective-permute-start | bytes 393224 | tf_op jit(solution)/shard_map/ppermute | solution.py:546
  59.5 2.2 %collective-permute-done.5.refs_5_ = f32[32,1024]{1,0:T(8,128)S(1)} collective-permute-done((f32[32,1024]{1,0:T(8,128)S(1)}, f32[32,1024]{1,0:T(8,128)S(1)}, u32[]{:S(2)}, u32[]{:S(2)}) %collective-permute-start.5) | collective-permute-done | bytes 131104 | tf_op jit(solution)/shard_map/ppermute | solution.py:546
  61.7 1.5 %collective-permute-start.6 = (f32[32,1024]{1,0:T(8,128)S(1)}, f32[32,1024]{1,0:T(8,128)S(1)}, u32[]{:S(2)}, u32[]{:S(2)}) collective-permute-start(f32[32,1024]{1,0:T(8,128)S(1)} %collective-permute-done.5.refs_5_), channel_id=1, source_target_pairs={{0,4},{2,6},{8,0},{10,2},{16,8},{18,10},{24,16},{26,18},{28,24},{3... | collective-permute-start | bytes 393224 | tf_op jit(solution)/shard_map/ppermute | solution.py:546
  64.5 1.5 %collective-permute-start.14 = (f32[32,1024]{1,0:T(8,128)S(1)}, f32[32,1024]{1,0:T(8,128)S(1)}, u32[]{:S(2)}, u32[]{:S(2)}) collective-permute-start(f32[32,1024]{1,0:T(8,128)S(1)} %collective-permute-done.13.refs_4_), channel_id=1, source_target_pairs={{0,4},{2,6},{8,0},{10,2},{16,8},{18,10},{24,16},{26,18},{28,24},{3... | collective-permute-start | bytes 393224 | tf_op jit(solution)/shard_map/ppermute | solution.py:546
  66.6 1.1 %unpack.1 = f32[8,16384]{1,0:T(8,128)} custom-call(f32[4,128,128]{2,1,0:T(8,128)S(1)} %get-tuple-element.50.refs_0_, f32[4,128,128]{2,1,0:T(8,128)S(1)} %collective-permute-done.4.refs_1_), custom_call_target="tpu_custom_call" | custom-call | flops 1 | bytes 1 | tf_op jit(solution)/shard_map/unpack/pallas_call | solution.py:512
  67.7 1.5 %collective-permute-start.16 = (f32[32,1024]{1,0:T(8,128)S(1)}, f32[32,1024]{1,0:T(8,128)S(1)}, u32[]{:S(2)}, u32[]{:S(2)}) collective-permute-start(f32[32,1024]{1,0:T(8,128)S(1)} %collective-permute-done.6.refs_9_), channel_id=1, source_target_pairs={{0,4},{2,6},{8,0},{10,2},{16,8},{18,10},{24,16},{26,18},{28,24},{3... | collective-permute-start | bytes 393224 | tf_op jit(solution)/shard_map/ppermute | solution.py:546
  70.5 1.5 %collective-permute-start.15 = (f32[32,1024]{1,0:T(8,128)S(1)}, f32[32,1024]{1,0:T(8,128)S(1)}, u32[]{:S(2)}, u32[]{:S(2)}) collective-permute-start(f32[32,1024]{1,0:T(8,128)S(1)} %collective-permute-done.14.refs_8_), channel_id=1, source_target_pairs={{0,4},{2,6},{8,0},{10,2},{16,8},{18,10},{24,16},{26,18},{28,24},{3... | collective-permute-start | bytes 393224 | tf_op jit(solution)/shard_map/ppermute | solution.py:546
  72.5 2.4 %rotate.4 = (f32[192,16384]{1,0:T(8,128)}, f32[5,64,1024]{2,1,0:T(8,128)S(1)}) custom-call(bf16[192,192]{1,0:T(8,128)(2,1)S(1)} %pad_maximum_fusion.table, f32[32,1024]{1,0:T(8,128)S(1)} %get-tuple-element.58.refs_0_, f32[32,1024]{1,0:T(8,128)S(1)} %get-tuple-element.55.refs_1_, f32[32,1024]{1,0:T(8,128)S(1)} %collective-permute-done.7.refs_2_, ...), custom_call_target="tpu_custom_call" | custom-call | flops 1000000000 | bytes 4000000 | tf_op jit(solution)/shard_map/rotate/pallas_call | solution.py:561
  77.7 1.2 %collective-permute-start.18 = (f32[32,1024]{1,0:T(8,128)S(1)}, f32[32,1024]{1,0:T(8,128)S(1)}, u32[]{:S(2)}, u32[]{:S(2)}) collective-permute-start(f32[32,1024]{1,0:T(8,128)S(1)} %collective-permute-done.16.refs_3_), channel_id=1, source_target_pairs={{0,4},{2,6},{8,0},{10,2},{16,8},{18,10},{24,16},{26,18},{28,24},{3... | collective-permute-start | bytes 393224 | tf_op jit(solution)/shard_map/ppermute | solution.py:546
  79.9 2.4 %rotate.5 = (f32[192,16384]{1,0:T(8,128)}, f32[2,64,1024]{2,1,0:T(8,128)S(1)}) custom-call(bf16[192,192]{1,0:T(8,128)(2,1)S(1)} %pad_maximum_fusion.table, f32[32,1024]{1,0:T(8,128)S(1)} %collective-permute-done.9.refs_0_, f32[32,1024]{1,0:T(8,128)S(1)} %collective-permute-done.12.refs_1_, ...), custom_call_target="tpu_custom_call", output_to_operand_aliasing={{0}: (6, {})} | custom-call | flops 1000000000 | bytes 4000000 | tf_op jit(solution)/shard_map/rotate/pallas_call | solution.py:561
  83.9 1.7 %rotate.6.refs_3_ = f32[192,16384]{1,0:T(8,128)} custom-call(bf16[192,192]{1,0:T(8,128)(2,1)S(1)} %pad_maximum_fusion.table, f32[32,1024]{1,0:T(8,128)S(1)} %collective-permute-done.17.refs_0_, f32[32,1024]{1,0:T(8,128)S(1)} %collective-permute-done.18.refs_1_, ...), custom_call_target="tpu_custom_call", output_to_operand_aliasing={{}: (4, {})} | custom-call | flops 1000000000 | bytes 4000000 | tf_op jit(solution)/shard_map/rotate/pallas_call | solution.py:561
  85.6 1.7 %rotate.7 = f32[192,16384]{1,0:T(8,128)} custom-call(bf16[192,192]{1,0:T(8,128)(2,1)S(1)} %pad_maximum_fusion.table, f32[2,64,1024]{2,1,0:T(8,128)S(1)} %collective-permute-done.20.refs_0_, f32[32,1024]{1,0:T(8,128)S(1)} %collective-permute-done.21.refs_1_, f32[32,1024]{1,0:T(8,128)S(1)} %collective-permute-done.22.refs_2_, ...), custom_call_target="tpu_custom_call", output_to_operand_aliasing={{}: (4, {})} | custom-call | flops 1000000000 | bytes 4000000 | tf_op jit(solution)/shard_map/rotate/pallas_call | solution.py:561
  (51 shorter events, 15.4 us)
Async XLA Ops:
  2.0 9.3 %collective-permute-start = (f32[4,128,128]{2,1,0:T(8,128)S(1)}, f32[4,128,128]{2,1,0:T(8,128)S(1)}, u32[]{:S(2)}, u32[]{:S(2)}) collective-permute-start(f32[4,128,128]{2,1,0:T(8,128)S(1)} %get-tuple-element.39), channel_id=1, source_target_pairs={{0,1},{1,0},{2,3},{3,2},{4,5},{5,4},{6,7},{7,6},{8,9},{9,8},{10,11... | collective-permute-start | bytes 786440 | tf_op jit(solution)/shard_map/ppermute | solution.py:408
  11.3 1.9 %collective-permute-start.2 = (f32[24,4096]{1,0:T(8,128)S(1)}, f32[24,4096]{1,0:T(8,128)S(1)}, u32[]{:S(2)}, u32[]{:S(2)}) collective-permute-start(f32[24,4096]{1,0:T(8,128)S(1)} %project.1.refs_2_), channel_id=1, source_target_pairs={{0,2},{2,0},{4,6},{6,4},{8,10},{10,8},{12,14},{14,12},{16,18},{18,... | collective-permute-start | bytes 1179656 | tf_op jit(solution)/shard_map/ppermute | solution.py:417
  11.3 11.0 %collective-permute-start.1 = (f32[24,4096]{1,0:T(8,128)S(1)}, f32[24,4096]{1,0:T(8,128)S(1)}, u32[]{:S(2)}, u32[]{:S(2)}) collective-permute-start(f32[24,4096]{1,0:T(8,128)S(1)} %project.1.refs_2_), channel_id=1, source_target_pairs={{0,3},{1,2},{2,1},{3,0},{4,7},{5,6},{6,5},{7,4},{8,11},{9,10},{10,... | collective-permute-start | bytes 1179656 | tf_op jit(solution)/shard_map/ppermute | solution.py:414
  22.3 1.7 %collective-permute-start.3 = (f32[24,4096]{1,0:T(8,128)S(1)}, f32[24,4096]{1,0:T(8,128)S(1)}, u32[]{:S(2)}, u32[]{:S(2)}) collective-permute-start(f32[24,4096]{1,0:T(8,128)S(1)} %collective-permute-done.1.refs_4_), channel_id=1, source_target_pairs={{0,2},{2,0},{4,6},{6,4},{8,10},{10,8},{12,14},{14,12},{16,18},{18,... | collective-permute-start | bytes 1179656 | tf_op jit(solution)/shard_map/ppermute | solution.py:417
  33.8 21.0 %all-to-all-start = ((f32[32,32,128]{2,1,0:T(8,128)}), f32[32,32,128]{2,1,0:T(8,128)S(1)}, u32[]{:S(2)}, u32[]{:S(2)}) async-start(f32[32,32,128]{2,1,0:T(8,128)} %get-tuple-element.53), calls=%async_computation | async-start | bytes 1048576 | tf_op jit(solution)/shard_map/all_to_all | solution.py:527
  40.2 26.4 %collective-permute-start.4 = (f32[4,128,128]{2,1,0:T(8,128)S(1)}, f32[4,128,128]{2,1,0:T(8,128)S(1)}, u32[]{:S(2)}, u32[]{:S(2)}) collective-permute-start(f32[4,128,128]{2,1,0:T(8,128)S(1)} %get-tuple-element.51), channel_id=1, source_target_pairs={{0,1},{1,0},{2,3},{3,2},{4,5},{5,4},{6,7},{7,6},{8,9},{9,8},{10,11... | collective-permute-start | bytes 786440 | tf_op jit(solution)/shard_map/ppermute | solution.py:408
  55.4 6.3 %collective-permute-start.5 = (f32[32,1024]{1,0:T(8,128)S(1)}, f32[32,1024]{1,0:T(8,128)S(1)}, u32[]{:S(2)}, u32[]{:S(2)}) collective-permute-start(f32[32,1024]{1,0:T(8,128)S(1)} %get-tuple-element.55.refs_1_), channel_id=1, source_target_pairs={{0,4},{2,6},{8,0},{10,2},{16,8},{18,10},{24,16},{26,18},{28,24},{3... | collective-permute-start | bytes 393224 | tf_op jit(solution)/shard_map/ppermute | solution.py:546
  56.9 6.3 %collective-permute-start.10 = (f32[32,1024]{1,0:T(8,128)S(1)}, f32[32,1024]{1,0:T(8,128)S(1)}, u32[]{:S(2)}, u32[]{:S(2)}) collective-permute-start(f32[32,1024]{1,0:T(8,128)S(1)} %get-tuple-element.55.refs_1_), channel_id=1, source_target_pairs={{0,8},{2,10},{8,16},{10,18},{16,24},{18,26},{24,28},{26,30},{28,20... | collective-permute-start | bytes 393224 | tf_op jit(solution)/shard_map/ppermute | solution.py:546
  57.5 7.1 %collective-permute-start.13 = (f32[32,1024]{1,0:T(8,128)S(1)}, f32[32,1024]{1,0:T(8,128)S(1)}, u32[]{:S(2)}, u32[]{:S(2)}) collective-permute-start(f32[32,1024]{1,0:T(8,128)S(1)} %get-tuple-element.58.refs_0_), channel_id=1, source_target_pairs={{0,4},{2,6},{8,0},{10,2},{16,8},{18,10},{24,16},{26,18},{28,24},{3... | collective-permute-start | bytes 393224 | tf_op jit(solution)/shard_map/ppermute | solution.py:546
  59.0 7.1 %collective-permute-start.7 = (f32[32,1024]{1,0:T(8,128)S(1)}, f32[32,1024]{1,0:T(8,128)S(1)}, u32[]{:S(2)}, u32[]{:S(2)}) collective-permute-start(f32[32,1024]{1,0:T(8,128)S(1)} %get-tuple-element.58.refs_0_), channel_id=1, source_target_pairs={{0,8},{2,10},{8,16},{10,18},{16,24},{18,26},{24,28},{26,30},{28,20... | collective-permute-start | bytes 393224 | tf_op jit(solution)/shard_map/ppermute | solution.py:546
  61.7 6.0 %collective-permute-start.6 = (f32[32,1024]{1,0:T(8,128)S(1)}, f32[32,1024]{1,0:T(8,128)S(1)}, u32[]{:S(2)}, u32[]{:S(2)}) collective-permute-start(f32[32,1024]{1,0:T(8,128)S(1)} %collective-permute-done.5.refs_5_), channel_id=1, source_target_pairs={{0,4},{2,6},{8,0},{10,2},{16,8},{18,10},{24,16},{26,18},{28,24},{3... | collective-permute-start | bytes 393224 | tf_op jit(solution)/shard_map/ppermute | solution.py:546
  63.3 6.0 %collective-permute-start.11 = (f32[32,1024]{1,0:T(8,128)S(1)}, f32[32,1024]{1,0:T(8,128)S(1)}, u32[]{:S(2)}, u32[]{:S(2)}) collective-permute-start(f32[32,1024]{1,0:T(8,128)S(1)} %collective-permute-done.10.refs_3_), channel_id=1, source_target_pairs={{0,8},{2,10},{8,16},{10,18},{16,24},{18,26},{24,28},{26,30},{28,20... | collective-permute-start | bytes 393224 | tf_op jit(solution)/shard_map/ppermute | solution.py:546
  64.5 5.9 %collective-permute-start.14 = (f32[32,1024]{1,0:T(8,128)S(1)}, f32[32,1024]{1,0:T(8,128)S(1)}, u32[]{:S(2)}, u32[]{:S(2)}) collective-permute-start(f32[32,1024]{1,0:T(8,128)S(1)} %collective-permute-done.13.refs_4_), channel_id=1, source_target_pairs={{0,4},{2,6},{8,0},{10,2},{16,8},{18,10},{24,16},{26,18},{28,24},{3... | collective-permute-start | bytes 393224 | tf_op jit(solution)/shard_map/ppermute | solution.py:546
  66.0 5.9 %collective-permute-start.8 = (f32[32,1024]{1,0:T(8,128)S(1)}, f32[32,1024]{1,0:T(8,128)S(1)}, u32[]{:S(2)}, u32[]{:S(2)}) collective-permute-start(f32[32,1024]{1,0:T(8,128)S(1)} %collective-permute-done.7.refs_2_), channel_id=1, source_target_pairs={{0,8},{2,10},{8,16},{10,18},{16,24},{18,26},{24,28},{26,30},{28,20... | collective-permute-start | bytes 393224 | tf_op jit(solution)/shard_map/ppermute | solution.py:546
  67.7 7.2 %collective-permute-start.16 = (f32[32,1024]{1,0:T(8,128)S(1)}, f32[32,1024]{1,0:T(8,128)S(1)}, u32[]{:S(2)}, u32[]{:S(2)}) collective-permute-start(f32[32,1024]{1,0:T(8,128)S(1)} %collective-permute-done.6.refs_9_), channel_id=1, source_target_pairs={{0,4},{2,6},{8,0},{10,2},{16,8},{18,10},{24,16},{26,18},{28,24},{3... | collective-permute-start | bytes 393224 | tf_op jit(solution)/shard_map/ppermute | solution.py:546
  69.2 6.1 %collective-permute-start.12 = (f32[32,1024]{1,0:T(8,128)S(1)}, f32[32,1024]{1,0:T(8,128)S(1)}, u32[]{:S(2)}, u32[]{:S(2)}) collective-permute-start(f32[32,1024]{1,0:T(8,128)S(1)} %collective-permute-done.11.refs_7_), channel_id=1, source_target_pairs={{0,8},{2,10},{8,16},{10,18},{16,24},{18,26},{24,28},{26,30},{28,20... | collective-permute-start | bytes 393224 | tf_op jit(solution)/shard_map/ppermute | solution.py:546
  70.5 5.4 %collective-permute-start.15 = (f32[32,1024]{1,0:T(8,128)S(1)}, f32[32,1024]{1,0:T(8,128)S(1)}, u32[]{:S(2)}, u32[]{:S(2)}) collective-permute-start(f32[32,1024]{1,0:T(8,128)S(1)} %collective-permute-done.14.refs_8_), channel_id=1, source_target_pairs={{0,4},{2,6},{8,0},{10,2},{16,8},{18,10},{24,16},{26,18},{28,24},{3... | collective-permute-start | bytes 393224 | tf_op jit(solution)/shard_map/ppermute | solution.py:546
  71.9 5.0 %collective-permute-start.9 = (f32[32,1024]{1,0:T(8,128)S(1)}, f32[32,1024]{1,0:T(8,128)S(1)}, u32[]{:S(2)}, u32[]{:S(2)}) collective-permute-start(f32[32,1024]{1,0:T(8,128)S(1)} %collective-permute-done.8.refs_6_), channel_id=1, source_target_pairs={{0,8},{2,10},{8,16},{10,18},{16,24},{18,26},{24,28},{26,30},{28,20... | collective-permute-start | bytes 393224 | tf_op jit(solution)/shard_map/ppermute | solution.py:546
  76.9 3.0 %collective-permute-start.19 = (f32[5,64,1024]{2,1,0:T(8,128)S(1)}, f32[5,64,1024]{2,1,0:T(8,128)S(1)}, u32[]{:S(2)}, u32[]{:S(2)}) collective-permute-start(f32[5,64,1024]{2,1,0:T(8,128)S(1)} %get-tuple-element.66), channel_id=1, source_target_pairs={{0,2},{2,0},{4,6},{6,4},{8,10},{10,8},{12,14},{14,12},{16,18},{18,... | collective-permute-start | bytes 3932168 | tf_op jit(solution)/shard_map/ppermute | solution.py:417
  76.9 5.9 %collective-permute-start.17 = (f32[32,1024]{1,0:T(8,128)S(1)}, f32[32,1024]{1,0:T(8,128)S(1)}, u32[]{:S(2)}, u32[]{:S(2)}) collective-permute-start(f32[32,1024]{1,0:T(8,128)S(1)} %collective-permute-done.9.refs_0_), channel_id=1, source_target_pairs={{0,8},{2,10},{8,16},{10,18},{16,24},{18,26},{24,28},{26,30},{28,20... | collective-permute-start | bytes 393224 | tf_op jit(solution)/shard_map/ppermute | solution.py:546
  77.7 5.6 %collective-permute-start.18 = (f32[32,1024]{1,0:T(8,128)S(1)}, f32[32,1024]{1,0:T(8,128)S(1)}, u32[]{:S(2)}, u32[]{:S(2)}) collective-permute-start(f32[32,1024]{1,0:T(8,128)S(1)} %collective-permute-done.16.refs_3_), channel_id=1, source_target_pairs={{0,4},{2,6},{8,0},{10,2},{16,8},{18,10},{24,16},{26,18},{28,24},{3... | collective-permute-start | bytes 393224 | tf_op jit(solution)/shard_map/ppermute | solution.py:546
  83.4 2.3 %collective-permute-start.20 = (f32[2,64,1024]{2,1,0:T(8,128)S(1)}, f32[2,64,1024]{2,1,0:T(8,128)S(1)}, u32[]{:S(2)}, u32[]{:S(2)}) collective-permute-start(f32[2,64,1024]{2,1,0:T(8,128)S(1)} %get-tuple-element.70), channel_id=1, source_target_pairs={{0,2},{2,0},{4,6},{6,4},{8,10},{10,8},{12,14},{14,12},{16,18},{18,... | collective-permute-start | bytes 1572872 | tf_op jit(solution)/shard_map/ppermute | solution.py:417
  83.4 2.2 %collective-permute-start.21 = (f32[32,1024]{1,0:T(8,128)S(1)}, f32[32,1024]{1,0:T(8,128)S(1)}, u32[]{:S(2)}, u32[]{:S(2)}) collective-permute-start(f32[32,1024]{1,0:T(8,128)S(1)} %collective-permute-done.17.refs_0_), channel_id=1, source_target_pairs={{0,2},{2,0},{4,6},{6,4},{8,10},{10,8},{12,14},{14,12},{16,18},{18,... | collective-permute-start | bytes 393224 | tf_op jit(solution)/shard_map/ppermute | solution.py:417
  83.9 1.8 %collective-permute-start.22 = (f32[32,1024]{1,0:T(8,128)S(1)}, f32[32,1024]{1,0:T(8,128)S(1)}, u32[]{:S(2)}, u32[]{:S(2)}) collective-permute-start(f32[32,1024]{1,0:T(8,128)S(1)} %collective-permute-done.18.refs_1_), channel_id=1, source_target_pairs={{0,2},{2,0},{4,6},{6,4},{8,10},{10,8},{12,14},{14,12},{16,18},{18,... | collective-permute-start | bytes 393224 | tf_op jit(solution)/shard_map/ppermute | solution.py:417
  (6 other events, 43.2 us)
